TPU v7x, 32 devices: a whole 2x2x4 slice. The times are simulated.
32 devices in a mesh: wide: 8 (over y, x, core), narrow: 4 (over z).
Axes of the slice: x: 2, y: 2, z: 4, core: 2. Of those that a mesh axis runs over, the one named last changes fastest.
Arguments:
- tokens: bfloat16 [32, 512, 768], P(('wide', 'narrow')), may hold values from -6 to 6
- lengths: int32 [32], P(('wide', 'narrow')), may hold values from 20 to 512, as said below
- gain_one: bfloat16 [768], P(('wide', 'narrow')), may hold values from 0.5 to 1.5
- w_value: bfloat16 [768, 768], P(('wide', 'narrow')), may hold values from -0.21875 to 0.21875
- w_first: bfloat16 [12, 768, 768], P(None, ('wide', 'narrow')), may hold values from -0.21875 to 0.21875
- b_first: bfloat16 [12, 768], P(None, ('wide', 'narrow')), may hold values from -3 to 3
- w_second: bfloat16 [12, 768, 512], P(None, ('wide', 'narrow')), may hold values from -0.4375 to 0.4375
- b_second: bfloat16 [6144], P(('wide', 'narrow')), may hold values from -4 to 4
- w_out: bfloat16 [768, 768], P(('wide', 'narrow')), may hold values from -0.625 to 0.625
- gain_two: bfloat16 [768], P(('wide', 'narrow')), may hold values from 0.5 to 1.5
- w_up: bfloat16 [768, 3072], P(('wide', 'narrow')), may hold values from -0.21875 to 0.21875
- w_down: bfloat16 [3072, 768], P(('wide', 'narrow')), may hold values from -0.15625 to 0.15625
- grad_out: float32 [32, 512, 768], P(('wide', 'narrow')), may hold values from -6 to 6
Outputs:
- block_out: float32 [32, 512, 768], P(('wide', 'narrow'))
- grad_tokens: float32 [32, 512, 768], P(('wide', 'narrow'))
- grad_gain_one: float32 [768], P(('wide', 'narrow'))
- grad_w_value: float32 [768, 768], P(('wide', 'narrow'))
- grad_w_first: float32 [12, 768, 768], P(None, ('wide', 'narrow'))
- grad_b_first: float32 [12, 768], P(None, ('wide', 'narrow'))
- grad_w_second: float32 [12, 768, 512], P(None, ('wide', 'narrow'))
- grad_b_second: float32 [6144], P(('wide', 'narrow'))
- grad_w_out: float32 [768, 768], P(('wide', 'narrow'))
- grad_gain_two: float32 [768], P(('wide', 'narrow'))
- grad_w_up: float32 [768, 3072], P(('wide', 'narrow'))
- grad_w_down: float32 [3072, 768], P(('wide', 'narrow'))
Inputs may be any that keep to these rules, and one draw needn't show every extreme that they name: `lengths`: some row holds an item of the full 512 slots.
All inputs are finite; a program needn't handle non-finite values.
Results may differ from a plain program's by a relative error of at most 0.013.
Values may be sent and summed in bfloat16 or wider, within the bound.
A program may use at most 256 MiB of HBM per device.

v0:
```python
import jax
import jax.numpy as jnp
from jax import lax
from jax.sharding import PartitionSpec as P

epsilon = 1e-05


def norm_rows(values, factor):
    average = jnp.mean(values, axis=-1, keepdims=True)
    centred = values - average
    spread = jnp.mean(centred * centred, axis=-1, keepdims=True)
    return centred * lax.rsqrt(spread + epsilon) * factor


def smooth(values):
    return jax.nn.gelu(values, approximate=False)


def attend_forward(normed, length, attn_set):
    w_value, w_first, b_first, w_second, b_second = (
        attn_set[1],
        attn_set[2],
        attn_set[3],
        attn_set[4],
        attn_set[5],
    )
    heads_count, model_width, slot_count = w_second.shape
    head_size = model_width // heads_count
    values = jnp.dot(normed, w_value, preferred_element_type=jnp.float32).astype(jnp.bfloat16)
    before = (
        jnp.einsum("sd,hde->hse", normed, w_first, preferred_element_type=jnp.float32)
        + b_first.astype(jnp.float32)[:, None, :]
    )
    hidden = smooth(before).astype(jnp.bfloat16)
    logits = jnp.einsum("hse,hej->hsj", hidden, w_second, preferred_element_type=jnp.float32)
    logits = logits + b_second.astype(jnp.float32).reshape(heads_count, slot_count)[:, None, :]
    visible = lax.broadcasted_iota(jnp.int32, (1, 1, slot_count), 2) < length
    masked = jnp.where(visible, logits, jnp.float32(-1e30))
    highest_score = jnp.max(masked, axis=-1, keepdims=True)
    scaled = jnp.exp(masked - highest_score)
    probabilities = scaled / jnp.sum(scaled, axis=-1, keepdims=True)
    weights = probabilities.astype(jnp.bfloat16)
    per_head = values.reshape(slot_count, heads_count, head_size).transpose(1, 0, 2)
    mixture = jnp.einsum("hsj,hjc->hsc", weights, per_head, preferred_element_type=jnp.float32)
    joined = mixture.transpose(1, 0, 2).reshape(slot_count, model_width).astype(jnp.bfloat16)
    return (before, hidden, probabilities, weights, per_head, joined)


def on_device(
    tokens,
    lengths,
    gain_one,
    w_value,
    w_first,
    b_first,
    w_second,
    b_second,
    w_out,
    gain_two,
    w_up,
    w_down,
    grad_out,
):
    row_count, slot_count, model_width = tokens.shape
    attn_set = (
        lax.all_gather(gain_one, ("wide", "narrow"), axis=0, tiled=True),
        lax.all_gather(w_value, ("wide", "narrow"), axis=0, tiled=True),
        lax.all_gather(w_first, ("wide", "narrow"), axis=1, tiled=True),
        lax.all_gather(b_first, ("wide", "narrow"), axis=1, tiled=True),
        lax.all_gather(w_second, ("wide", "narrow"), axis=1, tiled=True),
        lax.all_gather(b_second, ("wide", "narrow"), axis=0, tiled=True),
        lax.all_gather(w_out, ("wide", "narrow"), axis=0, tiled=True),
    )
    inputs = tokens.astype(jnp.float32)
    normed_one = norm_rows(inputs, attn_set[0].astype(jnp.float32)).astype(jnp.bfloat16)

    def forward_row(row_pair):
        pieces = attend_forward(row_pair[0], row_pair[1], attn_set)
        return jnp.dot(pieces[5], attn_set[6], preferred_element_type=jnp.float32)

    branch = lax.map(forward_row, (normed_one, lengths))
    middle = inputs + branch
    ffn_set = (
        lax.all_gather(gain_two, ("wide", "narrow"), axis=0, tiled=True),
        lax.all_gather(w_up, ("wide", "narrow"), axis=0, tiled=True),
        lax.all_gather(w_down, ("wide", "narrow"), axis=0, tiled=True),
    )
    normed_two = (
        norm_rows(middle, ffn_set[0].astype(jnp.float32))
        .astype(jnp.bfloat16)
        .reshape(row_count * slot_count, model_width)
    )
    upward = jnp.dot(normed_two, ffn_set[1], preferred_element_type=jnp.float32)
    active = smooth(upward).astype(jnp.bfloat16)
    downward = jnp.dot(active, ffn_set[2], preferred_element_type=jnp.float32)
    result = middle + downward.reshape(row_count, slot_count, model_width)
    ffn_back = (
        lax.all_gather(gain_two, ("wide", "narrow"), axis=0, tiled=True),
        lax.all_gather(w_up, ("wide", "narrow"), axis=0, tiled=True),
        lax.all_gather(w_down, ("wide", "narrow"), axis=0, tiled=True),
    )
    grad_branch = grad_out.reshape(row_count * slot_count, model_width).astype(jnp.bfloat16)
    grad_w_down = jnp.einsum("tf,td->fd", active, grad_branch, preferred_element_type=jnp.float32)
    grad_active = jnp.einsum(
        "td,fd->tf", grad_branch, ffn_back[2], preferred_element_type=jnp.float32
    )
    smooth_up, smooth_up_back = jax.vjp(smooth, upward)
    grad_upward = smooth_up_back(grad_active)[0].astype(jnp.bfloat16)
    grad_w_up = jnp.einsum("td,tf->df", normed_two, grad_upward, preferred_element_type=jnp.float32)
    grad_normed_two = jnp.einsum(
        "tf,df->td", grad_upward, ffn_back[1], preferred_element_type=jnp.float32
    ).reshape(row_count, slot_count, model_width)
    norm_two_value, norm_two_back = jax.vjp(norm_rows, middle, ffn_back[0].astype(jnp.float32))
    grad_middle_norm, grad_gain_two = norm_two_back(grad_normed_two)
    grad_middle = grad_out + grad_middle_norm
    ffn_grads = (grad_gain_two, grad_w_up, grad_w_down)
    ffn_shares = (
        lax.psum_scatter(ffn_grads[0], ("wide", "narrow"), scatter_dimension=0, tiled=True),
        lax.psum_scatter(ffn_grads[1], ("wide", "narrow"), scatter_dimension=0, tiled=True),
        lax.psum_scatter(ffn_grads[2], ("wide", "narrow"), scatter_dimension=0, tiled=True),
    )
    attn_back = (
        lax.all_gather(gain_one, ("wide", "narrow"), axis=0, tiled=True),
        lax.all_gather(w_value, ("wide", "narrow"), axis=0, tiled=True),
        lax.all_gather(w_first, ("wide", "narrow"), axis=1, tiled=True),
        lax.all_gather(b_first, ("wide", "narrow"), axis=1, tiled=True),
        lax.all_gather(w_second, ("wide", "narrow"), axis=1, tiled=True),
        lax.all_gather(b_second, ("wide", "narrow"), axis=0, tiled=True),
        lax.all_gather(w_out, ("wide", "narrow"), axis=0, tiled=True),
    )
    starting = tuple((jnp.zeros(array.shape, jnp.float32) for array in attn_back[1:]))

    def back_row(totals, triple):
        normed, length, grad_row = triple
        before, hidden, probabilities, weights, per_head, joined = attend_forward(
            normed, length, attn_back
        )
        w_value_full, w_first_full, w_second_full, w_out_full = (
            attn_back[1],
            attn_back[2],
            attn_back[4],
            attn_back[6],
        )
        heads_count = w_second_full.shape[0]
        head_size = model_width // heads_count
        grad_attn = grad_row.astype(jnp.bfloat16)
        grad_w_out = jnp.einsum("sd,se->de", joined, grad_attn, preferred_element_type=jnp.float32)
        grad_joined = jnp.einsum(
            "se,de->sd", grad_attn, w_out_full, preferred_element_type=jnp.float32
        ).astype(jnp.bfloat16)
        grad_mixture = grad_joined.reshape(slot_count, heads_count, head_size).transpose(1, 0, 2)
        grad_weights = jnp.einsum(
            "hsc,hjc->hsj", grad_mixture, per_head, preferred_element_type=jnp.float32
        )
        grad_heads = jnp.einsum(
            "hsj,hsc->hjc", weights, grad_mixture, preferred_element_type=jnp.float32
        )
        grad_values = (
            grad_heads.transpose(1, 0, 2).reshape(slot_count, model_width).astype(jnp.bfloat16)
        )
        centre = jnp.sum(probabilities * grad_weights, axis=-1, keepdims=True)
        grad_logits = (probabilities * (grad_weights - centre)).astype(jnp.bfloat16)
        grad_b_second = jnp.sum(grad_logits.astype(jnp.float32), axis=1).reshape(-1)
        grad_w_second = jnp.einsum(
            "hse,hsj->hej", hidden, grad_logits, preferred_element_type=jnp.float32
        )
        grad_hidden = jnp.einsum(
            "hsj,hej->hse", grad_logits, w_second_full, preferred_element_type=jnp.float32
        )
        smooth_value, smooth_back = jax.vjp(smooth, before)
        grad_before = smooth_back(grad_hidden)[0].astype(jnp.bfloat16)
        grad_b_first = jnp.sum(grad_before.astype(jnp.float32), axis=1)
        grad_w_first = jnp.einsum(
            "sd,hse->hde", normed, grad_before, preferred_element_type=jnp.float32
        )
        grad_w_value = jnp.einsum(
            "sd,se->de", normed, grad_values, preferred_element_type=jnp.float32
        )
        grad_normed = jnp.einsum(
            "hse,hde->sd", grad_before, w_first_full, preferred_element_type=jnp.float32
        )
        grad_normed = grad_normed + jnp.einsum(
            "se,de->sd", grad_values, w_value_full, preferred_element_type=jnp.float32
        )
        updated = (
            totals[0] + grad_w_value,
            totals[1] + grad_w_first,
            totals[2] + grad_b_first,
            totals[3] + grad_w_second,
            totals[4] + grad_b_second,
            totals[5] + grad_w_out,
        )
        return (updated, grad_normed)

    totals, grad_normed_one = lax.scan(back_row, starting, (normed_one, lengths, grad_middle))
    norm_one_value, norm_one_back = jax.vjp(norm_rows, inputs, attn_back[0].astype(jnp.float32))
    grad_inputs_norm, grad_gain_one = norm_one_back(grad_normed_one)
    grad_tokens = grad_middle + grad_inputs_norm
    attn_grads = (grad_gain_one, totals[0], totals[1], totals[2], totals[3], totals[4], totals[5])
    attn_shares = (
        lax.psum_scatter(attn_grads[0], ("wide", "narrow"), scatter_dimension=0, tiled=True),
        lax.psum_scatter(attn_grads[1], ("wide", "narrow"), scatter_dimension=0, tiled=True),
        lax.psum_scatter(attn_grads[2], ("wide", "narrow"), scatter_dimension=1, tiled=True),
        lax.psum_scatter(attn_grads[3], ("wide", "narrow"), scatter_dimension=1, tiled=True),
        lax.psum_scatter(attn_grads[4], ("wide", "narrow"), scatter_dimension=1, tiled=True),
        lax.psum_scatter(attn_grads[5], ("wide", "narrow"), scatter_dimension=0, tiled=True),
        lax.psum_scatter(attn_grads[6], ("wide", "narrow"), scatter_dimension=0, tiled=True),
    )
    return (
        result,
        grad_tokens,
        attn_shares[0],
        attn_shares[1],
        attn_shares[2],
        attn_shares[3],
        attn_shares[4],
        attn_shares[5],
        attn_shares[6],
        ffn_shares[0],
        ffn_shares[1],
        ffn_shares[2],
    )


def solution(mesh):
    return jax.shard_map(
        on_device,
        mesh=mesh,
        in_specs=(
            P(("wide", "narrow"), None, None),
            P(("wide", "narrow")),
            P(("wide", "narrow")),
            P(("wide", "narrow"), None),
            P(None, ("wide", "narrow"), None),
            P(None, ("wide", "narrow")),
            P(None, ("wide", "narrow"), None),
            P(("wide", "narrow")),
            P(("wide", "narrow"), None),
            P(("wide", "narrow")),
            P(("wide", "narrow"), None),
            P(("wide", "narrow"), None),
            P(("wide", "narrow"), None, None),
        ),
        out_specs=(
            P(("wide", "narrow"), None, None),
            P(("wide", "narrow"), None, None),
            P(("wide", "narrow")),
            P(("wide", "narrow"), None),
            P(None, ("wide", "narrow"), None),
            P(None, ("wide", "narrow")),
            P(None, ("wide", "narrow"), None),
            P(("wide", "narrow")),
            P(("wide", "narrow"), None),
            P(("wide", "narrow")),
            P(("wide", "narrow"), None),
            P(("wide", "narrow"), None),
        ),
        check_vma=False,
    )
```

profile of v0, /device:TPU:0, one launch (start us, length us, event | category | flops | bytes accessed | tf_op | source)
XLA Modules:
  0.0 1720.4 jit_solution(1639929495453045297)
XLA Ops:
  11.9 1.3 convert_reduce_fusion.2
  13.2 1.5 fusion.44
  14.7 0.8 dynamic-update-slice
  17.3 42.2 %all-reduce.8 = (bf16[6144]{0:T(1024)(128)(2,1)S(1)}, bf16[768]{0:T(1024)(128)(2,1)S(1)}, bf16[768]{0:T(1024)(128)(2,1)S(1)}) all-reduce(bf16[6144]{0:T(1024)(128)(2,1)S(1)} %dynamic-update-slice.1, bf16[768]{0:T(1024)(128)(2,1)S(1)} %dynamic-update-slice, ...), channel_id=1, replica_groups=mesh['wide'=8,'narrow'=4] {'wide','narrow'}, use_global_device_ids=true, to_apply=%add.1 | all-reduce | flops 7680 | bytes 30720
  60.1 68.0 %all-gather = bf16[32,24,12]{1,2,0:T(8,128)(2,1)S(1)} all-gather(bf16[1,24,12]{1,2,0:T(8,128)(2,1)} %bitcast.202), channel_id=1, replica_groups=mesh['wide'=8,'narrow'=4] {'wide','narrow'}, dimensions={0}, use_global_device_ids=true | all-gather | bytes 19008 | tf_op jit(solution)/shard_map/all_gather | solution.py:70
  128.6 2.4 convolution_convert_fusion.1
  131.2 42.3 %all-gather.8.cloned.1.call-done = bf16[12,768,768]{2,1,0:T(8,128)(2,1)} async-done(((bf16[12,24,768]{2,1,0:T(8,128)(2,1)}), bf16[12,768,768]{2,1,0:T(8,128)(2,1)}) %all-gather.8.cloned.1.call-update) | async-done | bytes 14155792 | tf_op jit(solution)/shard_map/all_gather | solution.py:69
  173.6 52.8 %fusion.3 = (bf16[12,512,768]{2,1,0:T(8,128)(2,1)}, f32[12,512,768]{2,1,0:T(8,128)}, f32[512,12,768]{2,0,1:T(8,128)}) fusion(f32[12,768]{1,0:T(8,128)S(1)} %bitcast.200, bf16[12,768,768]{2,1,0:T(8,128)(2,1)} %all-gather.8.cloned.1.call-done, f32[768]{0:T(1024)S(1)} %convert_element_type.112, f32[512]{0:T(512)S(1)} %fusion.74, ...), kind=kOutput, calls=%fused_computation.10 | convolution fusion | flops 7561150464 | bytes 62172160 | tf_op jit(solution)/shard_map/while/body/eval_jaxpr/sd,hde->hse/dot_general | solution.py:32
  226.4 30.3 %all-gather.10.cloned.1.call-done = bf16[12,768,512]{2,1,0:T(8,128)(2,1)} async-done(((bf16[12,24,512]{2,1,0:T(8,128)(2,1)}), bf16[12,768,512]{2,1,0:T(8,128)(2,1)}) %all-gather.10.cloned.1.call-update) | async-done | bytes 9437200 | tf_op jit(solution)/shard_map/all_gather | solution.py:71
  256.7 14.2 fusion.90
  270.9 5.8 fusion.48
  276.8 35.3 %all-gather.14.cloned.1.call-done = bf16[768,768]{1,0:T(8,128)(2,1)} async-done(((bf16[24,768]{1,0:T(8,128)(2,1)}), bf16[768,768]{1,0:T(8,128)(2,1)}) %all-gather.14.cloned.1.call-update) | async-done | bytes 1179664 | tf_op jit(solution)/shard_map/all_gather | solution.py:73
  312.1 2.2 fusion.91
  314.6 62.7 %all-gather.16.cloned.1.call-done = bf16[768,3072]{1,0:T(8,128)(2,1)} async-done(((bf16[24,3072]{1,0:T(8,128)(2,1)}), bf16[768,3072]{1,0:T(8,128)(2,1)}) %all-gather.16.cloned.1.call-update) | async-done | bytes 4718608 | tf_op jit(solution)/shard_map/all_gather | solution.py:86
  377.3 19.6 %multiply_convert_fusion.1 = (bf16[512,3072]{1,0:T(8,128)(2,1)}, f32[512,3072]{1,0:T(8,128)}, f32[512,3072]{1,0:T(8,128)}) fusion(bf16[768,3072]{1,0:T(8,128)(2,1)} %all-gather.16.cloned.1.call-done, f32[1,512,768]{2,1,0:T(8,128)S(1)} %get-tuple-element.166, f32[768]{0:T(1024)S(1)} %copy-done.8, f32[512]{0:T(512)S(1)} %fusion.75, ...), kind=kOutput, calls=%fused_computation.41 | convolution fusion | flops 2519728128 | bytes 22027264 | tf_op jit(solution)/shard_map/dot_general | solution.py:94
  396.8 45.5 %all-gather.18.cloned.1.call-done = bf16[3072,768]{1,0:T(8,128)(2,1)} async-done(((bf16[96,768]{1,0:T(8,128)(2,1)}), bf16[3072,768]{1,0:T(8,128)(2,1)}) %all-gather.18.cloned.1.call-update) | async-done | bytes 4718608 | tf_op jit(solution)/shard_map/all_gather | solution.py:87
  442.3 8.3 add_convert_fusion
  450.6 3.4 fusion.46
  455.3 1.7 convolution_convert_fusion
  457.0 2.3 copy.65
  459.3 7.8 fusion.51
  467.1 9.0 multiply_reduce_fusion
  476.1 8.6 convert_reduce_fusion.1
  485.3 3.5 fusion.94
  488.8 25.1 %convert_reduce_fusion = (f32[12,768]{1,0:T(8,128)}, bf16[12,512,768]{2,1,0:T(8,128)(2,1)}) fusion(f32[12,512,768]{2,1,0:T(8,128)} %get-tuple-element.161, f32[512,12,768]{2,0,1:T(8,128)} %get-tuple-element.162, f32[12,768]{1,0:T(8,128)S(1)} %bitcast.201, bf16[12,512,512]{1,2,0:T(8,128)(2,1)} %get-tuple-element.153, ...), kind=kOutput, calls=%fused_computation.17 | convolution fusion | flops 4912045056 | bytes 62988288 | tf_op jit(solution)/shard_map/while/body/eval_jaxpr/hsj,hej->hse/dot_general | solution.py:168
  514.0 15.5 fusion.45
  529.5 3.1 fusion.43
  532.7 16.2 convolution_bitcast_fusion
  548.9 33.6 %copy.71 = f32[12,768,768]{2,0,1:T(8,128)} copy(f32[12,768,768]{1,2,0:T(8,128)} %convolution_bitcast_fusion) | data formatting | bytes 56623104 | tf_op jit(solution)/shard_map/while/body/eval_jaxpr/sd,hse->hde/transpose | solution.py:174
  582.6 3.9 fusion.68
  586.6 3.3 fusion.55
  590.0 7.2 fusion.78
  597.2 8.6 fusion.58
  605.9 13.7 fusion.95
  619.6 3.3 add_add_fusion.2
  622.9 7.0 bitcast_add_fusion.1
  630.0 22.8 %all-reduce.11.cloned.1.call-done = (f32[768]{0:T(1024)}, f32[12,768]{1,0:T(8,128)}, f32[6144]{0:T(1024)}, f32[768]{0:T(1024)}) async-done(((f32[768]{0:T(1024)}, f32[12,768]{1,0:T(8,128)}, f32[6144]{0:T(1024)}, f32[768]{0:T(1024)}), (f32[768]{0:T(1024)}, f32[12,768]{1,0:T(8,128)}, f32[6144]{0:T(1024)}, f32[768]{0:T(1024)})) %all-reduce.11.cloned.1.call-update) | async-done | bytes 67600
  652.8 1.3 dynamic-slice
  654.1 1.3 dynamic-slice.3
  655.3 1.3 dynamic-slice.2
  656.6 1.4 constant_dynamic-slice_fusion
  658.0 351.7 %reduce-scatter.10.cloned.1.call-done = f32[12,24,768]{2,0,1:T(8,128)} async-done(((f32[12,768,768]{2,0,1:T(8,128)}), f32[12,24,768]{2,0,1:T(8,128)}) %reduce-scatter.10.cloned.1.call-update) | async-done | bytes 884752 | tf_op jit(solution)/shard_map/reduce_scatter | solution.py:204
  1009.7 2.7 copy.74
  1012.4 102.2 %reduce-scatter.8.cloned.1.call-done = f32[24,768]{1,0:T(8,128)} async-done(((f32[768,768]{1,0:T(8,128)}), f32[24,768]{1,0:T(8,128)}) %reduce-scatter.8.cloned.1.call-update) | async-done | bytes 73744 | tf_op jit(solution)/shard_map/reduce_scatter | solution.py:203
  1114.6 103.7 %reduce-scatter.14.cloned.1.call-done = f32[24,768]{1,0:T(8,128)} async-done(((f32[768,768]{1,0:T(8,128)}), f32[24,768]{1,0:T(8,128)}) %reduce-scatter.14.cloned.1.call-update) | async-done | bytes 73744 | tf_op jit(solution)/shard_map/reduce_scatter | solution.py:208
  1218.4 142.1 %reduce-scatter.16.cloned.1.call-done = f32[24,3072]{1,0:T(8,128)} async-done(((f32[768,3072]{1,0:T(8,128)}), f32[24,3072]{1,0:T(8,128)}) %reduce-scatter.16.cloned.1.call-update) | async-done | bytes 294928 | tf_op jit(solution)/shard_map/reduce_scatter | solution.py:120
  1360.5 140.8 %reduce-scatter.18.cloned.1.call-done = f32[96,768]{1,0:T(8,128)} async-done(((f32[3072,768]{1,0:T(8,128)}), f32[96,768]{1,0:T(8,128)}) %reduce-scatter.18.cloned.1.call-update) | async-done | bytes 294928 | tf_op jit(solution)/shard_map/reduce_scatter | solution.py:121
  1501.3 212.4 %reduce-scatter.12.cloned.1.call-done = f32[12,24,512]{2,1,0:T(8,128)} async-done(((f32[12,768,512]{2,1,0:T(8,128)}), f32[12,24,512]{2,1,0:T(8,128)}) %reduce-scatter.12.cloned.1.call-update) | async-done | bytes 589840 | tf_op jit(solution)/shard_map/reduce_scatter | solution.py:206
  (97 shorter events, 9.6 us)
Async XLA Ops:
  7.2 166.4 %copy-start = (bf16[1,512,768]{2,1,0:T(8,128)(2,1)S(1)}, bf16[1,512,768]{2,1,0:T(8,128)(2,1)}, u32[]{:S(2)}) copy-start(bf16[1,512,768]{2,1,0:T(8,128)(2,1)} %param.13) | copy-start | bytes 2359300
  7.2 121.4 %all-gather.12.cloned.1.call-start = ((), (), s32[]{:S(2)}) async-start(), calls=%async_computation.8 | async-start | bytes 1216512 | tf_op jit(solution)/shard_map/all_gather | solution.py:68
  7.9 165.6 %all-gather.8.cloned.1.call-start = ((), (), s32[]{:S(2)}) async-start(), calls=%async_computation.6 | async-start | bytes 14598144 | tf_op jit(solution)/shard_map/all_gather | solution.py:69
  8.7 248.0 %all-gather.10.cloned.1.call-start = ((), (), s32[]{:S(2)}) async-start(), calls=%async_computation.7 | async-start | bytes 9732096 | tf_op jit(solution)/shard_map/all_gather | solution.py:71
  9.4 302.7 %all-gather.14.cloned.1.call-start = ((), (), s32[]{:S(2)}) async-start(), calls=%async_computation.9 | async-start | bytes 1216512 | tf_op jit(solution)/shard_map/all_gather | solution.py:73
  10.0 367.3 %all-gather.16.cloned.1.call-start = ((), (), s32[]{:S(2)}) async-start(), calls=%async_computation.10 | async-start | bytes 4866048 | tf_op jit(solution)/shard_map/all_gather | solution.py:86
  10.6 431.7 %all-gather.18.cloned.1.call-start = ((), (), s32[]{:S(2)}) async-start(), calls=%async_computation.11 | async-start | bytes 4866048 | tf_op jit(solution)/shard_map/all_gather | solution.py:87
  11.1 641.7 %all-reduce.11.cloned.1.call-start = ((), (), s32[]{:S(2)}) async-start(), calls=%async_computation.18 | async-start | bytes 163840
  13.2 213.2 %copy-start.13 = (f32[512]{0:T(512)}, f32[512]{0:T(512)S(1)}, u32[]{:S(2)}) copy-start(f32[512]{0:T(512)S(1)} %broadcast_multiply_fusion.1) | copy-start | bytes 6148
  14.7 44.8 %copy-start.15 = (f32[512]{0:T(512)}, f32[512]{0:T(512)S(1)}, u32[]{:S(2)}) copy-start(f32[512]{0:T(512)S(1)} %fusion.44) | copy-start | bytes 6148
  14.7 211.7 %copy-start.11 = (f32[512]{0:T(512)}, f32[512]{0:T(512)S(1)}, u32[]{:S(2)}) copy-start(f32[512]{0:T(512)S(1)} %fusion.74) | copy-start | bytes 6148
  59.5 166.9 %copy-start.9 = (f32[768]{0:T(1024)}, f32[768]{0:T(1024)S(1)}, u32[]{:S(2)}) copy-start(f32[768]{0:T(1024)S(1)} %convert_element_type.112) | copy-start | bytes 9220
  131.2 139.7 %copy-start.5 = (bf16[512,768]{0,1:T(8,128)(2,1)}, bf16[512,768]{0,1:T(8,128)(2,1)S(1)}, u32[]{:S(2)}) copy-start(bf16[512,768]{0,1:T(8,128)(2,1)S(1)} %copy.63) | copy-start | bytes 2359300
  270.9 106.3 %copy-start.8 = (f32[768]{0:T(1024)S(1)}, f32[768]{0:T(1024)}, u32[]{:S(2)}) copy-start(f32[768]{0:T(1024)} %convert_element_type.121) | copy-start | bytes 9220
  276.7 37.8 %copy-start.4 = (bf16[12,512,64]{1,2,0:T(8,128)(2,1)}, bf16[12,512,64]{1,2,0:T(8,128)(2,1)S(1)}, u32[]{:S(2)}) copy-start(bf16[12,512,64]{1,2,0:T(8,128)(2,1)S(1)} %fusion.48) | copy-start | bytes 2359300
  314.6 127.7 %copy-start.1 = (f32[1,512,768]{2,1,0:T(8,128)S(1)}, f32[1,512,768]{2,1,0:T(8,128)}, u32[]{:S(2)}) copy-start(f32[1,512,768]{2,1,0:T(8,128)} %param.25) | copy-start | bytes 4718596
  442.3 8.3 copy-start.17
  450.6 3.4 copy-start.3
  450.6 4.1 copy-start.2
  454.0 1.3 copy-start.18
  459.3 7.8 copy-start.6
  459.3 7.8 copy-start.7
  459.3 16.8 slice-start
  459.3 16.8 slice-start.1
  467.1 9.0 slice-start.2
  488.8 25.2 %copy-start.10 = (f32[768]{0:T(1024)S(1)}, f32[768]{0:T(1024)}, u32[]{:S(2)}) copy-start(f32[768]{0:T(1024)} %copy-done.9) | copy-start | bytes 9220
  488.8 25.2 %copy-start.14 = (f32[512]{0:T(512)S(1)}, f32[512]{0:T(512)}, u32[]{:S(2)}) copy-start(f32[512]{0:T(512)} %copy-done.13) | copy-start | bytes 6148
  513.9 15.5 copy-start.16
  513.9 15.6 copy-start.12
  532.6 477.1 %reduce-scatter.10.cloned.1.call-start = ((), (), s32[]{:S(2)}) async-start(), calls=%async_computation.13 | async-start | bytes 38928384 | tf_op jit(solution)/shard_map/reduce_scatter | solution.py:204
  582.6 532.0 %reduce-scatter.8.cloned.1.call-start = ((), (), s32[]{:S(2)}) async-start(), calls=%async_computation.12 | async-start | bytes 2433024 | tf_op jit(solution)/shard_map/reduce_scatter | solution.py:203
  586.5 631.8 %reduce-scatter.14.cloned.1.call-start = ((), (), s32[]{:S(2)}) async-start(), calls=%async_computation.15 | async-start | bytes 2433024 | tf_op jit(solution)/shard_map/reduce_scatter | solution.py:208
  589.9 770.5 %reduce-scatter.16.cloned.1.call-start = ((), (), s32[]{:S(2)}) async-start(), calls=%async_computation.16 | async-start | bytes 9732096 | tf_op jit(solution)/shard_map/reduce_scatter | solution.py:120
  597.2 904.1 %reduce-scatter.18.cloned.1.call-start = ((), (), s32[]{:S(2)}) async-start(), calls=%async_computation.17 | async-start | bytes 9732096 | tf_op jit(solution)/shard_map/reduce_scatter | solution.py:121
  605.8 1107.9 %reduce-scatter.12.cloned.1.call-start = ((), (), s32[]{:S(2)}) async-start(), calls=%async_computation.14 | async-start | bytes 19464192 | tf_op jit(solution)/shard_map/reduce_scatter | solution.py:206
Sparse Core Ops, SparseCore 0:
  10.8 57.1 all-gather.11
  71.1 102.4 all-gather.7
  176.5 80.1 all-gather.9
  259.4 52.6 all-gather.13
  314.7 62.4 all-gather.15
  379.9 62.3 all-gather.17
  532.8 119.9 all-reduce.10
  659.2 350.4 reduce-scatter.9
  1016.5 98.1 reduce-scatter.7
  1120.4 97.9 reduce-scatter.13
  1225.9 134.5 reduce-scatter.15
  1366.8 134.4 reduce-scatter.17
  1509.4 204.2 reduce-scatter.11
where the time goes:
time: 1730 us; the launch traced here: 1720 us
  waiting for transfers between devices  1300 us (75%)
  matrix products  231 us (13%)
  blocking collectives  110 us (6%)
  local copies, waits for them, and re-layouts  48.1 us (3%)
  other arithmetic  19.7 us (1%)
    reduce_scatter x1, waiting for transfers between devices, on_device(): lax.psum_scatter(attn_grads[2], ('wide', 'narrow'), scatter_dimension=1,...  352 us
    reduce_scatter x1, waiting for transfers between devices, on_device(): lax.psum_scatter(attn_grads[4], ('wide', 'narrow'), scatter_dimension=1,...  212 us
    reduce_scatter x1, waiting for transfers between devices, on_device(): lax.psum_scatter(ffn_grads[1], ('wide', 'narrow'), scatter_dimension=0, t...  142 us
    reduce_scatter x1, waiting for transfers between devices, on_device(): lax.psum_scatter(ffn_grads[2], ('wide', 'narrow'), scatter_dimension=0, t...  141 us
    reduce_scatter x1, waiting for transfers between devices, on_device(): lax.psum_scatter(attn_grads[6], ('wide', 'narrow'), scatter_dimension=0,...  104 us
    reduce_scatter x1, waiting for transfers between devices, on_device(): lax.psum_scatter(attn_grads[1], ('wide', 'narrow'), scatter_dimension=0,...  102 us
    all_gather x1, blocking collectives, on_device(): lax.all_gather(b_first, ('wide', 'narrow'), axis=1, tiled=True)  68 us
    all_gather x1, waiting for transfers between devices, on_device(): lax.all_gather(w_up, ('wide', 'narrow'), axis=0, tiled=True)  62.7 us
  transfers between devices with their start and end apart: 13, of which 12 were waited for; matrix products, arithmetic and copies ran while one was open for 12% of the time, Pallas kernels for 0%

commit v1 on v0

v1 whole, which is shorter than its diff:
```python
import jax
import jax.numpy as jnp
from jax import lax
from jax.sharding import Mesh
from jax.sharding import PartitionSpec as P

epsilon = 1e-05
f32 = jnp.float32
bf16 = jnp.bfloat16
GROUP = 4


def norm_rows(values, factor):
    average = jnp.mean(values, axis=-1, keepdims=True)
    centred = values - average
    spread = jnp.mean(centred * centred, axis=-1, keepdims=True)
    return centred * lax.rsqrt(spread + epsilon) * factor


def smooth(values):
    return jax.nn.gelu(values, approximate=False)


def mm(spec, a, b):
    return jnp.einsum(spec, a, b, preferred_element_type=f32)


REST = ("rep", "narrow")
ALL = ("tp", "rep", "narrow")


def to_heads(shard):
    heads, depth, width = shard.shape
    pieces = lax.all_to_all(shard.reshape(GROUP, heads // GROUP, depth, width), "tp", 0, 0)
    whole = lax.all_gather(pieces, REST, axis=0)
    return whole.transpose(2, 1, 0, 3, 4).reshape(heads // GROUP, -1, width)


def from_heads(grad):
    heads, depth, width = grad.shape
    n = lax.axis_size("rep") * lax.axis_size("narrow")
    pieces = grad.astype(bf16).reshape(heads, GROUP, n, depth // (GROUP * n), width).transpose(2, 1, 0, 3, 4)
    pieces = pieces.reshape((n * GROUP,) + pieces.shape[2:])
    share = lax.psum_scatter(pieces, REST, scatter_dimension=0, tiled=True)
    share = lax.all_to_all(share, "tp", 0, 0)
    return share.reshape(heads * GROUP, depth // (GROUP * n), width).astype(f32)


def on_device(tokens, lengths, gain_one, w_value, w_first, b_first, w_second, b_second, w_out, gain_two, w_up, w_down, grad_out):
    row_count, slots, width = tokens.shape
    heads_all = w_first.shape[0]
    heads = heads_all // GROUP
    head_size = width // heads_all
    me = lax.axis_index("tp")
    depth = w_value.shape[0]

    small = [gain_one, gain_two, b_second, b_first.reshape(-1)]
    gathered = lax.all_gather(jnp.concatenate(small), ALL, axis=0)
    n_all = gathered.shape[0]
    g1 = gathered[:, :depth].reshape(-1).astype(f32)
    g2 = gathered[:, depth : 2 * depth].reshape(-1).astype(f32)
    b2_len = b_second.shape[0]
    b2 = gathered[:, 2 * depth : 2 * depth + b2_len].reshape(heads_all, slots).astype(f32)
    b1 = gathered[:, 2 * depth + b2_len :].reshape(n_all, heads_all, depth).transpose(1, 0, 2).reshape(heads_all, width).astype(f32)
    b1 = lax.dynamic_slice_in_dim(b1, me * heads, heads, 0)
    b2 = lax.dynamic_slice_in_dim(b2, me * heads, heads, 0)

    wf = to_heads(w_first)
    ws = to_heads(w_second)
    wv = to_heads(w_value.reshape(depth, GROUP, width // GROUP).transpose(1, 0, 2))[0]
    rows = lax.all_gather(tokens, "tp", axis=0, tiled=True)
    lens = lax.all_gather(lengths, "tp", axis=0, tiled=True)
    n_rows = rows.shape[0]

    normed = norm_rows(rows.astype(f32), g1).astype(bf16)
    values = mm("rsd,de->rse", normed, wv).astype(bf16)
    per_head = values.reshape(n_rows, slots, heads, head_size).transpose(2, 0, 1, 3)
    before = mm("rsd,hde->hrse", normed, wf) + b1[:, None, None, :]
    hidden = smooth(before).astype(bf16)
    logits = mm("hrse,hej->hrsj", hidden, ws) + b2[:, None, None, :]
    visible = lax.broadcasted_iota(jnp.int32, (1, n_rows, 1, slots), 3) < lens[None, :, None, None]
    masked = jnp.where(visible, logits, f32(-1e30))
    scaled = jnp.exp(masked - jnp.max(masked, axis=-1, keepdims=True))
    probabilities = scaled / jnp.sum(scaled, axis=-1, keepdims=True)
    weights = probabilities.astype(bf16)
    mixture = mm("hrsj,hrjc->rshc", weights, per_head).astype(bf16)
    mixture = mixture.reshape(GROUP, row_count, slots, heads * head_size)
    joined = lax.all_to_all(mixture, "tp", 0, 0).transpose(1, 2, 0, 3).reshape(row_count * slots, width)

    wo = lax.all_gather(w_out, ALL, axis=0, tiled=True)
    wu = lax.all_gather(w_up, ALL, axis=0, tiled=True)
    wd = lax.all_gather(w_down, ALL, axis=0, tiled=True)
    inputs = tokens.astype(f32).reshape(-1, width)
    middle = inputs + mm("sd,de->se", joined, wo)
    normed_two, norm_two_back = jax.vjp(norm_rows, middle, g2)
    normed_two = normed_two.astype(bf16)
    upward = mm("td,df->tf", normed_two, wu)
    active, smooth_up_back = jax.vjp(smooth, upward)
    active = active.astype(bf16)
    result = middle + mm("tf,fd->td", active, wd)

    g_out = grad_out.reshape(-1, width)
    grad_branch = g_out.astype(bf16)
    grad_w_down = mm("tf,td->fd", active, grad_branch)
    grad_upward = smooth_up_back(mm("td,fd->tf", grad_branch, wd))[0].astype(bf16)
    grad_w_up = mm("td,tf->df", normed_two, grad_upward)
    grad_middle_norm, grad_gain_two = norm_two_back(mm("tf,df->td", grad_upward, wu))
    grad_middle = g_out + grad_middle_norm
    grad_attn = grad_middle.astype(bf16)
    grad_w_out = mm("sd,se->de", joined, grad_attn)
    grad_joined = mm("se,de->sd", grad_attn, wo).astype(bf16)

    grad_mixture = grad_joined.reshape(row_count, slots, GROUP, heads * head_size).transpose(2, 0, 1, 3)
    grad_mixture = lax.all_to_all(grad_mixture, "tp", 0, 0).reshape(n_rows, slots, heads, head_size).transpose(2, 0, 1, 3)
    grad_weights = mm("hrsc,hrjc->hrsj", grad_mixture, per_head)
    grad_values = mm("hrsj,hrsc->rjhc", weights, grad_mixture).astype(bf16).reshape(n_rows, slots, heads * head_size)
    centre = jnp.sum(probabilities * grad_weights, axis=-1, keepdims=True)
    grad_logits = (probabilities * (grad_weights - centre)).astype(bf16)
    grad_b_second = jnp.sum(grad_logits.astype(f32), axis=(1, 2))
    grad_w_second = mm("hrse,hrsj->hej", hidden, grad_logits)
    grad_hidden = mm("hrsj,hej->hrse", grad_logits, ws)
    smooth_value, smooth_back = jax.vjp(smooth, before)
    grad_before = smooth_back(grad_hidden)[0].astype(bf16)
    grad_b_first = jnp.sum(grad_before.astype(f32), axis=(1, 2))
    grad_w_first = mm("rsd,hrse->hde", normed, grad_before)
    grad_w_value = mm("rsd,rse->de", normed, grad_values)
    grad_normed = mm("hrse,hde->rsd", grad_before, wf) + mm("rse,de->rsd", grad_values, wv)
    grad_normed = lax.psum_scatter(grad_normed.astype(bf16), "tp", scatter_dimension=0, tiled=True)
    value, norm_one_back = jax.vjp(norm_rows, inputs, g1)
    grad_inputs_norm, grad_gain_one = norm_one_back(grad_normed.astype(f32).reshape(-1, width))
    grad_tokens = grad_middle + grad_inputs_norm

    out_first = from_heads(grad_w_first)
    out_second = from_heads(grad_w_second)
    out_value = from_heads(grad_w_value[None]).transpose(1, 0, 2).reshape(depth, width)

    def share(grad):
        return lax.psum_scatter(grad.astype(bf16), ALL, scatter_dimension=0, tiled=True).astype(f32)

    vec_tp = jnp.concatenate([grad_b_first.reshape(-1), grad_b_second.reshape(-1)])
    vec_tp = lax.dynamic_update_slice_in_dim(jnp.zeros((GROUP, vec_tp.shape[0]), f32), vec_tp[None], me, 0)
    vec = jnp.concatenate([vec_tp.reshape(-1), grad_gain_one, grad_gain_two])
    vec = lax.psum(vec, ALL)
    index = (me * lax.axis_size("rep") + lax.axis_index("rep")) * lax.axis_size("narrow") + lax.axis_index("narrow")
    n_tp = GROUP * (heads * width + heads * slots)
    tp_part = vec[:n_tp].reshape(GROUP, -1)
    gb1 = tp_part[:, : heads * width].reshape(heads_all, width)
    gb2 = tp_part[:, heads * width :].reshape(-1)
    gb1 = lax.dynamic_slice_in_dim(gb1, index * depth, depth, 1)
    gb2 = lax.dynamic_slice_in_dim(gb2, index * b2_len, b2_len, 0)
    gg1 = lax.dynamic_slice_in_dim(vec[n_tp : n_tp + width], index * depth, depth, 0)
    gg2 = lax.dynamic_slice_in_dim(vec[n_tp + width :], index * depth, depth, 0)
    shape = tokens.shape
    return (
        result.reshape(shape),
        grad_tokens.reshape(shape),
        gg1,
        out_value,
        out_first,
        gb1,
        out_second,
        gb2,
        share(grad_w_out),
        gg2,
        share(grad_w_up),
        share(grad_w_down),
    )


def solution(mesh):
    wide, narrow = mesh.shape["wide"], mesh.shape["narrow"]
    grouped = Mesh(mesh.devices.reshape(GROUP, wide // GROUP, narrow), ALL)
    vec = P(ALL)
    flat = P(ALL, None)
    mid = P(None, ALL, None)
    row = P(ALL, None, None)
    return jax.shard_map(
        on_device,
        mesh=grouped,
        in_specs=(row, vec, vec, flat, mid, P(None, ALL), mid, vec, flat, vec, flat, flat, row),
        out_specs=(row, row, vec, flat, mid, P(None, ALL), mid, vec, flat, vec, flat, flat),
        check_vma=False,
    )
```

time: 1730 us -> 1120 us (0.65)
  waiting for transfers between devices: 1300 us -> 670 us
  other arithmetic: 19.7 us -> 62.3 us
  matrix products: 231 us -> 201 us
  local copies, waits for them, and re-layouts: 48.1 us -> 28.3 us
  starting transfers between devices: 0.52 us -> 18.8 us
    reduce_scatter x6, waiting for transfers between devices: 1050 us -> 455 us  [the longest x3 317 us: share(): lax.psum_scatter(grad.astype(bf16), ALL, scatter_dimension=0, tiled=True)]
    all_gather x6, waiting for transfers between devices: 216 us -> 74.5 us  [the longest x1 45.6 us: on_device(): wd = lax.all_gather(w_down, ALL, axis=0, tiled=True)]
    psum x0 -> x1, waiting for transfers between devices: none -> 120 us  [on_device(): vec = lax.psum(vec, ALL)]
    all_gather x1, blocking collectives: 68 us -> 27.6 us  [to_heads(): whole = lax.all_gather(pieces, REST, axis=0)]
    all_to_all x0 -> x3, blocking collectives: none -> 39.2 us  [the longest x2 23.3 us: to_heads(): lax.all_to_all(shard.reshape(GROUP, heads // GROUP, depth, width), 'tp',...]
    sub x0 -> x2, other arithmetic: none -> 29.9 us  [the longest x1 22.7 us: on_device(): grad_logits = (probabilities * (grad_weights - centre)).astype(bf16)]
    transpose x1 -> x4, local copies, waits for them, and re-layouts: 33.6 us -> 6.6 us  [the longest x3 5.83 us: to_heads(): return whole.transpose(2, 1, 0, 3, 4).reshape(heads // GROUP, -1, width)]
    unnamed x14 -> x15, waiting for transfers between devices: 26.6 us -> 4.92 us
  transfers between devices with their start and end apart: 13 -> 19, of which waited for: 12 -> 13; matrix products, arithmetic and copies ran while one was open for 12% -> 18% of each run, Pallas kernels for 0% -> 0%
where the time goes in v1:
time: 1120 us; the launch traced here: 1110 us
  waiting for transfers between devices  670 us (60%)
  matrix products  201 us (18%)
  blocking collectives  117 us (10%)
  other arithmetic  62.3 us (6%)
  local copies, waits for them, and re-layouts  28.3 us (3%)
  starting transfers between devices  18.8 us (2%)
  between operations  15.6 us (1%)
    reduce_scatter x3, waiting for transfers between devices, share(): lax.psum_scatter(grad.astype(bf16), ALL, scatter_dimension=0, tiled=True)  317 us
    dot_general x21, matrix products, mm(): return jnp.einsum(spec, a, b, preferred_element_type=f32)  201 us
    reduce_scatter x3, waiting for transfers between devices, from_heads(): share = lax.psum_scatter(pieces, REST, scatter_dimension=0, tiled=True)  138 us
    psum x1, waiting for transfers between devices, on_device(): vec = lax.psum(vec, ALL)  120 us
    unnamed x2, blocking collectives  49.9 us
    all_gather x1, waiting for transfers between devices, on_device(): wd = lax.all_gather(w_down, ALL, axis=0, tiled=True)  45.6 us
    all_gather x1, blocking collectives, to_heads(): whole = lax.all_gather(pieces, REST, axis=0)  27.6 us
    all_to_all x2, blocking collectives, to_heads(): lax.all_to_all(shard.reshape(GROUP, heads // GROUP, depth, width), 'tp',...  23.3 us
  transfers between devices with their start and end apart: 19, of which 13 were waited for; matrix products, arithmetic and copies ran while one was open for 18% of the time, Pallas kernels for 0%

profile of v1, /device:TPU:0, one launch (start us, length us, event | category | flops | bytes accessed | tf_op | source)
XLA Modules:
  0.0 1113.2 jit_solution(6259310267432662958)
XLA Ops:
  7.2 12.1 %all_to_all.40 = bf16[4,3,24,512]{3,2,1,0:T(8,128)(2,1)} all-to-all(bf16[4,3,24,512]{3,2,1,0:T(8,128)(2,1)} %bitcast.306), channel_id=1, replica_groups=mesh['tp'=4,'rep'=2,'narrow'=4] {'tp'}, dimensions={0} | all-to-all | bytes 589824 | tf_op jit(solution)/shard_map/all_to_all | solution.py:34
  20.1 11.3 %all_to_all.41 = bf16[4,3,24,768]{3,2,1,0:T(8,128)(2,1)} all-to-all(bf16[4,3,24,768]{3,2,1,0:T(8,128)(2,1)} %bitcast.305), channel_id=1, replica_groups=mesh['tp'=4,'rep'=2,'narrow'=4] {'tp'}, dimensions={0} | all-to-all | bytes 884736 | tf_op jit(solution)/shard_map/all_to_all | solution.py:34
  34.1 3.3 all-to-all-start
  39.8 41.6 %all-reduce = bf16[16896]{0:T(1024)(128)(2,1)S(1)} all-reduce(bf16[16896]{0:T(1024)(128)(2,1)S(1)} %dynamic-update-slice), channel_id=2, replica_groups=mesh['tp'=4,'rep'=2,'narrow'=4] {'tp','rep','narrow'}, use_global_device_ids=true, to_apply=%add | all-reduce | flops 16896 | bytes 67584
  85.5 8.3 all-reduce.1
  95.7 27.6 %all-gather.1 = bf16[32,1,24,192]{3,2,1,0:T(8,128)(2,1)S(1)} all-gather(bf16[4,1,24,192]{3,2,1,0:T(8,128)(2,1)S(1)} %all-to-all-done), channel_id=3, replica_groups=mesh['tp'=4,'rep'=2,'narrow'=4] {'rep','narrow'}, dimensions={0}, use_global_device_ids=true | all-gather | bytes 331776 | tf_op jit(solution)/shard_map/all_gather | solution.py:35
  123.4 3.5 copy.108
  126.9 2.5 convert_reduce_fusion.2
  129.5 3.0 fusion.31
  133.0 2.8 convolution_convert_fusion.4
  135.9 7.6 all-gather.19.cloned.1.call-done
  145.8 50.2 %fusion.4 = (bf16[3,4,512,768]{3,2,0,1:T(8,128)(2,1)}, f32[3,4,512,768]{3,2,0,1:T(8,128)}, f32[4,512,3,768]{3,1,2,0:T(8,128)}) fusion(f32[3,768]{1,0:T(4,128)S(1)} %copy-done.25, bf16[3,768,768,1]{2,1,0,3:T(8,128)(2,1)S(1)} %bitcast.283, f32[768]{0:T(1024)S(1)} %reshape.286, f32[4,512]{1,0:T(4,128)S(1)} %copy-done.30, ...), kind=kOutput, calls=%fused_computation.11 | convolution fusion | flops 7567048704 | bytes 53899264 | tf_op jit(solution)/shard_map/rsd,hde->hrse/dot_general | solution.py:25
  196.1 8.0 fusion.25
  204.1 7.2 fusion.103
  211.3 9.1 fusion.96
  220.5 4.9 fusion.72
  225.3 3.5 all-to-all-start.3
  229.2 11.5 %all-to-all-done.3 = bf16[4,1,512,192]{2,3,1,0:T(8,128)(2,1)S(1)} async-done(((bf16[4,1,512,192]{2,3,1,0:T(8,128)(2,1)}), bf16[4,1,512,192]{2,3,1,0:T(8,128)(2,1)S(1)}, u32[]{:S(2)}, u32[]{:S(2)}) %all-to-all-start.3) | async-done | bytes 786464 | tf_op jit(solution)/shard_map/all_to_all | solution.py:88
  243.5 21.4 %all-gather.15.cloned.1.call-done = bf16[768,3072]{1,0:T(8,128)(2,1)} async-done(((bf16[24,3072]{1,0:T(8,128)(2,1)}), bf16[768,3072]{1,0:T(8,128)(2,1)}) %all-gather.15.cloned.1.call-update) | async-done | bytes 4718608 | tf_op jit(solution)/shard_map/all_gather | solution.py:91
  264.9 19.5 %multiply_convert_fusion.1 = (bf16[512,3072]{1,0:T(8,128)(2,1)}, f32[512,3072]{1,0:T(8,128)}, f32[512,3072]{1,0:T(8,128)}) fusion(bf16[768,3072]{1,0:T(8,128)(2,1)} %all-gather.15.cloned.1.call-done, f32[512,768]{1,0:T(8,128)S(1)} %get-tuple-element.34, f32[768]{0:T(1024)S(1)} %reshape.289, f32[512]{0:T(512)S(1)} %fusion.88, ...), kind=kOutput, calls=%fused_computation.54 | convolution fusion | flops 2519728128 | bytes 22027264 | tf_op jit(solution)/shard_map/td,df->tf/dot_general | solution.py:25
  284.3 45.6 %all-gather.17.cloned.1.call-done = bf16[3072,768]{1,0:T(8,128)(2,1)} async-done(((bf16[96,768]{1,0:T(8,128)(2,1)}), bf16[3072,768]{1,0:T(8,128)(2,1)}) %all-gather.17.cloned.1.call-update) | async-done | bytes 4718608 | tf_op jit(solution)/shard_map/all_gather | solution.py:92
  329.9 10.6 add_convert_fusion
  340.5 3.4 multiply_reduce_fusion.1
  349.3 15.9 %all_to_all.42 = bf16[4,1,512,192]{2,3,1,0:T(8,128)(2,1)S(1)} all-to-all(bf16[4,1,512,192]{2,3,1,0:T(8,128)(2,1)} %bitcast.290), channel_id=1, replica_groups=mesh['tp'=4,'rep'=2,'narrow'=4] {'tp'}, dimensions={0} | all-to-all | bytes 1572864 | tf_op jit(solution)/shard_map/all_to_all | solution.py:114
  365.2 7.6 fusion.80
  372.8 22.7 %convert_reduce_fusion.1 = (f32[3,512]{1,0:T(4,128)}, bf16[3,4,512,512]{2,3,1,0:T(8,128)(2,1)}) fusion(f32[3,4,512,512]{2,3,1,0:T(8,128)} %fusion.80, f32[3,4,512,512]{2,3,1,0:T(8,128)} %get-tuple-element.32, f32[3,4,512]{2,1,0:T(4,128)S(1)} %get-tuple-element.31), kind=kOutput, calls=%fused_computation.32 | output fusion | flops 25170944 | bytes 31488000 | tf_op jit(solution)/shard_map/sub | solution.py:118
  398.6 22.3 %convert_reduce_fusion = (f32[3,768]{1,0:T(4,128)}, bf16[3,4,512,768]{3,2,0,1:T(8,128)(2,1)}) fusion(f32[3,4,512,768]{3,2,0,1:T(8,128)} %get-tuple-element.23, bf16[3,768,512,1]{2,1,0,3:T(8,128)(2,1)} %bitcast.292, bf16[3,4,512,512]{2,3,1,0:T(8,128)(2,1)} %get-tuple-element.38, f32[4,512,3,768]{3,1,2,0:T(8,128)} %get-tuple-element.30, ...), kind=kOutput, calls=%fused_computation.18 | convolution fusion | flops 4912052224 | bytes 55855104 | tf_op jit(solution)/shard_map/hrsj,hej->hrse/dot_general | solution.py:25
  420.9 11.3 %fusion.35 = bf16[4,512,768]{2,1,0:T(8,128)(2,1)} fusion(f32[4,512,768]{2,1,0:T(8,128)S(1)} %fusion.110, bf16[3,4,512,768]{3,2,0,1:T(8,128)(2,1)} %get-tuple-element.40, bf16[3,768,768,1]{2,1,0,3:T(8,128)(2,1)S(1)} %bitcast.284), kind=kOutput, calls=%fused_computation.52 | convolution fusion | flops 7250903040 | bytes 22413312 | tf_op jit(solution)/shard_map/hrse,hde->rsd/dot_general | solution.py:25
  432.5 4.2 fusion.78
  438.7 12.5 %bitcast_convert_fusion.1 = bf16[3,768,512]{2,1,0:T(8,128)(2,1)} fusion(bf16[3,4,512,768]{3,2,0,1:T(8,128)(2,1)} %get-tuple-element.22, bf16[3,4,512,512]{2,3,1,0:T(8,128)(2,1)} %get-tuple-element.38), kind=kOutput, calls=%fused_computation.82 | convolution fusion | flops 4833017856 | bytes 18087936 | tf_op jit(solution)/shard_map/hrse,hrsj->hej/dot_general | solution.py:25
  451.2 3.3 copy.133
  454.5 2.9 convolution_convert_fusion.2
  457.6 6.5 convolution_convert_fusion.1
  464.2 7.3 fusion.105
  476.4 2.7 fusion.71
  480.0 12.5 %bitcast_convert_fusion = bf16[3,768,768]{1,2,0:T(8,128)(2,1)S(1)} fusion(bf16[3,4,512,768]{3,2,0,1:T(8,128)(2,1)} %get-tuple-element.40, bf16[4,512,768]{2,1,0:T(8,128)(2,1)} %all-gather.11.cloned.1.call-done, f32[768]{0:T(1024)S(1)} %copy-done.16, f32[4,512]{1,0:T(4,128)S(1)} %copy-done.32, f32[4,512]{1,0:T(4,128)S(1)} %copy-done.18), kind=kOutput, calls=%fused_computation.46 | convolution fusion | flops 7257391104 | bytes 16141312 | tf_op jit(solution)/shard_map/rsd,hrse->hde/dot_general | solution.py:25
  494.7 14.8 %reduce-scatter.10.cloned.1.call-done = bf16[4,1,24,192]{3,2,0,1:T(8,128)(2,1)} async-done(((bf16[32,1,24,192]{3,2,0,1:T(8,128)(2,1)}), bf16[4,1,24,192]{3,2,0,1:T(8,128)(2,1)}) %reduce-scatter.10.cloned.1.call-update) | async-done | bytes 36880 | tf_op jit(solution)/shard_map/reduce_scatter | solution.py:44
  509.4 3.5 all-to-all-start.5
  513.0 7.6 add_bitcast_fusion.1
  520.6 44.0 %reduce-scatter.14.cloned.1.call-done = bf16[4,3,24,512]{3,2,1,0:T(8,128)(2,1)} async-done(((bf16[32,3,24,512]{3,2,1,0:T(8,128)(2,1)}), bf16[4,3,24,512]{3,2,1,0:T(8,128)(2,1)}) %reduce-scatter.14.cloned.1.call-update) | async-done | bytes 294928 | tf_op jit(solution)/shard_map/reduce_scatter | solution.py:44
  564.6 3.7 all-to-all-start.7
  569.1 96.6 %reduce-scatter.16.cloned.1.call-done = bf16[24,768]{1,0:T(8,128)(2,1)} async-done(((bf16[768,768]{1,0:T(8,128)(2,1)}), bf16[24,768]{1,0:T(8,128)(2,1)}) %reduce-scatter.16.cloned.1.call-update) | async-done | bytes 36880 | tf_op jit(solution)/shard_map/reduce_scatter | solution.py:138
  668.0 110.2 %reduce-scatter.18.cloned.1.call-done = bf16[24,3072]{1,0:T(8,128)(2,1)} async-done(((bf16[768,3072]{1,0:T(8,128)(2,1)}), bf16[24,3072]{1,0:T(8,128)(2,1)}) %reduce-scatter.18.cloned.1.call-update) | async-done | bytes 147472 | tf_op jit(solution)/shard_map/reduce_scatter | solution.py:138
  779.8 109.8 %reduce-scatter.20.cloned.1.call-done = bf16[96,768]{1,0:T(8,128)(2,1)} async-done(((bf16[3072,768]{1,0:T(8,128)(2,1)}), bf16[96,768]{1,0:T(8,128)(2,1)}) %reduce-scatter.20.cloned.1.call-update) | async-done | bytes 147472 | tf_op jit(solution)/shard_map/reduce_scatter | solution.py:138
  893.7 120.1 %all-reduce.5.cloned.1.call-done = f32[16896]{0:T(1024)} async-done(((f32[16896]{0:T(1024)}), f32[16896]{0:T(1024)}) %all-reduce.5.cloned.1.call-update) | async-done | bytes 67600 | tf_op jit(solution)/shard_map/psum | solution.py:143
  1014.6 79.6 %reduce-scatter.12.cloned.1.call-done = bf16[4,3,24,768]{3,2,1,0:T(8,128)(2,1)} async-done(((bf16[32,3,24,768]{3,2,1,0:T(8,128)(2,1)}), bf16[4,3,24,768]{3,2,1,0:T(8,128)(2,1)}) %reduce-scatter.12.cloned.1.call-update) | async-done | bytes 442384 | tf_op jit(solution)/shard_map/reduce_scatter | solution.py:44
  1094.2 3.7 all-to-all-start.6
  1101.1 4.3 all-to-all-done.6
  (194 shorter events, 50.1 us)
Async XLA Ops:
  7.2 116.2 %all-gather.21.cloned.1.call-start = ((), (), s32[]{:S(2)}) async-start(), calls=%async_computation.27 | async-start | bytes 2654208 | tf_op jit(solution)/shard_map/all_gather | solution.py:35
  19.3 107.6 %all-gather.11.cloned.1.call-start = ((), (), s32[]{:S(2)}) async-start(), calls=%async_computation.15 | async-start | bytes 3932160 | tf_op jit(solution)/shard_map/all_gather | solution.py:71
  20.1 123.4 %all-gather.19.cloned.1.call-start = ((), (), s32[]{:S(2)}) async-start(), calls=%async_computation.26 | async-start | bytes 3981312 | tf_op jit(solution)/shard_map/all_gather | solution.py:35
  31.4 197.8 %all-gather.13.cloned.1.call-start = ((), (), s32[]{:S(2)}) async-start(), calls=%async_computation.16 | async-start | bytes 1216512 | tf_op jit(solution)/shard_map/all_gather | solution.py:90
  32.0 232.9 %all-gather.15.cloned.1.call-start = ((), (), s32[]{:S(2)}) async-start(), calls=%async_computation.17 | async-start | bytes 4866048 | tf_op jit(solution)/shard_map/all_gather | solution.py:91
  34.1 61.6 %all-to-all-start = ((bf16[4,1,24,192]{3,2,1,0:T(8,128)(2,1)}), bf16[4,1,24,192]{3,2,1,0:T(8,128)(2,1)S(1)}, u32[]{:S(2)}, u32[]{:S(2)}) async-start(bf16[4,1,24,192]{3,2,1,0:T(8,128)(2,1)} %copy.101), calls=%async_computation | async-start | bytes 98304 | tf_op jit(solution)/shard_map/all_to_all | solution.py:34
  37.4 292.5 %all-gather.17.cloned.1.call-start = ((), (), s32[]{:S(2)}) async-start(), calls=%async_computation.18 | async-start | bytes 4866048 | tf_op jit(solution)/shard_map/all_gather | solution.py:92
  95.7 50.1 %copy-start.15 = (f32[768]{0:T(1024)}, f32[768]{0:T(1024)S(1)}, u32[]{:S(2)}) copy-start(f32[768]{0:T(1024)S(1)} %reshape.286) | copy-start | bytes 9220
  123.4 12.5 %copy-start.9 = (bf16[1,4,8,24,192]{4,3,2,1,0:T(8,128)(2,1)}, bf16[1,4,8,24,192]{4,3,2,1,0:T(8,128)(2,1)S(1)}, u32[]{:S(2)}) copy-start(bf16[1,4,8,24,192]{4,3,2,1,0:T(8,128)(2,1)S(1)} %copy.102) | copy-start | bytes 884740
  129.4 16.4 %copy-start.17 = (f32[4,512]{1,0:T(4,128)}, f32[4,512]{1,0:T(4,128)S(1)}, u32[]{:S(2)}) copy-start(f32[4,512]{1,0:T(4,128)S(1)} %broadcast_multiply_fusion) | copy-start | bytes 24580
  145.8 50.3 %copy-start.5 = (bf16[3,4,8,24,768]{4,3,2,1,0:T(8,128)(2,1)}, bf16[3,4,8,24,768]{4,3,2,1,0:T(8,128)(2,1)S(1)}, u32[]{:S(2)}) copy-start(bf16[3,4,8,24,768]{4,3,2,1,0:T(8,128)(2,1)S(1)} %copy.105) | copy-start | bytes 10616836
  145.8 50.2 %copy-start.8 = (bf16[3,4,8,24,512]{4,3,2,1,0:T(8,128)(2,1)S(1)}, bf16[3,4,8,24,512]{4,3,2,1,0:T(8,128)(2,1)}, u32[]{:S(2)}) copy-start(bf16[3,4,8,24,512]{4,3,2,1,0:T(8,128)(2,1)} %copy.108) | copy-start | bytes 7077892
  196.1 8.0 copy-start.34
  196.1 8.0 copy-start.36
  211.3 9.1 copy-start.12
  220.5 8.6 copy-start.14
  220.5 20.3 %copy-start = (bf16[1,512,768]{2,1,0:T(8,128)(2,1)S(1)}, bf16[1,512,768]{2,1,0:T(8,128)(2,1)}, u32[]{:S(2)}) copy-start(bf16[1,512,768]{2,1,0:T(8,128)(2,1)} %param.13) | copy-start | bytes 2359300
  225.3 15.4 %all-to-all-start.3 = ((bf16[4,1,512,192]{2,3,1,0:T(8,128)(2,1)}), bf16[4,1,512,192]{2,3,1,0:T(8,128)(2,1)S(1)}, u32[]{:S(2)}, u32[]{:S(2)}) async-start(bf16[4,1,512,192]{2,3,1,0:T(8,128)(2,1)} %bitcast.29), calls=%async_computation.3 | async-start | bytes 1572864 | tf_op jit(solution)/shard_map/all_to_all | solution.py:88
  228.8 245.8 %reduce-scatter.22.cloned.1.call-start = ((), (), s32[]{:S(2)}) async-start(), calls=%async_computation.28 | async-start | bytes 3932160
  229.2 114.8 %copy-start.23 = (f32[768]{0:T(1024)}, f32[768]{0:T(1024)S(1)}, u32[]{:S(2)}) copy-start(f32[768]{0:T(1024)S(1)} %reshape.289) | copy-start | bytes 9220
  240.7 43.6 %copy-start.7 = (bf16[4,1,512,192]{2,3,1,0:T(8,128)(2,1)}, bf16[4,1,512,192]{2,3,1,0:T(8,128)(2,1)S(1)}, u32[]{:S(2)}) copy-start(bf16[4,1,512,192]{2,3,1,0:T(8,128)(2,1)S(1)} %all-to-all-done.3) | copy-start | bytes 2359300
  243.2 214.4 %copy-start.4 = (f32[512,768]{1,0:T(8,128)}, f32[512,768]{1,0:T(8,128)S(1)}, u32[]{:S(2)}) copy-start(f32[512,768]{1,0:T(8,128)S(1)} %get-tuple-element.34) | copy-start | bytes 4718596
  243.5 100.5 %copy-start.27 = (f32[512]{0:T(512)}, f32[512]{0:T(512)S(1)}, u32[]{:S(2)}) copy-start(f32[512]{0:T(512)S(1)} %fusion.88) | copy-start | bytes 6148
  329.9 10.6 copy-start.37
  365.2 30.3 %slice-start = ((s8[6291456]{0:T(1024)(128)(4,1)}), s8[4194304]{0:T(1024)(128)(4,1)S(1)}, s32[]{:S(2)}) async-start(s8[6291456]{0:T(1024)(128)(4,1)} %bitcast.280), calls=%async_computation.29 | async-start | bytes 8388608
  372.8 22.7 %slice-start.1 = ((s8[6291456]{0:T(1024)(128)(4,1)}), s8[2097152]{0:T(1024)(128)(4,1)S(1)}, s32[]{:S(2)}) async-start(s8[6291456]{0:T(1024)(128)(4,1)} %bitcast.280), calls=%async_computation.30 | async-start | bytes 4194304
  398.5 22.4 %copy-start.6 = (bf16[3,4,8,24,768]{4,3,2,1,0:T(8,128)(2,1)S(1)}, bf16[3,4,8,24,768]{4,3,2,1,0:T(8,128)(2,1)}, u32[]{:S(2)}) copy-start(bf16[3,4,8,24,768]{4,3,2,1,0:T(8,128)(2,1)} %copy-done.5) | copy-start | bytes 10616836
  420.9 11.5 %copy-start.16 = (f32[768]{0:T(1024)S(1)}, f32[768]{0:T(1024)}, u32[]{:S(2)}) copy-start(f32[768]{0:T(1024)} %copy-done.15) | copy-start | bytes 9220
  420.9 11.6 %copy-start.18 = (f32[4,512]{1,0:T(4,128)S(1)}, f32[4,512]{1,0:T(4,128)}, u32[]{:S(2)}) copy-start(f32[4,512]{1,0:T(4,128)} %copy-done.17) | copy-start | bytes 24580
  420.9 11.6 %copy-start.31 = (f32[4,512]{1,0:T(4,128)S(1)}, f32[4,512]{1,0:T(4,128)}, u32[]{:S(2)}) copy-start(f32[4,512]{1,0:T(4,128)} %copy-done.29) | copy-start | bytes 24580
  432.2 77.2 %reduce-scatter.10.cloned.1.call-start = ((), (), s32[]{:S(2)}) async-start(), calls=%async_computation.20 | async-start | bytes 442368 | tf_op jit(solution)/shard_map/reduce_scatter | solution.py:44
  438.7 125.9 %reduce-scatter.14.cloned.1.call-start = ((), (), s32[]{:S(2)}) async-start(), calls=%async_computation.22 | async-start | bytes 2654208 | tf_op jit(solution)/shard_map/reduce_scatter | solution.py:44
  454.5 211.2 %reduce-scatter.16.cloned.1.call-start = ((), (), s32[]{:S(2)}) async-start(), calls=%async_computation.23 | async-start | bytes 1216512 | tf_op jit(solution)/shard_map/reduce_scatter | solution.py:138
  457.5 320.7 %reduce-scatter.18.cloned.1.call-start = ((), (), s32[]{:S(2)}) async-start(), calls=%async_computation.24 | async-start | bytes 4866048 | tf_op jit(solution)/shard_map/reduce_scatter | solution.py:138
  464.1 425.5 %reduce-scatter.20.cloned.1.call-start = ((), (), s32[]{:S(2)}) async-start(), calls=%async_computation.25 | async-start | bytes 4866048 | tf_op jit(solution)/shard_map/reduce_scatter | solution.py:138
  464.2 7.6 copy-start.33
  471.5 7.6 copy-start.35
  471.5 8.5 copy-start.32
  471.5 542.2 %all-reduce.5.cloned.1.call-start = ((), (), s32[]{:S(2)}) async-start(), calls=%async_computation.19 | async-start | bytes 139264 | tf_op jit(solution)/shard_map/psum | solution.py:143
  476.4 16.1 %copy-start.19 = (f32[512]{0:T(512)}, f32[512]{0:T(512)S(1)}, u32[]{:S(2)}) copy-start(f32[512]{0:T(512)S(1)} %get-tuple-element.28) | copy-start | bytes 6148
  476.4 16.1 %copy-start.21 = (f32[512]{0:T(512)}, f32[512]{0:T(512)S(1)}, u32[]{:S(2)}) copy-start(f32[512]{0:T(512)S(1)} %get-tuple-element.29) | copy-start | bytes 6148
  479.7 614.5 %reduce-scatter.12.cloned.1.call-start = ((), (), s32[]{:S(2)}) async-start(), calls=%async_computation.21 | async-start | bytes 3981312 | tf_op jit(solution)/shard_map/reduce_scatter | solution.py:44
  509.4 11.2 %all-to-all-start.5 = ((bf16[4,1,24,192]{3,2,1,0:T(8,128)(2,1)}), bf16[4,1,24,192]{3,2,1,0:T(8,128)(2,1)S(1)}, u32[]{:S(2)}, u32[]{:S(2)}) async-start(bf16[4,1,24,192]{3,2,1,0:T(8,128)(2,1)} %bitcast.308), calls=%async_computation.6 | async-start | bytes 98304 | tf_op jit(solution)/shard_map/all_to_all | solution.py:45
  513.0 379.0 %copy-start.3 = (bf16[1,512,768]{2,1,0:T(8,128)(2,1)S(1)}, bf16[1,512,768]{2,1,0:T(8,128)(2,1)}, u32[]{:S(2)}) copy-start(bf16[1,512,768]{2,1,0:T(8,128)(2,1)} %reduce-scatter.22.cloned.1.call-done) | copy-start | bytes 2359300
  513.0 379.0 %copy-start.20 = (f32[512]{0:T(512)S(1)}, f32[512]{0:T(512)}, u32[]{:S(2)}) copy-start(f32[512]{0:T(512)} %copy-done.19) | copy-start | bytes 6148
  513.0 379.0 %copy-start.22 = (f32[512]{0:T(512)S(1)}, f32[512]{0:T(512)}, u32[]{:S(2)}) copy-start(f32[512]{0:T(512)} %copy-done.21) | copy-start | bytes 6148
  564.6 102.5 %all-to-all-start.7 = ((bf16[4,3,24,512]{3,2,1,0:T(8,128)(2,1)}), bf16[4,3,24,512]{3,2,1,0:T(8,128)(2,1)S(1)}, u32[]{:S(2)}, u32[]{:S(2)}) async-start(bf16[4,3,24,512]{3,2,1,0:T(8,128)(2,1)} %reduce-scatter.14.cloned.1.call-done), calls=%async_computation.10 | async-start | bytes 589824 | tf_op jit(solution)/shard_map/all_to_all | solution.py:45
  1094.2 11.2 %all-to-all-start.6 = ((bf16[4,3,24,768]{3,2,1,0:T(8,128)(2,1)}), bf16[4,3,24,768]{3,2,1,0:T(8,128)(2,1)S(1)}, u32[]{:S(2)}, u32[]{:S(2)}) async-start(bf16[4,3,24,768]{3,2,1,0:T(8,128)(2,1)} %reduce-scatter.12.cloned.1.call-done), calls=%async_computation.8 | async-start | bytes 884736 | tf_op jit(solution)/shard_map/all_to_all | solution.py:45
  (13 other events, 51.2 us)
Sparse Core Ops, SparseCore 0:
  19.4 31.2 all-gather.20
  52.5 43.6 all-gather.10
  97.8 45.5 all-gather.18
  146.1 52.8 all-gather.12
  201.6 63.1 all-gather.14
  267.5 62.3 all-gather.16
  432.3 42.2 reduce-scatter.21
  477.4 31.9 reduce-scatter.9
  511.9 52.6 reduce-scatter.13
  570.3 95.2 reduce-scatter.15
  672.1 106.0 reduce-scatter.17
  783.5 106.0 reduce-scatter.19
  896.7 116.9 all-reduce.4
  1016.0 78.1 reduce-scatter.11

commit v2 on v1

--- a/solution.py
+++ b/solution.py
@@ -1,6 +1,8 @@
 import jax
 import jax.numpy as jnp
 from jax import lax
+from jax.experimental import pallas as pl
+from jax.experimental.pallas import tpu as pltpu
 from jax.sharding import Mesh
 from jax.sharding import PartitionSpec as P
 
@@ -167,6 +169,759 @@
     )
 
 
+MESH = pl.DeviceIdType.MESH
+VMEM_LIMIT = 60 * 2**20
+ANY = pl.BlockSpec(memory_space=pl.ANY)
+FULL = pl.BlockSpec(memory_space=pltpu.VMEM)
+DMA = pltpu.SemaphoreType.DMA
+
+
+def shape_of(dims, kind):
+    return jax.ShapeDtypeStruct(dims, kind)
+
+
+def dot_nt(a, b):
+    return lax.dot_general(a, b, (((1,), (1,)), ((), ())), preferred_element_type=f32)
+
+
+def dot_tn(a, b):
+    return lax.dot_general(a, b, (((0,), (0,)), ((), ())), preferred_element_type=f32)
+
+
+def dot_nn(a, b):
+    return lax.dot_general(a, b, (((1,), (0,)), ((), ())), preferred_element_type=f32)
+
+
+def place():
+    return lax.axis_index("tp"), lax.axis_index("rep"), lax.axis_index("narrow")
+
+
+def group_peers():
+    t, c, z = place()
+    along_x = t + 1 - 2 * (t % 2)
+    along_y = (t + 2) % GROUP
+    return [along_x, along_y, GROUP - 1 - t]
+
+
+def line_peers():
+    z = lax.axis_index("narrow")
+    return [(z + k) % 4 for k in (1, 2, 3)]
+
+
+def greet(devices):
+    barrier = pltpu.get_barrier_semaphore()
+    for device in devices:
+        pl.semaphore_signal(barrier, inc=1, device_id=device, device_id_type=MESH)
+    pl.semaphore_wait(barrier, len(devices))
+
+
+def remote(src, dst, send, recv, device):
+    copy = pltpu.make_async_remote_copy(
+        src_ref=src, dst_ref=dst, send_sem=send, recv_sem=recv, device_id=device, device_id_type=MESH
+    )
+    copy.start()
+    return copy
+
+
+def local(src, dst, sem):
+    copy = pltpu.make_async_copy(src, dst, sem)
+    copy.start()
+    return copy
+
+
+def gather_kernel(pa, pt, pf, la, lt, lf, own, s1, r1, s2, r2, s3, r3, st, rt, sf, rf):
+    t, c, z = place()
+    sibling = (t, 1 - c, z)
+    tps, zs = group_peers(), line_peers()
+    greet([(p, c, z) for p in tps] + [(t, c, p) for p in zs] + [sibling])
+    y, x = t // 2, t % 2
+    slow, fast = (1 - c) * y + c * x, (1 - c) * x + c * y
+    fast_peer = (1 - c) * tps[0] + c * tps[1]
+    slow_peer = (1 - c) * tps[1] + c * tps[0]
+    heads = la.shape[0]
+    mine = [local(pa.at[t, h], la.at[h, c, z, t], own.at[h]) for h in range(heads)]
+    mine_f = local(pf, lf.at[c, slow, fast, z], own.at[heads])
+    mine_t = local(pt, lt.at[t], own.at[heads + 1])
+    one, two, three = [], [], []
+    for h in range(heads):
+        one.append(
+            [remote(pa.at[p, h], la.at[h, c, z, t], s1.at[h, k], r1.at[h, k], (p, c, z)) for k, p in enumerate(tps)]
+        )
+    f1 = [remote(pf, lf.at[c, slow, fast, z], sf.at[k], rf.at[k], (t, c, p)) for k, p in enumerate(zs)]
+    toks = [remote(pt, lt.at[t], st.at[k], rt.at[k], (p, c, z)) for k, p in enumerate(tps)]
+    for h in range(heads):
+        mine[h].wait()
+        for copy in one[h]:
+            copy.wait()
+        two.append(
+            [remote(la.at[h, c, z], la.at[h, c, z], s2.at[h, k], r2.at[h, k], (t, c, p)) for k, p in enumerate(zs)]
+        )
+    mine_f.wait()
+    for copy in f1:
+        copy.wait()
+    f2 = remote(lf.at[c, slow, fast], lf.at[c, slow, fast], sf.at[3], rf.at[3], (fast_peer, c, z))
+    for h in range(heads):
+        if h == 1:
+            f2.wait()
+            f3 = remote(lf.at[c, slow], lf.at[c, slow], sf.at[4], rf.at[4], (slow_peer, c, z))
+        for copy in two[h]:
+            copy.wait()
+        three.append(remote(la.at[h, c], la.at[h, c], s3.at[h], r3.at[h], sibling))
+    f3.wait()
+    f4 = remote(lf.at[c], lf.at[c], sf.at[5], rf.at[5], sibling)
+    mine_t.wait()
+    for copy in toks + three + [f4]:
+        copy.wait()
+
+
+def gather_call(pa, pt, pf):
+    heads = pa.shape[1]
+    return pl.pallas_call(
+        gather_kernel,
+        out_shape=(
+            shape_of((heads, 2, 4, GROUP) + pa.shape[2:], bf16),
+            shape_of((GROUP,) + pt.shape, bf16),
+            shape_of((2, 2, 2, 4) + pf.shape, bf16),
+        ),
+        in_specs=[ANY] * 3,
+        out_specs=(ANY,) * 3,
+        scratch_shapes=[
+            DMA((heads + 2,)),
+            DMA((heads, 3)),
+            DMA((heads, 3)),
+            DMA((heads, 3)),
+            DMA((heads, 3)),
+            DMA((heads,)),
+            DMA((heads,)),
+            DMA((3,)),
+            DMA((3,)),
+            DMA((6,)),
+            DMA((6,)),
+        ],
+        compiler_params=pltpu.CompilerParams(collective_id=1, has_side_effects=True),
+    )(pa, pt, pf)
+
+
+def trade_kernel(src, dst, own, send, recv):
+    t, c, z = place()
+    tps = group_peers()
+    greet([(p, c, z) for p in tps])
+    mine = local(src.at[t], dst.at[t], own)
+    copies = [remote(src.at[p], dst.at[t], send.at[k], recv.at[k], (p, c, z)) for k, p in enumerate(tps)]
+    mine.wait()
+    for copy in copies:
+        copy.wait()
+
+
+def trade_call(pieces, collective_id):
+    return pl.pallas_call(
+        lambda *refs: trade_kernel(*refs),
+        out_shape=shape_of(pieces.shape, pieces.dtype),
+        in_specs=[ANY],
+        out_specs=ANY,
+        scratch_shapes=[DMA, DMA((3,)), DMA((3,))],
+        compiler_params=pltpu.CompilerParams(collective_id=collective_id, has_side_effects=True),
+    )(pieces)
+
+
+def gelu_pair(v):
+    cdf = 0.5 * (1.0 + lax.erf(v * 0.7071067811865476))
+    return v * cdf, cdf + v * (jnp.exp(-0.5 * v * v) * 0.3989422804014327)
+
+
+def centre_rows(v):
+    shifted = v - jnp.mean(v, axis=-1, keepdims=True)
+    scale = lax.rsqrt(jnp.mean(shifted * shifted, axis=-1, keepdims=True) + epsilon)
+    return shifted * scale, scale
+
+
+def attend_kernel(la, lt, b2, wf, ws, wv, small, normed, values, hid, slope, prob, join, nrm, val, cols):
+    h, r = pl.program_id(0), pl.program_id(1)
+    width = wf.shape[-1]
+
+    @pl.when(r == 0)
+    def _():
+        def unpack(t, carry):
+            for c in range(2):
+                for z in range(0, 4, 2):
+                    tops, lows = [], []
+                    for k in range(2):
+                        tops.append(la[0, c, z + k, t, 0:32, :].astype(f32)[0:24])
+                        lows.append(la[0, c, z + k, t, 16:48, :].astype(f32)[8:32])
+                    top, low = jnp.concatenate(tops, 0), jnp.concatenate(lows, 0)
+                    at = pl.ds(pl.multiple_of((t * 8 + c * 4 + z) * 24, 48), 48)
+                    wf[0, at, :] = top.astype(bf16)
+                    ws[0, at, :] = low[:, :512].astype(bf16)
+
+                    @pl.when(h == 0)
+                    def _():
+                        last = low[:, 640:768]
+                        cols[at, :] = last
+                        lane = lax.broadcasted_iota(jnp.int32, last.shape, 1)
+                        wv[at, 0:128] = low[:, 512:640].astype(bf16)
+                        wv[at, 128:256] = jnp.where(lane < 64, last, 0.0).astype(bf16)
+
+            return carry
+
+        lax.fori_loop(0, GROUP, unpack, 0)
+
+        @pl.when(h == 0)
+        def _():
+            small[...] = cols[...].T[64:72]
+
+    @pl.when(h == 0)
+    def _():
+        unit, _ = centre_rows(lt[0, 0:512, :].astype(f32))
+        out = (unit * small[3:4]).astype(bf16)
+        nrm[r] = out
+        normed[0] = out
+        v = dot_nn(out, wv[...]).astype(bf16)
+        val[r] = v
+        values[0] = v
+
+    mask = lt[0, 512:528, 0:512].astype(f32)[0:1]
+    row = lax.broadcasted_iota(jnp.int32, (8, width), 0)
+    b1 = jnp.sum(jnp.where(row == h, small[...], 0.0), axis=0, keepdims=True)
+    row = lax.broadcasted_iota(jnp.int32, b2.shape, 0)
+    shift = jnp.sum(jnp.where(row == h, b2[...], 0.0), axis=0, keepdims=True) + mask
+    tile = pl.ds(pl.multiple_of((h // 2) * 128, 128), 128)
+    step = 256
+    for m in range(0, 512, step):
+        at = slice(m, m + step)
+        before = dot_nn(nrm[r, at, :], wf[0]) + b1
+        out, grad = gelu_pair(before)
+        hidden = out.astype(bf16)
+        hid[0, 0, at, :] = hidden
+        slope[0, 0, at, :] = grad.astype(bf16)
+        logits = dot_nn(hidden, ws[0]) + shift
+        e = jnp.exp(logits - jnp.max(logits, axis=-1, keepdims=True))
+        p = (e / jnp.sum(e, axis=-1, keepdims=True)).astype(bf16)
+        prob[0, 0, at, :] = p
+        mix = dot_nn(p, val[r, :, tile])
+        lane = lax.broadcasted_iota(jnp.int32, mix.shape, 1)
+        old = join[r, at, tile].astype(f32)
+        join[r, at, tile] = jnp.where((h == 1) & (lane < 64), old, mix).astype(bf16)
+
+
+def attend_call(la, lt, b2):
+    heads, width = la.shape[0], la.shape[-1]
+    slots = 512
+    by_row = lambda h, r: (jnp.where(h == 0, r, GROUP - 1), 0, 0)
+    by_head = lambda h, r: (h, 0, 0)
+    both = lambda h, r: (h, r, 0, 0)
+    return pl.pallas_call(
+        attend_kernel,
+        grid=(heads, GROUP),
+        out_shape=(
+            shape_of((heads, width, width), bf16),
+            shape_of((heads, width, slots), bf16),
+            shape_of((width, 256), bf16),
+            shape_of((8, width), f32),
+            shape_of((GROUP, slots, width), bf16),
+            shape_of((GROUP, slots, 256), bf16),
+            shape_of((heads, GROUP, slots, width), bf16),
+            shape_of((heads, GROUP, slots, width), bf16),
+            shape_of((heads, GROUP, slots, slots), bf16),
+            shape_of((GROUP, slots, 256), bf16),
+        ),
+        in_specs=[
+            pl.BlockSpec((1,) + la.shape[1:], lambda h, r: (h, 0, 0, 0, 0, 0)),
+            pl.BlockSpec((1,) + lt.shape[1:], lambda h, r: (r, 0, 0)),
+            pl.BlockSpec(b2.shape, lambda h, r: (0, 0)),
+        ],
+        out_specs=(
+            pl.BlockSpec((1, width, width), by_head),
+            pl.BlockSpec((1, width, slots), by_head),
+            pl.BlockSpec((width, 256), lambda h, r: (0, 0)),
+            pl.BlockSpec((8, width), lambda h, r: (0, 0)),
+            pl.BlockSpec((1, slots, width), by_row),
+            pl.BlockSpec((1, slots, 256), by_row),
+            pl.BlockSpec((1, 1, slots, width), both),
+            pl.BlockSpec((1, 1, slots, width), both),
+            pl.BlockSpec((1, 1, slots, slots), both),
+            pl.BlockSpec((GROUP, slots, 256), lambda h, r: (0, 0, 0)),
+        ),
+        scratch_shapes=[
+            pltpu.VMEM((GROUP, slots, width), bf16),
+            pltpu.VMEM((GROUP, slots, 256), bf16),
+            pltpu.VMEM((width, 128), f32),
+        ],
+        compiler_params=pltpu.CompilerParams(vmem_limit_bytes=VMEM_LIMIT),
+    )(la, lt, b2)
+
+
+def slab(t, c, z):
+    y, x = t // 2, t % 2
+    return (0, y, x, z) if c == 0 else (1, x, y, z)
+
+
+def ffn_kernel(lf, joined, tokens, small, gout, result, gmid, gj, gf, gg2, wu, wo, n2, acc, gn2, gwu):
+    width = tokens.shape[-1]
+    wo[...] = jnp.zeros_like(wo)
+    for t in range(GROUP):
+        for c in range(2):
+            for z in range(0, 4, 2):
+                pair = [lf[slab(t, c, z + k)][96:128].astype(f32)[0:24] for k in range(2)]
+                wo[t, (c * 4 + z) * 24 : (c * 4 + z) * 24 + 48, :] = jnp.concatenate(pair, 0).astype(bf16)
+    middle = tokens[...].astype(f32)
+    for t in range(GROUP):
+        middle = middle + dot_nn(joined[t], wo[t])
+    acc[...] = middle
+    g2 = small[4:5]
+    unit, _ = centre_rows(middle)
+    n2[...] = (unit * g2).astype(bf16)
+    gn2[...] = jnp.zeros_like(gn2)
+
+    def block(p, carry):
+        rows = pl.ds(pl.multiple_of(p * 48, 16), 48)
+        for t in range(GROUP):
+            for c in range(2):
+                for z in range(0, 4, 2):
+                    ends = [lf[slab(t, c, z + k) + (rows,)].astype(f32) for k in range(2)]
+                    at = (t * 8 + c * 4 + z) * 24
+                    for k in range(2):
+                        both = jnp.concatenate([e[24 * k : 24 * k + 24] for e in ends], 0)
+                        wu[k, at : at + 48, :] = both.astype(bf16)
+        branch = gout[...].astype(bf16)
+        for k in range(2):
+            wd = jnp.concatenate(
+                [lf[0, p, k, :, 128:224, :].reshape(384, width), lf[1, k, p, :, 128:224, :].reshape(384, width)], 0
+            )
+            up = dot_nn(n2[...], wu[k])
+            act, slope = gelu_pair(up)
+            act = act.astype(bf16)
+            acc[...] += dot_nn(act, wd)
+            gup = (dot_nt(branch, wd) * slope).astype(bf16)
+            gwd = dot_tn(act, branch).astype(bf16)
+            gf[0, p, k, :, 128:224, :] = gwd[:384].reshape(4, 96, width)
+            gf[1, k, p, :, 128:224, :] = gwd[384:].reshape(4, 96, width)
+            gwu[k] = dot_tn(n2[...], gup)
+            gn2[...] += dot_nt(gup, wu[k])
+        for t in range(GROUP):
+            for c in range(2):
+                for z in range(4):
+                    at = (t * 8 + c * 4 + z) * 24
+                    both = jnp.concatenate([gwu[0, at : at + 24, :], gwu[1, at : at + 24, :]], 0)
+                    gf[slab(t, c, z) + (rows,)] = both.astype(bf16)
+        return carry
+
+    lax.fori_loop(0, 2, block, 0)
+    result[...] = acc[...]
+    middle = tokens[...].astype(f32)
+    for t in range(GROUP):
+        middle = middle + dot_nn(joined[t], wo[t])
+    unit, scale = centre_rows(middle)
+    gn = gn2[...]
+    gg2[...] = jnp.sum((gn * unit).reshape(-1, 8, width), axis=0)
+    gu = gn * g2
+    back = scale * (
+        gu - jnp.mean(gu, axis=-1, keepdims=True) - unit * jnp.mean(gu * unit, axis=-1, keepdims=True)
+    )
+    gm = gout[...] + back
+    gmid[...] = gm
+    ga = gm.astype(bf16)
+    for t in range(GROUP):
+        gj[t] = dot_nt(ga, wo[t]).astype(bf16)
+        gwo = dot_tn(joined[t], ga)
+        for c in range(2):
+            for z in range(4):
+                at = (c * 4 + z) * 24
+                padded = jnp.concatenate([gwo[at : at + 24, :], jnp.zeros((8, width), f32)], 0)
+                gf[slab(t, c, z) + (slice(96, 128),)] = padded.astype(bf16)
+
+
+def ffn_call(lf, joined, tokens, small, gout):
+    slots, width = tokens.shape
+    return pl.pallas_call(
+        ffn_kernel,
+        out_shape=(
+            shape_of((slots, width), f32),
+            shape_of((slots, width), f32),
+            shape_of(joined.shape, bf16),
+            shape_of(lf.shape, bf16),
+            shape_of((8, width), f32),
+        ),
+        in_specs=[FULL] * 5,
+        out_specs=(FULL,) * 5,
+        scratch_shapes=[
+            pltpu.VMEM((2, width, width), bf16),
+            pltpu.VMEM((GROUP, 256, width), bf16),
+            pltpu.VMEM((slots, width), bf16),
+            pltpu.VMEM((slots, width), f32),
+            pltpu.VMEM((slots, width), f32),
+            pltpu.VMEM((2, width, width), f32),
+        ],
+        compiler_params=pltpu.CompilerParams(vmem_limit_bytes=VMEM_LIMIT),
+    )(lf, joined, tokens, small, gout)
+
+
+def back_kernel(
+    wf, ws, wv, normed, values, hid, slope, prob, gmix, lt, gg2, ga, gs, gn_out, awf, aws, ab1, ab2, gn, gv, awv, ag1
+):
+    h, r = pl.program_id(0), pl.program_id(1)
+    width = wf.shape[-1]
+
+    @pl.when(r == 0)
+    def _():
+        awf[...] = jnp.zeros_like(awf)
+        aws[...] = jnp.zeros_like(aws)
+        ab1[...] = jnp.zeros_like(ab1)
+        ab2[h] = jnp.zeros(ab2.shape[1:], f32)
+
+    tile = pl.ds(pl.multiple_of((h // 2) * 128, 128), 128)
+    lane = lax.broadcasted_iota(jnp.int32, (512, 128), 1)
+    gm = jnp.where(lane // 64 == h % 2, gmix[0, :, tile].astype(f32), 0.0).astype(bf16)
+    gw = dot_nt(gm, values[0, :, tile])
+    p = prob[0, 0]
+    p32 = p.astype(f32)
+    gl = (p32 * (gw - jnp.sum(p32 * gw, axis=-1, keepdims=True))).astype(bf16)
+    ab2[h] += jnp.sum(gl.astype(f32).reshape(-1, 8, 512), axis=0)
+    gvh = dot_tn(p, gm)
+
+    @pl.when(h != 1)
+    def _():
+        gv[r, :, tile] = gvh
+
+    @pl.when(h == 1)
+    def _():
+        gv[r, :, tile] += gvh
+
+    aws[...] += dot_tn(hid[0, 0], gl)
+    gb = (dot_nt(gl, ws[0]) * slope[0, 0].astype(f32)).astype(bf16)
+    ab1[...] += jnp.sum(gb.astype(f32).reshape(-1, 8, width), axis=0)
+    awf[...] += dot_tn(normed[0], gb)
+    part = dot_nt(gb, wf[0])
+
+    @pl.when(h == 0)
+    def _():
+        gn[r] = part
+
+    @pl.when(h == 1)
+    def _():
+        gn[r] += part
+
+    @pl.when(h == 2)
+    def _():
+        gvb = gv[r].astype(bf16)
+        total = gn[r] + part + dot_nt(gvb, wv[...])
+        gn_out[0] = total.astype(bf16)
+        unit, _ = centre_rows(lt[0, 0:512, :].astype(f32))
+        first = jnp.where(r == 0, 0.0, 1.0)
+        ag1[...] = jnp.where(r == 0, 0.0, ag1[...]) + jnp.sum((total * unit).reshape(-1, 8, width), axis=0)
+        more = dot_tn(normed[0], gvb)
+
+        @pl.when(r == 0)
+        def _():
+            awv[...] = more
+
+        @pl.when(r != 0)
+        def _():
+            awv[...] += more
+
+    @pl.when(r == GROUP - 1)
+    def _():
+        last = h == 2
+        row = lax.broadcasted_iota(jnp.int32, (128, width), 0)
+        stack = jnp.where(row == 64, jnp.sum(ab1[...], axis=0, keepdims=True), 0.0)
+        stack = jnp.where(last & (row == 65), jnp.sum(ag1[...], axis=0, keepdims=True), stack)
+        stack = jnp.where(last & (row == 66), jnp.sum(gg2[...], axis=0, keepdims=True), stack)
+        cols = stack.T
+        lane = lax.broadcasted_iota(jnp.int32, (width, 128), 1)
+
+        @pl.when(jnp.logical_not(last))
+        def _():
+            awv[:, 0:128] = jnp.zeros((width, 128), f32)
+            awv[:, 128:256] = cols
+
+        @pl.when(last)
+        def _():
+            awv[:, 128:256] = jnp.where(lane < 64, awv[:, 128:256], cols)
+
+        def pack(t, carry):
+            for c in range(2):
+                for z in range(4):
+                    at = pl.ds(pl.multiple_of((t * 8 + c * 4 + z) * 24, 8), 24)
+                    low = jnp.concatenate([aws[at, :], awv[at, :]], 1)
+                    ga[0, c, z, t] = jnp.concatenate([awf[at, :], low], 0).astype(bf16)
+            return carry
+
+        lax.fori_loop(0, GROUP, pack, 0)
+
+        @pl.when(last)
+        def _():
+            flat = jnp.concatenate([jnp.sum(ab2[k], axis=0, keepdims=True) for k in range(3)], 1)
+            flat = jnp.broadcast_to(flat, (8, 1536))
+            for c in range(2):
+                for z in range(4):
+                    s = (c * 4 + z) * 192
+                    gs[c, z] = (pltpu.roll(flat, 1536 - s, 1) if s else flat)[:, 0:256]
+
+
+def back_call(wf, ws, wv, normed, values, hid, slope, prob, gmix, lt, gg2):
+    heads, width, slots = ws.shape
+    by_head = lambda h, r: (h, 0, 0)
+    row = lambda h, r: (r, 0, 0)
+    both = lambda h, r: (h, r, 0, 0)
+    return pl.pallas_call(
+        back_kernel,
+        grid=(heads, GROUP),
+        out_shape=(
+            shape_of((heads, 2, 4, GROUP, 48, width), bf16),
+            shape_of((2, 4, 8, 256), f32),
+            shape_of((GROUP, slots, width), bf16),
+        ),
+        in_specs=[
+            pl.BlockSpec((1, width, width), by_head),
+            pl.BlockSpec((1, width, slots), by_head),
+            pl.BlockSpec((width, 256), lambda h, r: (0, 0)),
+            pl.BlockSpec((1, slots, width), row),
+            pl.BlockSpec((1, slots, 256), row),
+            pl.BlockSpec((1, 1, slots, width), both),
+            pl.BlockSpec((1, 1, slots, width), both),
+            pl.BlockSpec((1, 1, slots, slots), both),
+            pl.BlockSpec((1, slots, 256), row),
+            pl.BlockSpec((1,) + lt.shape[1:], lambda h, r: (jnp.where(h == 2, r, 0), 0, 0)),
+            pl.BlockSpec((8, width), lambda h, r: (0, 0)),
+        ],
+        out_specs=(
+            pl.BlockSpec((1, 2, 4, GROUP, 48, width), lambda h, r: (h, 0, 0, 0, 0, 0)),
+            pl.BlockSpec((2, 4, 8, 256), lambda h, r: (0, 0, 0, 0)),
+            pl.BlockSpec((1, slots, width), lambda h, r: (jnp.where(h == 2, r, 0), 0, 0)),
+        ),
+        scratch_shapes=[
+            pltpu.VMEM((width, width), f32),
+            pltpu.VMEM((width, slots), f32),
+            pltpu.VMEM((8, width), f32),
+            pltpu.VMEM((heads, 8, slots), f32),
+            pltpu.VMEM((GROUP, slots, width), f32),
+            pltpu.VMEM((GROUP, slots, 256), f32),
+            pltpu.VMEM((width, 256), f32),
+            pltpu.VMEM((8, width), f32),
+        ],
+        compiler_params=pltpu.CompilerParams(vmem_limit_bytes=VMEM_LIMIT),
+    )(wf, ws, wv, normed, values, hid, slope, prob, gmix, lt, gg2)
+
+
+def add_into(total, more, count):
+    def one(i, carry):
+        total[i] = (total[i].astype(f32) + more[i].astype(f32)).astype(bf16)
+        return carry
+
+    lax.fori_loop(0, count, one, 0)
+
+
+def reduce_kernel(
+    gf, ga, gs, gn, tokens, gmid, small, out_f, out_a, out_s, gtok,
+    fs, fb1, fb2, fb3, fb4, asum, ab1, ab2, ss, sb1, sb2, nb, own, s1, r1, s2, r2, s3, r3, sn, rn, sf, rf, sv, rv,
+):
+    t, c, z = place()
+    sibling = (t, 1 - c, z)
+    tps, zs = group_peers(), line_peers()
+    greet([(p, c, z) for p in tps] + [(t, c, p) for p in zs] + [sibling])
+    y, x = t // 2, t % 2
+    slow, fast = (1 - c) * y + c * x, (1 - c) * x + c * y
+    fast_peer = (1 - c) * tps[0] + c * tps[1]
+    slow_peer = (1 - c) * tps[1] + c * tps[0]
+    heads = ga.shape[0]
+    one = [remote(ga.at[h, 1 - c], ab1.at[h], s1.at[h], r1.at[h], sibling) for h in range(heads)]
+    v1 = remote(gs.at[1 - c], sb1, sv.at[0], rv.at[0], sibling)
+    f1 = remote(gf.at[1 - c], fb1, sf.at[0], rf.at[0], sibling)
+    mine = [local(ga.at[h, c], asum.at[h], own.at[h]) for h in range(heads)]
+    mine_s = local(gs.at[c], ss, own.at[heads])
+    mine_f = local(gf.at[c], fs, own.at[heads + 1])
+    mine_n = local(gn.at[t], nb.at[3], own.at[heads + 2])
+    parts = [remote(gn.at[p], nb.at[k], sn.at[k], rn.at[k], (p, c, z)) for k, p in enumerate(tps)]
+    two = []
+    for h in range(heads):
+        mine[h].wait()
+        one[h].wait()
+
+        def line(i, carry):
+            add_into(asum.at[h, i], ab1.at[h, i], GROUP)
+            return carry
+
+        lax.fori_loop(0, 4, line, 0)
+        two.append(
+            [remote(asum.at[h, p], ab2.at[h, k], s2.at[h, k], r2.at[h, k], (t, c, p)) for k, p in enumerate(zs)]
+        )
+        if h == 0:
+            mine_s.wait()
+            v1.wait()
+            ss[...] += sb1[...]
+            v2 = [remote(ss.at[p], sb2.at[k], sv.at[1 + k], rv.at[1 + k], (t, c, p)) for k, p in enumerate(zs)]
+    mine_f.wait()
+    f1.wait()
+
+    for which in (1 - slow, slow):
+        for j in range(2):
+            add_into(fs.at[which, j], fb1.at[which, j], 4)
+        if which is not slow:
+            f2 = remote(fs.at[1 - slow], fb2, sf.at[1], rf.at[1], (slow_peer, c, z))
+    mine_n.wait()
+    for copy in parts:
+        copy.wait()
+
+    def ln_back(i, carry):
+        at = pl.ds(pl.multiple_of(i * 128, 128), 128)
+        g = nb[0, at, :].astype(f32) + nb[1, at, :].astype(f32) + nb[2, at, :].astype(f32) + nb[3, at, :].astype(f32)
+        unit, scale = centre_rows(tokens[at, :].astype(f32))
+        gu = g * small[3:4]
+        back = scale * (
+            gu - jnp.mean(gu, axis=-1, keepdims=True) - unit * jnp.mean(gu * unit, axis=-1, keepdims=True)
+        )
+        gtok[at, :] = gmid[at, :] + back
+        return carry
+
+    lax.fori_loop(0, 4, ln_back, 0)
+    f2.wait()
+    for which in (1 - fast, fast):
+        add_into(fs.at[slow, which], fb2.at[which], 4)
+        if which is not fast:
+            f3 = remote(fs.at[slow, 1 - fast], fb3, sf.at[2], rf.at[2], (fast_peer, c, z))
+    f3.wait()
+    add_into(fs.at[slow, fast], fb3, 4)
+    f4 = [
+        remote(fs.at[slow, fast, p], fb4.at[k], sf.at[3 + k], rf.at[3 + k], (t, c, p)) for k, p in enumerate(zs)
+    ]
+    three, mine_a = [], []
+    for h in range(heads):
+        for copy in two[h]:
+            copy.wait()
+
+        def fold(i, carry):
+            total = asum[h, z, i].astype(f32)
+            for k in range(3):
+                total = total + ab2[h, k, i].astype(f32)
+            asum[h, z, i] = total.astype(bf16)
+            return carry
+
+        lax.fori_loop(0, GROUP, fold, 0)
+        mine_a.append(local(asum.at[h, z, t], out_a.at[h, t], own.at[h]))
+        three.append(
+            [remote(asum.at[h, z, p], out_a.at[h, t], s3.at[h, k], r3.at[h, k], (p, c, z)) for k, p in enumerate(tps)]
+        )
+    for copy in v2:
+        copy.wait()
+    out_s[...] = ss[z] + sb2[0] + sb2[1] + sb2[2]
+    for copy in f4:
+        copy.wait()
+    total = fs[slow, fast, z].astype(f32)
+    for k in range(3):
+        total = total + fb4[k].astype(f32)
+    out_f[...] = total
+    for copy in mine_a:
+        copy.wait()
+    for copies in three:
+        for copy in copies:
+            copy.wait()
+
+
+def reduce_call(gf, ga, gs, gn, tokens, gmid, small):
+    heads, width = ga.shape[0], ga.shape[-1]
+    rows = gf.shape[-2]
+    return pl.pallas_call(
+        reduce_kernel,
+        out_shape=(
+            shape_of((rows, width), f32),
+            shape_of((heads, GROUP, 48, width), bf16),
+            shape_of((8, 256), f32),
+            shape_of(tokens.shape, f32),
+        ),
+        in_specs=[ANY] * 4 + [FULL] * 3,
+        out_specs=(FULL, ANY, FULL, FULL),
+        scratch_shapes=[
+            pltpu.VMEM((2, 2, 4, rows, width), bf16),
+            pltpu.VMEM((2, 2, 4, rows, width), bf16),
+            pltpu.VMEM((2, 4, rows, width), bf16),
+            pltpu.VMEM((4, rows, width), bf16),
+            pltpu.VMEM((3, rows, width), bf16),
+            pltpu.VMEM((heads, 4, GROUP, 48, width), bf16),
+            pltpu.VMEM((heads, 4, GROUP, 48, width), bf16),
+            pltpu.VMEM((heads, 3, GROUP, 48, width), bf16),
+            pltpu.VMEM((4, 8, 256), f32),
+            pltpu.VMEM((4, 8, 256), f32),
+            pltpu.VMEM((3, 8, 256), f32),
+            pltpu.VMEM((4,) + tokens.shape, bf16),
+            DMA((heads + 3,)),
+            DMA((heads,)),
+            DMA((heads,)),
+            DMA((heads, 3)),
+            DMA((heads, 3)),
+            DMA((heads, 3)),
+            DMA((heads, 3)),
+            DMA((3,)),
+            DMA((3,)),
+            DMA((6,)),
+            DMA((6,)),
+            DMA((4,)),
+            DMA((4,)),
+        ],
+        compiler_params=pltpu.CompilerParams(collective_id=4, has_side_effects=True, vmem_limit_bytes=VMEM_LIMIT),
+    )(gf, ga, gs, gn, tokens, gmid, small)
+
+
+def pack_inputs(tokens, lengths, gain_one, w_value, w_first, b_first, w_second, b_second, w_out, gain_two, w_up, w_down):
+    _, slots, width = tokens.shape
+    heads_all, depth, _ = w_first.shape
+    heads = heads_all // GROUP
+    split = lambda v: v.reshape((GROUP, heads) + v.shape[1:])
+    cols = jnp.concatenate(
+        [
+            b_first.reshape(GROUP, heads, depth).transpose(0, 2, 1),
+            jnp.broadcast_to(jnp.stack([gain_one, gain_two], 1), (GROUP, depth, 2)),
+            jnp.zeros((GROUP, depth, 59), bf16),
+        ],
+        2,
+    )
+    head_zero = jnp.concatenate([w_value.reshape(depth, GROUP, -1).transpose(1, 0, 2), cols], 2)
+    head_one = jnp.broadcast_to(jnp.pad(b_second[None, :], ((0, depth - 1), (0, 256 - b_second.shape[0]))), head_zero.shape)
+    extra = jnp.stack([head_zero, head_one, jnp.zeros_like(head_zero)], 1)
+    low = jnp.concatenate([split(w_second), extra], 3)
+    pa = jnp.concatenate([split(w_first), low], 2)
+    spot = lax.broadcasted_iota(jnp.int32, (16, width), 1)
+    mask = jnp.where(spot < lengths[0], 0.0, -1e30).astype(bf16)
+    pt = jnp.concatenate([tokens[0], mask], 0)
+    ups = [w_up[:, k * width : (k + 1) * width] for k in range(w_up.shape[1] // width)]
+    pf = jnp.concatenate(ups + [w_out, jnp.zeros((8, width), bf16), w_down], 0)
+    return pa, pt, pf
+
+
+def on_device_fast(tokens, lengths, gain_one, w_value, w_first, b_first, w_second, b_second, w_out, gain_two, w_up, w_down, grad_out):
+    _, slots, width = tokens.shape
+    heads_all, depth, _ = w_first.shape
+    heads = heads_all // GROUP
+    me = lax.axis_index("tp")
+    pa, pt, pf = pack_inputs(
+        tokens, lengths, gain_one, w_value, w_first, b_first, w_second, b_second, w_out, gain_two, w_up, w_down
+    )
+    la, lt, lf = gather_call(pa, pt, pf)
+    b2 = lax.dynamic_index_in_dim(la[1, :, :, :, 24, 512:704], me, 2, False).reshape(heads, slots).astype(f32)
+    wf, ws, wv, small, normed, values, hid, slope, prob, join = attend_call(la, lt, b2)
+    joined = trade_call(join, 2)
+    result, gmid, gj, gf, gg2 = ffn_call(lf, joined, tokens[0], small, grad_out[0])
+    gmix = trade_call(gj, 3)
+    ga, gs, gn = back_call(wf, ws, wv, normed, values, hid, slope, prob, gmix, lt, gg2)
+    out_f, out_a, out_s, gtok = reduce_call(gf, ga, gs, gn, tokens[0], gmid, small)
+    low = out_a[:, :, 24:].astype(f32)
+    to_all = lambda v: v.transpose((1, 0) + tuple(range(2, v.ndim))).reshape((heads_all,) + v.shape[2:])
+    gb1 = to_all(low[:, :, :, 704])
+    gains = jnp.sum(low[2, :, :, 705:707], axis=0)
+    return (
+        result[None],
+        gtok[None],
+        gains[:, 0],
+        low[2, :, :, 512:704].transpose(1, 0, 2).reshape(depth, width),
+        to_all(out_a[:, :, :24].astype(f32)),
+        gb1,
+        to_all(low[:, :, :, :512]),
+        out_s[0, : b_second.shape[0]],
+        out_f[4 * depth : 5 * depth],
+        gains[:, 1],
+        out_f[: 4 * depth].reshape(4, depth, width).transpose(1, 0, 2).reshape(depth, 4 * width),
+        out_f[128:],
+    )
+
+
 def solution(mesh):
     wide, narrow = mesh.shape["wide"], mesh.shape["narrow"]
     grouped = Mesh(mesh.devices.reshape(GROUP, wide // GROUP, narrow), ALL)
@@ -174,8 +929,9 @@
     flat = P(ALL, None)
     mid = P(None, ALL, None)
     row = P(ALL, None, None)
+    body = on_device_fast if (wide, narrow) == (8, 4) else on_device
     return jax.shard_map(
-        on_device,
+        body,
         mesh=grouped,
         in_specs=(row, vec, vec, flat, mid, P(None, ALL), mid, vec, flat, vec, flat, flat, row),
         out_specs=(row, row, vec, flat, mid, P(None, ALL), mid, vec, flat, vec, flat, flat),

time: 1120 us -> 420 us (0.38)
  waiting for transfers between devices: 670 us -> 0 us
  Pallas kernels: 0 us -> 391 us
  matrix products: 201 us -> 0 us
  blocking collectives: 117 us -> 0 us
  other arithmetic: 62.3 us -> 3.1 us
  starting transfers between devices: 18.8 us -> 0 us
  between operations: 15.6 us -> 1.57 us
    reduce_scatter x6 -> x0, waiting for transfers between devices: 455 us -> none  [the longest x3 317 us: share(): lax.psum_scatter(grad.astype(bf16), ALL, scatter_dimension=0, tiled=True)]
    pallas_call x0 -> x7, Pallas kernels: none -> 391 us  [the longest x1 124 us: gather_call(): pl.pallas_call(gather_kernel, out_shape=(shape_of((heads, 2, 4, GROUP) +...]
    dot_general x21 -> x0, matrix products: 201 us -> none  [mm(): return jnp.einsum(spec, a, b, preferred_element_type=f32)]
    psum x1 -> x0, waiting for transfers between devices: 120 us -> none  [on_device(): vec = lax.psum(vec, ALL)]
    all_gather x6 -> x0, waiting for transfers between devices: 74.5 us -> none  [the longest x1 45.6 us: on_device(): wd = lax.all_gather(w_down, ALL, axis=0, tiled=True)]
    unnamed x2 -> x0, blocking collectives: 49.9 us -> none
    all_to_all x3 -> x0, blocking collectives: 39.2 us -> none  [the longest x2 23.3 us: to_heads(): lax.all_to_all(shard.reshape(GROUP, heads // GROUP, depth, width), 'tp',...]
    sub x2 -> x0, other arithmetic: 29.9 us -> none  [the longest x1 22.7 us: on_device(): grad_logits = (probabilities * (grad_weights - centre)).astype(bf16)]
  transfers between devices with their start and end apart: 19 -> 0, of which waited for: 13 -> 0; matrix products, arithmetic and copies ran while one was open for 18% -> 0% of each run, Pallas kernels for 0% -> 0%
where the time goes in v2:
time: 420 us; the launch traced here: 416 us
  Pallas kernels  391 us (93%)
  local copies, waits for them, and re-layouts  19.8 us (5%)
    pallas_call x1, Pallas kernels, gather_call(): pl.pallas_call(gather_kernel, out_shape=(shape_of((heads, 2, 4, GROUP) +...  124 us
    pallas_call x1, Pallas kernels, reduce_call(): pl.pallas_call(reduce_kernel, out_shape=(shape_of((rows, width), f32), sh...  119 us
    pallas_call x1, Pallas kernels, back_call(): pl.pallas_call(back_kernel, grid=(heads, GROUP), out_shape=(shape_of((hea...  50.7 us
    pallas_call x1, Pallas kernels, attend_call(): pl.pallas_call(attend_kernel, grid=(heads, GROUP), out_shape=(shape_of((h...  36.6 us
    pallas_call x1, Pallas kernels, ffn_call(): pl.pallas_call(ffn_kernel, out_shape=(shape_of((slots, width), f32), shap...  31.5 us
    pallas_call x2, Pallas kernels, trade_call(): pl.pallas_call(lambda *refs: trade_kernel(*refs), out_shape=shape_of(piec...  30.2 us

profile of v2, /device:TPU:0, one launch (start us, length us, event | category | flops | bytes accessed | tf_op | source)
XLA Modules:
  0.0 415.6 jit_solution(17599433741928027916)
XLA Ops:
  0.6 0.0 copy-start.5
  0.7 0.0 copy-start.3
  1.4 0.7 pad_maximum_fusion.1
  2.1 0.1 pad.15.clone
  2.1 0.7 broadcast_in_dim.28
  2.8 0.7 reshape.66
  3.5 0.1 copy.45
  3.6 0.1 copy.44
  3.8 0.9 reshape.65
  4.6 0.0 copy-start
  4.7 0.1 maximum_bitcast_fusion
  4.8 0.8 slice_dynamic-update-slice_fusion.3
  5.6 0.8 slice_dynamic-update-slice_fusion.2
  6.4 0.8 slice_dynamic-update-slice_fusion.1
  7.2 0.8 slice_dynamic-update-slice_fusion
  8.0 0.8 constant_dynamic-update-slice_fusion.2
  8.7 0.9 constant_dynamic-update-slice_fusion.pf
  9.7 0.0 copy-done.5
  9.7 0.0 copy-done.3
  9.7 0.0 copy-start.4
  9.7 1.1 maximum_maximum_fusion.pa
  10.8 0.0 copy-done
  10.8 0.9 pad_maximum_fusion.pt
  11.7 0.0 copy-done.4
  11.7 123.6 %shard_map.220 = (bf16[3,2,4,4,48,768]{5,4,3,2,1,0:T(8,128)(2,1)}, bf16[4,528,768]{2,1,0:T(8,128)(2,1)}, bf16[2,2,2,4,224,768]{5,4,3,2,1,0:T(8,128)(2,1)}) custom-call(bf16[4,3,48,768]{3,2,1,0:T(8,128)(2,1)} %maximum_maximum_fusion.pa, bf16[528,768]{1,0:T(8,128)(2,1)} %pad_maximum_fusion.pt, bf16[224,768]{1,0:T(8,128)(2,1)} %copy-done.4), custom_call_target="tpu_custom_call" | custom-call | tf_op jit(solution)/shard_map/pallas_call | solution.py:279
  135.3 0.9 slice.55
  136.3 0.7 reshape.74.b2
  137.0 36.6 %shard_map.221 = (bf16[3,768,768]{2,1,0:T(8,128)(2,1)}, bf16[3,768,512]{2,1,0:T(8,128)(2,1)}, bf16[768,256]{1,0:T(8,128)(2,1)}, f32[8,768]{1,0:T(8,128)}, bf16[4...) custom-call(bf16[3,2,4,4,48,768]{5,4,3,2,1,0:T(8,128)(2,1)} %get-tup, ...), custom_call_target="tpu_custom_call" | custom-call | tf_op jit(solution)/shard_map/pallas_call | solution.py:412
  173.6 15.5 %shard_map.222.joined = bf16[4,512,256]{2,1,0:T(8,128)(2,1)} custom-call(bf16[4,512,256]{2,1,0:T(8,128)(2,1)} %get-tuple-element.40.refs_0_), custom_call_target="tpu_custom_call" | custom-call | tf_op jit(solution)/shard_map/pallas_call | solution.py:317
  189.1 31.5 %shard_map.223 = (f32[512,768]{1,0:T(8,128)}, f32[512,768]{1,0:T(8,128)}, bf16[4,512,256]{2,1,0:T(8,128)(2,1)}, bf16[2,2,2,4,224,768]{5,4,3,2,1,0:T(8,128)(2,1)}, f32[8,768]{1,0:T(8,128)}) custom-call(bf16[2,2,2,4,224,768]{5,4,3,2,1,0:T(8,128)(2,1)} %get-tuple-element.37.lf, bf16[4,512,256]{2,1,0:T(8,128)(2,1)} %shard_map.222.joined, ...), custom_call_target="tpu_custom_call" | custom-call | tf_op jit(solution)/shard_map/pallas_call | solution.py:535
  220.6 14.7 %shard_map.224.gmix = bf16[4,512,256]{2,1,0:T(8,128)(2,1)} custom-call(bf16[4,512,256]{2,1,0:T(8,128)(2,1)} %get-tuple-element.52.refs_0_), custom_call_target="tpu_custom_call" | custom-call | tf_op jit(solution)/shard_map/pallas_call | solution.py:317
  235.3 50.7 %shard_map.225 = (bf16[3,2,4,4,48,768]{5,4,3,2,1,0:T(8,128)(2,1)}, f32[2,4,8,256]{3,2,1,0:T(8,128)}, bf16[4,512,768]{2,1,0:T(8,128)(2,1)}) custom-call(bf16[3,768,768]{2,1,0:T(8,128)(2,1)} %get-tuple-element.44.wf, bf16[3,768,512]{2,1,0:T(8,128)(2,1)} %get-tuple-element.45.ws, bf16[768,256]{1,0:T(8,128)(2,1)} %get-tuple-element.46.wv, ...), custom_call_target="tpu_custom_call" | custom-call | tf_op jit(solution)/shard_map/pallas_call | solution.py:665
  286.0 118.6 %shard_map.226 = (f32[224,768]{1,0:T(8,128)}, bf16[3,4,48,768]{3,2,1,0:T(8,128)(2,1)}, f32[8,256]{1,0:T(8,128)}, f32[512,768]{1,0:T(8,128)}) custom-call(bf16[2,2,2,4,224,768]{5,4,3,2,1,0:T(8,128)(2,1)} %get-tuple-element.43.gf, bf16[3,2,4,4,48,768]{5,4,3,2,1,0:T(8,128)(2,1)} %get-tuple-element.54.ga, f32[2,4,8,256]{3,2,1,0:T(8,128)} %get-tuple-element.55.gs, ...), custom_call_target="tpu_custom_call" | custom-call | tf_op jit(solution)/shard_map/pallas_call | solution.py:822
  404.6 0.0 copy-start.2
  404.6 1.3 slice.63
  406.0 1.5 slice.64
  407.5 1.8 fusion
  409.3 0.7 copy.51
  410.0 0.2 convert_bitcast_fusion
  410.2 1.0 copy.47
  411.2 0.2 slice_reduce_fusion
  411.4 0.6 reshape.70
  412.0 0.1 slice_reduce_fusion.1
  412.1 0.7 slice_reduce_fusion.2
  412.8 0.1 slice_bitcast_fusion
  412.8 0.9 copy.49
  413.7 0.7 reshape.67
  414.5 1.1 copy.62
  (17 shorter events, 0.2 us)
Async XLA Ops:
  0.6 9.0 %copy-start.5 = (bf16[12,24,512]{2,1,0:T(8,128)(2,1)S(1)}, bf16[12,24,512]{2,1,0:T(8,128)(2,1)}, u32[]{:S(2)}) copy-start(bf16[12,24,512]{2,1,0:T(8,128)(2,1)} %param.19) | copy-start | bytes 884740
  0.7 9.0 %copy-start.3 = (bf16[12,24,768]{2,1,0:T(8,128)(2,1)S(1)}, bf16[12,24,768]{2,1,0:T(8,128)(2,1)}, u32[]{:S(2)}) copy-start(bf16[12,24,768]{2,1,0:T(8,128)(2,1)} %param.17) | copy-start | bytes 1327108
  4.6 6.2 %copy-start = (bf16[1,512,768]{2,1,0:T(8,128)(2,1)S(1)}, bf16[1,512,768]{2,1,0:T(8,128)(2,1)}, u32[]{:S(2)}) copy-start(bf16[1,512,768]{2,1,0:T(8,128)(2,1)} %param.13) | copy-start | bytes 2359300
  9.7 2.1 copy-start.4
  404.6 5.4 %copy-start.2 = (bf16[3,4,48,768]{3,2,1,0:T(8,128)(2,1)S(1)}, bf16[3,4,48,768]{3,2,1,0:T(8,128)(2,1)}, u32[]{:S(2)}) copy-start(bf16[3,4,48,768]{3,2,1,0:T(8,128)(2,1)} %get-tuple-element.59) | copy-start | bytes 2654212
  411.2 3.3 copy-start.1

commit v3 on v2

--- a/solution.py
+++ b/solution.py
@@ -216,112 +216,33 @@
 
 
 def remote(src, dst, send, recv, device):
-    copy = pltpu.make_async_remote_copy(
+    return pltpu.make_async_remote_copy(
         src_ref=src, dst_ref=dst, send_sem=send, recv_sem=recv, device_id=device, device_id_type=MESH
     )
-    copy.start()
-    return copy
 
 
 def local(src, dst, sem):
-    copy = pltpu.make_async_copy(src, dst, sem)
-    copy.start()
-    return copy
-
-
-def gather_kernel(pa, pt, pf, la, lt, lf, own, s1, r1, s2, r2, s3, r3, st, rt, sf, rf):
+    return pltpu.make_async_copy(src, dst, sem)
+
+
+def start(copies):
+    for copy in copies:
+        copy.start()
+
+
+def wait(copies):
+    for copy in copies:
+        copy.wait()
+
+
+def square():
     t, c, z = place()
-    sibling = (t, 1 - c, z)
-    tps, zs = group_peers(), line_peers()
-    greet([(p, c, z) for p in tps] + [(t, c, p) for p in zs] + [sibling])
     y, x = t // 2, t % 2
+    tps = group_peers()
     slow, fast = (1 - c) * y + c * x, (1 - c) * x + c * y
     fast_peer = (1 - c) * tps[0] + c * tps[1]
     slow_peer = (1 - c) * tps[1] + c * tps[0]
-    heads = la.shape[0]
-    mine = [local(pa.at[t, h], la.at[h, c, z, t], own.at[h]) for h in range(heads)]
-    mine_f = local(pf, lf.at[c, slow, fast, z], own.at[heads])
-    mine_t = local(pt, lt.at[t], own.at[heads + 1])
-    one, two, three = [], [], []
-    for h in range(heads):
-        one.append(
-            [remote(pa.at[p, h], la.at[h, c, z, t], s1.at[h, k], r1.at[h, k], (p, c, z)) for k, p in enumerate(tps)]
-        )
-    f1 = [remote(pf, lf.at[c, slow, fast, z], sf.at[k], rf.at[k], (t, c, p)) for k, p in enumerate(zs)]
-    toks = [remote(pt, lt.at[t], st.at[k], rt.at[k], (p, c, z)) for k, p in enumerate(tps)]
-    for h in range(heads):
-        mine[h].wait()
-        for copy in one[h]:
-            copy.wait()
-        two.append(
-            [remote(la.at[h, c, z], la.at[h, c, z], s2.at[h, k], r2.at[h, k], (t, c, p)) for k, p in enumerate(zs)]
-        )
-    mine_f.wait()
-    for copy in f1:
-        copy.wait()
-    f2 = remote(lf.at[c, slow, fast], lf.at[c, slow, fast], sf.at[3], rf.at[3], (fast_peer, c, z))
-    for h in range(heads):
-        if h == 1:
-            f2.wait()
-            f3 = remote(lf.at[c, slow], lf.at[c, slow], sf.at[4], rf.at[4], (slow_peer, c, z))
-        for copy in two[h]:
-            copy.wait()
-        three.append(remote(la.at[h, c], la.at[h, c], s3.at[h], r3.at[h], sibling))
-    f3.wait()
-    f4 = remote(lf.at[c], lf.at[c], sf.at[5], rf.at[5], sibling)
-    mine_t.wait()
-    for copy in toks + three + [f4]:
-        copy.wait()
-
-
-def gather_call(pa, pt, pf):
-    heads = pa.shape[1]
-    return pl.pallas_call(
-        gather_kernel,
-        out_shape=(
-            shape_of((heads, 2, 4, GROUP) + pa.shape[2:], bf16),
-            shape_of((GROUP,) + pt.shape, bf16),
-            shape_of((2, 2, 2, 4) + pf.shape, bf16),
-        ),
-        in_specs=[ANY] * 3,
-        out_specs=(ANY,) * 3,
-        scratch_shapes=[
-            DMA((heads + 2,)),
-            DMA((heads, 3)),
-            DMA((heads, 3)),
-            DMA((heads, 3)),
-            DMA((heads, 3)),
-            DMA((heads,)),
-            DMA((heads,)),
-            DMA((3,)),
-            DMA((3,)),
-            DMA((6,)),
-            DMA((6,)),
-        ],
-        compiler_params=pltpu.CompilerParams(collective_id=1, has_side_effects=True),
-    )(pa, pt, pf)
-
-
-def trade_kernel(src, dst, own, send, recv):
-    t, c, z = place()
-    tps = group_peers()
-    greet([(p, c, z) for p in tps])
-    mine = local(src.at[t], dst.at[t], own)
-    copies = [remote(src.at[p], dst.at[t], send.at[k], recv.at[k], (p, c, z)) for k, p in enumerate(tps)]
-    mine.wait()
-    for copy in copies:
-        copy.wait()
-
-
-def trade_call(pieces, collective_id):
-    return pl.pallas_call(
-        lambda *refs: trade_kernel(*refs),
-        out_shape=shape_of(pieces.shape, pieces.dtype),
-        in_specs=[ANY],
-        out_specs=ANY,
-        scratch_shapes=[DMA, DMA((3,)), DMA((3,))],
-        compiler_params=pltpu.CompilerParams(collective_id=collective_id, has_side_effects=True),
-    )(pieces)
+    return slow, fast, (slow_peer, c, z), (fast_peer, c, z)
 
 
 def gelu_pair(v):
@@ -335,21 +256,86 @@
     return shifted * scale, scale
 
 
-def attend_kernel(la, lt, b2, wf, ws, wv, small, normed, values, hid, slope, prob, join, nrm, val, cols):
+def attend_kernel(
+    pa, pt, pf, wf, ws, wv, small, normed, values, hid, slope, prob, joined, lf,
+    la, lt, nrm, val, cols, b2, join, own, s1, r1, s2, r2, s3, r3, st, rt, sf, rf, sj, rj,
+):
     h, r = pl.program_id(0), pl.program_id(1)
     width = wf.shape[-1]
+    heads = la.shape[0]
+    t, c, z = place()
+    sibling = (t, 1 - c, z)
+    tps, zs = group_peers(), line_peers()
+    slow, fast, slow_dev, fast_dev = square()
+
+    a1 = lambda i: [
+        remote(pa.at[p, i], la.at[i, c, z, t], s1.at[i, k], r1.at[i, k], (p, c, z)) for k, p in enumerate(tps)
+    ]
+    a2 = lambda i: [
+        remote(la.at[i, c, z], la.at[i, c, z], s2.at[i, k], r2.at[i, k], (t, c, p)) for k, p in enumerate(zs)
+    ]
+    a3 = lambda i: [remote(la.at[i, c], la.at[i, c], s3.at[i], r3.at[i], sibling)]
+    mine = lambda i: [local(pa.at[t, i], la.at[i, c, z, t], own.at[i])]
+    mine_t = lambda: [local(pt, lt.at[3], own.at[heads])]
+    mine_f = lambda: [local(pf, lf.at[c, slow, fast, z], own.at[heads + 1])]
+    mine_j = lambda: [local(join.at[3], joined.at[t], own.at[heads + 2])]
+    toks = lambda: [remote(pt, lt.at[k], st.at[k], rt.at[k], (p, c, z)) for k, p in enumerate(tps)]
+    f1 = lambda: [remote(pf, lf.at[c, slow, fast, z], sf.at[k], rf.at[k], (t, c, p)) for k, p in enumerate(zs)]
+    f2 = lambda: [remote(lf.at[c, slow, fast], lf.at[c, slow, fast], sf.at[3], rf.at[3], fast_dev)]
+    f3 = lambda: [remote(lf.at[c, slow], lf.at[c, slow], sf.at[4], rf.at[4], slow_dev)]
+    f4 = lambda: [remote(lf.at[c, slow], lf.at[c, slow], sf.at[5], rf.at[5], sibling)]
+    f5 = lambda: [remote(lf.at[c, 1 - slow], lf.at[c, 1 - slow], sf.at[6], rf.at[6], sibling)]
+    out_j = lambda k: [remote(join.at[k], joined.at[t], sj.at[k], rj.at[k], (tps[k], c, z))]
+
+    def at_step(i, j):
+        return pl.when((h == i) & (r == j))
+
+    @at_step(0, 0)
+    def _():
+        greet([(p, c, z) for p in tps] + [(t, c, p) for p in zs] + [sibling])
+        for i in range(heads):
+            start(mine(i) + a1(i))
+        start(mine_f() + f1() + mine_t() + toks())
+        for i in range(heads):
+            wait(mine(i) + a1(i))
+            start(a2(i))
+        wait(a2(0))
+        start(a3(0))
+        wait(mine_t() + toks() + a3(0))
+
+    @at_step(0, 1)
+    def _():
+        wait(mine_f() + f1())
+        start(f2())
+
+    @at_step(1, 0)
+    def _():
+        wait(a2(1))
+        start(a3(1))
+        wait(a3(1))
+
+    @at_step(1, 1)
+    def _():
+        wait(f2())
+        start(f3() + f4())
+
+    @at_step(2, 0)
+    def _():
+        wait(a2(2))
+        start(a3(2))
+        wait(a3(2))
 
     @pl.when(r == 0)
     def _():
-        def unpack(t, carry):
-            for c in range(2):
-                for z in range(0, 4, 2):
+        def unpack(i, carry):
+            for cc in range(2):
+                for zz in range(0, 4, 2):
                     tops, lows = [], []
                     for k in range(2):
-                        tops.append(la[0, c, z + k, t, 0:32, :].astype(f32)[0:24])
-                        lows.append(la[0, c, z + k, t, 16:48, :].astype(f32)[8:32])
+                        tops.append(la[h, cc, zz + k, i, 0:32, :].astype(f32)[0:24])
+                        lows.append(la[h, cc, zz + k, i, 16:48, :].astype(f32)[8:32])
                     top, low = jnp.concatenate(tops, 0), jnp.concatenate(lows, 0)
-                    at = pl.ds(pl.multiple_of((t * 8 + c * 4 + z) * 24, 48), 48)
+                    at = pl.ds(pl.multiple_of((i * 8 + cc * 4 + zz) * 24, 48), 48)
                     wf[0, at, :] = top.astype(bf16)
                     ws[0, at, :] = low[:, :512].astype(bf16)
 
@@ -368,10 +354,19 @@
         @pl.when(h == 0)
         def _():
             small[...] = cols[...].T[64:72]
+            mine_rows = cols[pl.ds(pl.multiple_of(t * 192, 192), 192), :].astype(bf16)
+            lane = lax.broadcasted_iota(jnp.int32, (128, 512), 0)
+            spot = lax.broadcasted_iota(jnp.int32, (128, 512), 1)
+            spread = dot_nn(mine_rows, jnp.where(lane - 69 == spot % 8, 1.0, 0.0).astype(bf16))
+            row = lax.broadcasted_iota(jnp.int32, (64, 512), 0)
+            spot = lax.broadcasted_iota(jnp.int32, (64, 512), 1)
+            for i in range(heads):
+                picked = jnp.where(row == spot // 8, spread[64 * i : 64 * i + 64], 0.0)
+                b2[i] = jnp.broadcast_to(jnp.sum(picked, axis=0, keepdims=True), (8, 512))
 
     @pl.when(h == 0)
     def _():
-        unit, _ = centre_rows(lt[0, 0:512, :].astype(f32))
+        unit, _ = centre_rows(lt[r, 0:512, :].astype(f32))
         out = (unit * small[3:4]).astype(bf16)
         nrm[r] = out
         normed[0] = out
@@ -379,11 +374,10 @@
         val[r] = v
         values[0] = v
 
-    mask = lt[0, 512:528, 0:512].astype(f32)[0:1]
+    mask = lt[r, 512:528, 0:512].astype(f32)[0:1]
     row = lax.broadcasted_iota(jnp.int32, (8, width), 0)
     b1 = jnp.sum(jnp.where(row == h, small[...], 0.0), axis=0, keepdims=True)
-    row = lax.broadcasted_iota(jnp.int32, b2.shape, 0)
-    shift = jnp.sum(jnp.where(row == h, b2[...], 0.0), axis=0, keepdims=True) + mask
+    shift = b2[h, 0:1] + mask
     tile = pl.ds(pl.multiple_of((h // 2) * 128, 128), 128)
     step = 256
     for m in range(0, 512, step):
@@ -402,9 +396,27 @@
         old = join[r, at, tile].astype(f32)
         join[r, at, tile] = jnp.where((h == 1) & (lane < 64), old, mix).astype(bf16)
 
-
-def attend_call(la, lt, b2):
-    heads, width = la.shape[0], la.shape[-1]
+    for k in range(3):
+
+        @at_step(2, k)
+        def _():
+            start(out_j(k))
+
+    @at_step(2, 2)
+    def _():
+        wait(f3())
+        start(f5())
+
+    @at_step(2, 3)
+    def _():
+        start(mine_j())
+        for k in range(3):
+            wait(out_j(k))
+        wait(mine_j() + f4() + f5())
+
+
+def attend_call(pa, pt, pf):
+    heads, width = pa.shape[1], pa.shape[-1]
     slots = 512
     by_row = lambda h, r: (jnp.where(h == 0, r, GROUP - 1), 0, 0)
     by_head = lambda h, r: (h, 0, 0)
@@ -423,12 +435,9 @@
             shape_of((heads, GROUP, slots, width), bf16),
             shape_of((heads, GROUP, slots, slots), bf16),
             shape_of((GROUP, slots, 256), bf16),
+            shape_of((2, 2, 2, 4) + pf.shape, bf16),
         ),
-        in_specs=[
-            pl.BlockSpec((1,) + la.shape[1:], lambda h, r: (h, 0, 0, 0, 0, 0)),
-            pl.BlockSpec((1,) + lt.shape[1:], lambda h, r: (r, 0, 0)),
-            pl.BlockSpec(b2.shape, lambda h, r: (0, 0)),
-        ],
+        in_specs=[ANY] * 3,
         out_specs=(
             pl.BlockSpec((1, width, width), by_head),
             pl.BlockSpec((1, width, slots), by_head),
@@ -439,15 +448,33 @@
             pl.BlockSpec((1, 1, slots, width), both),
             pl.BlockSpec((1, 1, slots, width), both),
             pl.BlockSpec((1, 1, slots, slots), both),
-            pl.BlockSpec((GROUP, slots, 256), lambda h, r: (0, 0, 0)),
+            ANY,
+            ANY,
         ),
         scratch_shapes=[
+            pltpu.VMEM((heads, 2, 4, GROUP) + pa.shape[2:], bf16),
+            pltpu.VMEM((GROUP,) + pt.shape, bf16),
             pltpu.VMEM((GROUP, slots, width), bf16),
             pltpu.VMEM((GROUP, slots, 256), bf16),
             pltpu.VMEM((width, 128), f32),
+            pltpu.VMEM((heads, 8, slots), f32),
+            pltpu.VMEM((GROUP, slots, 256), bf16),
+            DMA((heads + 3,)),
+            DMA((heads, 3)),
+            DMA((heads, 3)),
+            DMA((heads, 3)),
+            DMA((heads, 3)),
+            DMA((heads,)),
+            DMA((heads,)),
+            DMA((3,)),
+            DMA((3,)),
+            DMA((7,)),
+            DMA((7,)),
+            DMA((3,)),
+            DMA((3,)),
         ],
-        compiler_params=pltpu.CompilerParams(vmem_limit_bytes=VMEM_LIMIT),
-    )(la, lt, b2)
+        compiler_params=pltpu.CompilerParams(collective_id=1, has_side_effects=True, vmem_limit_bytes=VMEM_LIMIT),
+    )(pa, pt, pf)
 
 
 def slab(t, c, z):
@@ -455,8 +482,22 @@
     return (0, y, x, z) if c == 0 else (1, x, y, z)
 
 
-def ffn_kernel(lf, joined, tokens, small, gout, result, gmid, gj, gf, gg2, wu, wo, n2, acc, gn2, gwu):
+def ffn_kernel(
+    lf, joined, tokens, small, gout, result, gmid, gmix, half, gg2,
+    gf, gj, more, wu, wo, n2, acc, gn2, gwu, own, sg, rg, sx, rx,
+):
     width = tokens.shape[-1]
+    me, core, z_me = place()
+    tps = group_peers()
+    sibling = (me, 1 - core, z_me)
+    parts = (slice(0, 96), slice(128, 224), slice(96, 128))
+    cross = lambda k: [
+        remote(
+            gf.at[1 - core, :, :, :, parts[k], :], more.at[:, :, :, parts[k], :], sx.at[k], rx.at[k], sibling
+        )
+    ]
+    out_g = lambda k: [remote(gj.at[tps[k]], gmix.at[k], sg.at[k], rg.at[k], (tps[k], core, z_me))]
+    greet([(p, core, z_me) for p in tps] + [sibling])
     wo[...] = jnp.zeros_like(wo)
     for t in range(GROUP):
         for c in range(2):
@@ -506,6 +547,7 @@
         return carry
 
     lax.fori_loop(0, 2, block, 0)
+    start(cross(0) + cross(1))
     result[...] = acc[...]
     middle = tokens[...].astype(f32)
     for t in range(GROUP):
@@ -522,12 +564,32 @@
     ga = gm.astype(bf16)
     for t in range(GROUP):
         gj[t] = dot_nt(ga, wo[t]).astype(bf16)
+    for k in range(3):
+        start(out_g(k))
+    mine = local(gj.at[me], gmix.at[3], own)
+    mine.start()
+    for t in range(GROUP):
         gwo = dot_tn(joined[t], ga)
         for c in range(2):
             for z in range(4):
                 at = (c * 4 + z) * 24
                 padded = jnp.concatenate([gwo[at : at + 24, :], jnp.zeros((8, width), f32)], 0)
                 gf[slab(t, c, z) + (slice(96, 128),)] = padded.astype(bf16)
+    start(cross(2))
+    for k in range(3):
+        wait(cross(k))
+
+        def fold(i, carry):
+            for j in range(2):
+                for z in range(4):
+                    spot = (i, j, z, parts[k])
+                    half[spot] = (gf[(core,) + spot].astype(f32) + more[spot].astype(f32)).astype(bf16)
+            return carry
+
+        lax.fori_loop(0, 2, fold, 0)
+    for k in range(3):
+        wait(out_g(k))
+    mine.wait()
 
 
 def ffn_call(lf, joined, tokens, small, gout):
@@ -538,28 +600,121 @@
             shape_of((slots, width), f32),
             shape_of((slots, width), f32),
             shape_of(joined.shape, bf16),
-            shape_of(lf.shape, bf16),
+            shape_of(lf.shape[1:], bf16),
             shape_of((8, width), f32),
         ),
         in_specs=[FULL] * 5,
-        out_specs=(FULL,) * 5,
+        out_specs=(FULL, FULL, ANY, FULL, FULL),
         scratch_shapes=[
+            pltpu.VMEM(lf.shape, bf16),
+            pltpu.VMEM(joined.shape, bf16),
+            pltpu.VMEM(lf.shape[1:], bf16),
             pltpu.VMEM((2, width, width), bf16),
             pltpu.VMEM((GROUP, 256, width), bf16),
             pltpu.VMEM((slots, width), bf16),
             pltpu.VMEM((slots, width), f32),
             pltpu.VMEM((slots, width), f32),
             pltpu.VMEM((2, width, width), f32),
+            DMA,
+            DMA((3,)),
+            DMA((3,)),
+            DMA((3,)),
+            DMA((3,)),
         ],
-        compiler_params=pltpu.CompilerParams(vmem_limit_bytes=VMEM_LIMIT),
+        compiler_params=pltpu.CompilerParams(collective_id=2, has_side_effects=True, vmem_limit_bytes=VMEM_LIMIT),
     )(lf, joined, tokens, small, gout)
 
 
 def back_kernel(
-    wf, ws, wv, normed, values, hid, slope, prob, gmix, lt, gg2, ga, gs, gn_out, awf, aws, ab1, ab2, gn, gv, awv, ag1
+    wf, ws, wv, normed, values, hid, slope, prob, gmix, gg2, half, tokens, gmid, small, out_f, out_a, out_s, gtok,
+    awf, aws, ab1, ab2, gn, gv, awv, ag1, ga, gs, gnb, nb, fs, fb2, fb3, fb4, cb1, cb2, sb1, sb2,
+    own, s1, r1, s2, r2, s3, r3, sn, rn, sf, rf, sv, rv,
 ):
     h, r = pl.program_id(0), pl.program_id(1)
     width = wf.shape[-1]
+    heads = ga.shape[0]
+    t, c, z = place()
+    sibling = (t, 1 - c, z)
+    tps, zs = group_peers(), line_peers()
+    slow, fast, slow_dev, fast_dev = square()
+
+    a1 = lambda i: [remote(ga.at[i, 1 - c], cb1.at[i], s1.at[i], r1.at[i], sibling)]
+    a2 = lambda i: [
+        remote(ga.at[i, c, p], cb2.at[i, k], s2.at[i, k], r2.at[i, k], (t, c, p)) for k, p in enumerate(zs)
+    ]
+    a3 = lambda i: [
+        remote(ga.at[i, c, z, p], out_a.at[i, t], s3.at[i, k], r3.at[i, k], (p, c, z)) for k, p in enumerate(tps)
+    ]
+    mine = lambda i: [local(ga.at[i, c, z, t], out_a.at[i, t], own.at[i])]
+    mine_f = lambda: [local(half.at[slow], fs, own.at[heads])]
+    v1 = lambda: [remote(gs.at[1 - c], sb1, sv.at[0], rv.at[0], sibling)]
+    v2 = lambda: [remote(gs.at[c, p], sb2.at[k], sv.at[1 + k], rv.at[1 + k], (t, c, p)) for k, p in enumerate(zs)]
+    f2 = lambda: [remote(half.at[1 - slow], fb2, sf.at[0], rf.at[0], slow_dev)]
+    f3 = lambda: [remote(fs.at[1 - fast], fb3, sf.at[1], rf.at[1], fast_dev)]
+    f4 = lambda: [
+        remote(fs.at[fast, p], fb4.at[k], sf.at[2 + k], rf.at[2 + k], (t, c, p)) for k, p in enumerate(zs)
+    ]
+    out_n = lambda k: [remote(gnb.at[k], nb.at[k], sn.at[k], rn.at[k], (tps[k], c, z))]
+
+    def at_step(i, j):
+        return pl.when((h == i) & (r == j))
+
+    def meet(i):
+        wait(a1(i))
+
+        def line(k, carry):
+            for j in range(GROUP):
+                ga[i, c, k, j] = (ga[i, c, k, j].astype(f32) + cb1[i, k, j].astype(f32)).astype(bf16)
+            return carry
+
+        lax.fori_loop(0, 4, line, 0)
+        start(a2(i))
+
+    def deal(i):
+        wait(a2(i))
+
+        def fold(j, carry):
+            total = ga[i, c, z, j].astype(f32)
+            for k in range(3):
+                total = total + cb2[i, k, j].astype(f32)
+            ga[i, c, z, j] = total.astype(bf16)
+            return carry
+
+        lax.fori_loop(0, GROUP, fold, 0)
+        start(mine(i) + a3(i))
+
+    def add_slabs(total, more):
+        def one(k, carry):
+            fs[total, k] = (fs[total, k].astype(f32) + more[k].astype(f32)).astype(bf16)
+            return carry
+
+        lax.fori_loop(0, 4, one, 0)
+
+    @at_step(0, 0)
+    def _():
+        greet([(p, c, z) for p in tps] + [(t, c, p) for p in zs] + [sibling])
+        start(f2() + mine_f())
+
+    @at_step(1, 0)
+    def _():
+        meet(0)
+
+    @at_step(1, 3)
+    def _():
+        wait(f2() + mine_f())
+        add_slabs(1 - fast, fb2.at[1 - fast])
+        start(f3())
+        add_slabs(fast, fb2.at[fast])
+
+    @at_step(2, 0)
+    def _():
+        meet(1)
+
+    @at_step(2, 3)
+    def _():
+        wait(f3())
+        add_slabs(fast, fb3)
+        start(f4())
 
     @pl.when(r == 0)
     def _():
@@ -604,10 +759,9 @@
     def _():
         gvb = gv[r].astype(bf16)
         total = gn[r] + part + dot_nt(gvb, wv[...])
-        gn_out[0] = total.astype(bf16)
-        unit, _ = centre_rows(lt[0, 0:512, :].astype(f32))
-        first = jnp.where(r == 0, 0.0, 1.0)
-        ag1[...] = jnp.where(r == 0, 0.0, ag1[...]) + jnp.sum((total * unit).reshape(-1, 8, width), axis=0)
+        gn[r] = total
+        both = (total * normed[0].astype(f32)).reshape(-1, 8, width)
+        ag1[...] = jnp.where(r == 0, 0.0, ag1[...]) + jnp.sum(both, axis=0)
         more = dot_tn(normed[0], gvb)
 
         @pl.when(r == 0)
@@ -618,12 +772,20 @@
         def _():
             awv[...] += more
 
+        for k in range(3):
+
+            @pl.when(r == k)
+            def _():
+                gnb[k] = total.astype(bf16)
+                start(out_n(k))
+
     @pl.when(r == GROUP - 1)
     def _():
         last = h == 2
         row = lax.broadcasted_iota(jnp.int32, (128, width), 0)
         stack = jnp.where(row == 64, jnp.sum(ab1[...], axis=0, keepdims=True), 0.0)
-        stack = jnp.where(last & (row == 65), jnp.sum(ag1[...], axis=0, keepdims=True), stack)
+        gains = jnp.sum(ag1[...], axis=0, keepdims=True) / small[3:4]
+        stack = jnp.where(last & (row == 65), gains, stack)
         stack = jnp.where(last & (row == 66), jnp.sum(gg2[...], axis=0, keepdims=True), stack)
         cols = stack.T
         lane = lax.broadcasted_iota(jnp.int32, (width, 128), 1)
@@ -637,57 +799,97 @@
         def _():
             awv[:, 128:256] = jnp.where(lane < 64, awv[:, 128:256], cols)
 
-        def pack(t, carry):
-            for c in range(2):
-                for z in range(4):
-                    at = pl.ds(pl.multiple_of((t * 8 + c * 4 + z) * 24, 8), 24)
+        def pack(i, carry):
+            for cc in range(2):
+                for zz in range(4):
+                    at = pl.ds(pl.multiple_of((i * 8 + cc * 4 + zz) * 24, 8), 24)
                     low = jnp.concatenate([aws[at, :], awv[at, :]], 1)
-                    ga[0, c, z, t] = jnp.concatenate([awf[at, :], low], 0).astype(bf16)
+                    ga[h, cc, zz, i] = jnp.concatenate([awf[at, :], low], 0).astype(bf16)
             return carry
 
         lax.fori_loop(0, GROUP, pack, 0)
 
-        @pl.when(last)
+    for i in range(heads):
+
+        @at_step(i, 3)
         def _():
-            flat = jnp.concatenate([jnp.sum(ab2[k], axis=0, keepdims=True) for k in range(3)], 1)
-            flat = jnp.broadcast_to(flat, (8, 1536))
-            for c in range(2):
-                for z in range(4):
-                    s = (c * 4 + z) * 192
-                    gs[c, z] = (pltpu.roll(flat, 1536 - s, 1) if s else flat)[:, 0:256]
-
-
-def back_call(wf, ws, wv, normed, values, hid, slope, prob, gmix, lt, gg2):
+            start(a1(i))
+
+    @at_step(2, 3)
+    def _():
+        flat = jnp.concatenate([jnp.sum(ab2[k], axis=0, keepdims=True) for k in range(3)], 1)
+        flat = jnp.broadcast_to(flat, (8, 1536))
+        for cc in range(2):
+            for zz in range(4):
+                s = (cc * 4 + zz) * 192
+                gs[cc, zz] = (pltpu.roll(flat, 1536 - s, 1) if s else flat)[:, 0:256]
+        start(v1())
+        meet(2)
+        wait(v1())
+        gs[c] += sb1[...]
+        start(v2())
+        deal(0)
+        for k in range(3):
+            wait(out_n(k))
+
+        def ln_back(i, carry):
+            at = pl.ds(pl.multiple_of(i * 128, 128), 128)
+            g = gn[3, at, :] + nb[0, at, :].astype(f32) + nb[1, at, :].astype(f32) + nb[2, at, :].astype(f32)
+            unit, scale = centre_rows(tokens[at, :].astype(f32))
+            gu = g * small[3:4]
+            back = scale * (
+                gu - jnp.mean(gu, axis=-1, keepdims=True) - unit * jnp.mean(gu * unit, axis=-1, keepdims=True)
+            )
+            gtok[at, :] = gmid[at, :] + back
+            return carry
+
+        lax.fori_loop(0, 4, ln_back, 0)
+        deal(1)
+        wait(f4())
+        total = fs[fast, z].astype(f32)
+        for k in range(3):
+            total = total + fb4[k].astype(f32)
+        out_f[...] = total
+        wait(v2())
+        out_s[...] = gs[c, z] + sb2[0] + sb2[1] + sb2[2]
+        deal(2)
+        for i in range(heads):
+            wait(mine(i) + a3(i))
+
+
+def back_call(wf, ws, wv, normed, values, hid, slope, prob, gmix, gg2, half, tokens, gmid, small):
     heads, width, slots = ws.shape
+    rows = half.shape[-2]
     by_head = lambda h, r: (h, 0, 0)
     row = lambda h, r: (r, 0, 0)
     both = lambda h, r: (h, r, 0, 0)
+    flat = lambda h, r: (0, 0)
     return pl.pallas_call(
         back_kernel,
         grid=(heads, GROUP),
         out_shape=(
-            shape_of((heads, 2, 4, GROUP, 48, width), bf16),
-            shape_of((2, 4, 8, 256), f32),
-            shape_of((GROUP, slots, width), bf16),
+            shape_of((rows, width), f32),
+            shape_of((heads, GROUP, 48, width), bf16),
+            shape_of((8, 256), f32),
+            shape_of(tokens.shape, f32),
         ),
         in_specs=[
             pl.BlockSpec((1, width, width), by_head),
             pl.BlockSpec((1, width, slots), by_head),
-            pl.BlockSpec((width, 256), lambda h, r: (0, 0)),
+            pl.BlockSpec((width, 256), flat),
             pl.BlockSpec((1, slots, width), row),
             pl.BlockSpec((1, slots, 256), row),
             pl.BlockSpec((1, 1, slots, width), both),
             pl.BlockSpec((1, 1, slots, width), both),
             pl.BlockSpec((1, 1, slots, slots), both),
             pl.BlockSpec((1, slots, 256), row),
-            pl.BlockSpec((1,) + lt.shape[1:], lambda h, r: (jnp.where(h == 2, r, 0), 0, 0)),
-            pl.BlockSpec((8, width), lambda h, r: (0, 0)),
+            pl.BlockSpec((8, width), flat),
+            ANY,
+            FULL,
+            FULL,
+            pl.BlockSpec((8, width), flat),
         ],
-        out_specs=(
-            pl.BlockSpec((1, 2, 4, GROUP, 48, width), lambda h, r: (h, 0, 0, 0, 0, 0)),
-            pl.BlockSpec((2, 4, 8, 256), lambda h, r: (0, 0, 0, 0)),
-            pl.BlockSpec((1, slots, width), lambda h, r: (jnp.where(h == 2, r, 0), 0, 0)),
-        ),
+        out_specs=(FULL, ANY, FULL, FULL),
         scratch_shapes=[
             pltpu.VMEM((width, width), f32),
             pltpu.VMEM((width, slots), f32),
@@ -697,152 +899,19 @@
             pltpu.VMEM((GROUP, slots, 256), f32),
             pltpu.VMEM((width, 256), f32),
             pltpu.VMEM((8, width), f32),
-        ],
-        compiler_params=pltpu.CompilerParams(vmem_limit_bytes=VMEM_LIMIT),
-    )(wf, ws, wv, normed, values, hid, slope, prob, gmix, lt, gg2)
-
-
-def add_into(total, more, count):
-    def one(i, carry):
-        total[i] = (total[i].astype(f32) + more[i].astype(f32)).astype(bf16)
-        return carry
-
-    lax.fori_loop(0, count, one, 0)
-
-
-def reduce_kernel(
-    gf, ga, gs, gn, tokens, gmid, small, out_f, out_a, out_s, gtok,
-    fs, fb1, fb2, fb3, fb4, asum, ab1, ab2, ss, sb1, sb2, nb, own, s1, r1, s2, r2, s3, r3, sn, rn, sf, rf, sv, rv,
-):
-    t, c, z = place()
-    sibling = (t, 1 - c, z)
-    tps, zs = group_peers(), line_peers()
-    greet([(p, c, z) for p in tps] + [(t, c, p) for p in zs] + [sibling])
-    y, x = t // 2, t % 2
-    slow, fast = (1 - c) * y + c * x, (1 - c) * x + c * y
-    fast_peer = (1 - c) * tps[0] + c * tps[1]
-    slow_peer = (1 - c) * tps[1] + c * tps[0]
-    heads = ga.shape[0]
-    one = [remote(ga.at[h, 1 - c], ab1.at[h], s1.at[h], r1.at[h], sibling) for h in range(heads)]
-    v1 = remote(gs.at[1 - c], sb1, sv.at[0], rv.at[0], sibling)
-    f1 = remote(gf.at[1 - c], fb1, sf.at[0], rf.at[0], sibling)
-    mine = [local(ga.at[h, c], asum.at[h], own.at[h]) for h in range(heads)]
-    mine_s = local(gs.at[c], ss, own.at[heads])
-    mine_f = local(gf.at[c], fs, own.at[heads + 1])
-    mine_n = local(gn.at[t], nb.at[3], own.at[heads + 2])
-    parts = [remote(gn.at[p], nb.at[k], sn.at[k], rn.at[k], (p, c, z)) for k, p in enumerate(tps)]
-    two = []
-    for h in range(heads):
-        mine[h].wait()
-        one[h].wait()
-
-        def line(i, carry):
-            add_into(asum.at[h, i], ab1.at[h, i], GROUP)
-            return carry
-
-        lax.fori_loop(0, 4, line, 0)
-        two.append(
-            [remote(asum.at[h, p], ab2.at[h, k], s2.at[h, k], r2.at[h, k], (t, c, p)) for k, p in enumerate(zs)]
-        )
-        if h == 0:
-            mine_s.wait()
-            v1.wait()
-            ss[...] += sb1[...]
-            v2 = [remote(ss.at[p], sb2.at[k], sv.at[1 + k], rv.at[1 + k], (t, c, p)) for k, p in enumerate(zs)]
-    mine_f.wait()
-    f1.wait()
-
-    for which in (1 - slow, slow):
-        for j in range(2):
-            add_into(fs.at[which, j], fb1.at[which, j], 4)
-        if which is not slow:
-            f2 = remote(fs.at[1 - slow], fb2, sf.at[1], rf.at[1], (slow_peer, c, z))
-    mine_n.wait()
-    for copy in parts:
-        copy.wait()
-
-    def ln_back(i, carry):
-        at = pl.ds(pl.multiple_of(i * 128, 128), 128)
-        g = nb[0, at, :].astype(f32) + nb[1, at, :].astype(f32) + nb[2, at, :].astype(f32) + nb[3, at, :].astype(f32)
-        unit, scale = centre_rows(tokens[at, :].astype(f32))
-        gu = g * small[3:4]
-        back = scale * (
-            gu - jnp.mean(gu, axis=-1, keepdims=True) - unit * jnp.mean(gu * unit, axis=-1, keepdims=True)
-        )
-        gtok[at, :] = gmid[at, :] + back
-        return carry
-
-    lax.fori_loop(0, 4, ln_back, 0)
-    f2.wait()
-    for which in (1 - fast, fast):
-        add_into(fs.at[slow, which], fb2.at[which], 4)
-        if which is not fast:
-            f3 = remote(fs.at[slow, 1 - fast], fb3, sf.at[2], rf.at[2], (fast_peer, c, z))
-    f3.wait()
-    add_into(fs.at[slow, fast], fb3, 4)
-    f4 = [
-        remote(fs.at[slow, fast, p], fb4.at[k], sf.at[3 + k], rf.at[3 + k], (t, c, p)) for k, p in enumerate(zs)
-    ]
-    three, mine_a = [], []
-    for h in range(heads):
-        for copy in two[h]:
-            copy.wait()
-
-        def fold(i, carry):
-            total = asum[h, z, i].astype(f32)
-            for k in range(3):
-                total = total + ab2[h, k, i].astype(f32)
-            asum[h, z, i] = total.astype(bf16)
-            return carry
-
-        lax.fori_loop(0, GROUP, fold, 0)
-        mine_a.append(local(asum.at[h, z, t], out_a.at[h, t], own.at[h]))
-        three.append(
-            [remote(asum.at[h, z, p], out_a.at[h, t], s3.at[h, k], r3.at[h, k], (p, c, z)) for k, p in enumerate(tps)]
-        )
-    for copy in v2:
-        copy.wait()
-    out_s[...] = ss[z] + sb2[0] + sb2[1] + sb2[2]
-    for copy in f4:
-        copy.wait()
-    total = fs[slow, fast, z].astype(f32)
-    for k in range(3):
-        total = total + fb4[k].astype(f32)
-    out_f[...] = total
-    for copy in mine_a:
-        copy.wait()
-    for copies in three:
-        for copy in copies:
-            copy.wait()
-
-
-def reduce_call(gf, ga, gs, gn, tokens, gmid, small):
-    heads, width = ga.shape[0], ga.shape[-1]
-    rows = gf.shape[-2]
-    return pl.pallas_call(
-        reduce_kernel,
-        out_shape=(
-            shape_of((rows, width), f32),
-            shape_of((heads, GROUP, 48, width), bf16),
-            shape_of((8, 256), f32),
-            shape_of(tokens.shape, f32),
-        ),
-        in_specs=[ANY] * 4 + [FULL] * 3,
-        out_specs=(FULL, ANY, FULL, FULL),
-        scratch_shapes=[
-            pltpu.VMEM((2, 2, 4, rows, width), bf16),
-            pltpu.VMEM((2, 2, 4, rows, width), bf16),
+            pltpu.VMEM((heads, 2, 4, GROUP, 48, width), bf16),
+            pltpu.VMEM((2, 4, 8, 256), f32),
+            pltpu.VMEM((3, slots, width), bf16),
+            pltpu.VMEM((3, slots, width), bf16),
+            pltpu.VMEM((2, 4, rows, width), bf16),
             pltpu.VMEM((2, 4, rows, width), bf16),
             pltpu.VMEM((4, rows, width), bf16),
             pltpu.VMEM((3, rows, width), bf16),
             pltpu.VMEM((heads, 4, GROUP, 48, width), bf16),
-            pltpu.VMEM((heads, 4, GROUP, 48, width), bf16),
             pltpu.VMEM((heads, 3, GROUP, 48, width), bf16),
             pltpu.VMEM((4, 8, 256), f32),
-            pltpu.VMEM((4, 8, 256), f32),
             pltpu.VMEM((3, 8, 256), f32),
-            pltpu.VMEM((4,) + tokens.shape, bf16),
-            DMA((heads + 3,)),
+            DMA((heads + 1,)),
             DMA((heads,)),
             DMA((heads,)),
             DMA((heads, 3)),
@@ -851,13 +920,13 @@
             DMA((heads, 3)),
             DMA((3,)),
             DMA((3,)),
-            DMA((6,)),
-            DMA((6,)),
+            DMA((5,)),
+            DMA((5,)),
             DMA((4,)),
             DMA((4,)),
         ],
-        compiler_params=pltpu.CompilerParams(collective_id=4, has_side_effects=True, vmem_limit_bytes=VMEM_LIMIT),
-    )(gf, ga, gs, gn, tokens, gmid, small)
+        compiler_params=pltpu.CompilerParams(collective_id=3, has_side_effects=True, vmem_limit_bytes=VMEM_LIMIT),
+    )(wf, ws, wv, normed, values, hid, slope, prob, gmix, gg2, half, tokens, gmid, small)
 
 
 def pack_inputs(tokens, lengths, gain_one, w_value, w_first, b_first, w_second, b_second, w_out, gain_two, w_up, w_down):
@@ -869,13 +938,13 @@
         [
             b_first.reshape(GROUP, heads, depth).transpose(0, 2, 1),
             jnp.broadcast_to(jnp.stack([gain_one, gain_two], 1), (GROUP, depth, 2)),
-            jnp.zeros((GROUP, depth, 59), bf16),
+            jnp.broadcast_to(b_second.reshape(depth, 8), (GROUP, depth, 8)),
+            jnp.zeros((GROUP, depth, 51), bf16),
         ],
         2,
     )
     head_zero = jnp.concatenate([w_value.reshape(depth, GROUP, -1).transpose(1, 0, 2), cols], 2)
-    head_one = jnp.broadcast_to(jnp.pad(b_second[None, :], ((0, depth - 1), (0, 256 - b_second.shape[0]))), head_zero.shape)
-    extra = jnp.stack([head_zero, head_one, jnp.zeros_like(head_zero)], 1)
+    extra = jnp.pad(head_zero[:, None], ((0, 0), (0, heads - 1), (0, 0), (0, 0)))
     low = jnp.concatenate([split(w_second), extra], 3)
     pa = jnp.concatenate([split(w_first), low], 2)
     spot = lax.broadcasted_iota(jnp.int32, (16, width), 1)
@@ -890,18 +959,14 @@
     _, slots, width = tokens.shape
     heads_all, depth, _ = w_first.shape
     heads = heads_all // GROUP
-    me = lax.axis_index("tp")
     pa, pt, pf = pack_inputs(
         tokens, lengths, gain_one, w_value, w_first, b_first, w_second, b_second, w_out, gain_two, w_up, w_down
     )
-    la, lt, lf = gather_call(pa, pt, pf)
-    b2 = lax.dynamic_index_in_dim(la[1, :, :, :, 24, 512:704], me, 2, False).reshape(heads, slots).astype(f32)
-    wf, ws, wv, small, normed, values, hid, slope, prob, join = attend_call(la, lt, b2)
-    joined = trade_call(join, 2)
-    result, gmid, gj, gf, gg2 = ffn_call(lf, joined, tokens[0], small, grad_out[0])
-    gmix = trade_call(gj, 3)
-    ga, gs, gn = back_call(wf, ws, wv, normed, values, hid, slope, prob, gmix, lt, gg2)
-    out_f, out_a, out_s, gtok = reduce_call(gf, ga, gs, gn, tokens[0], gmid, small)
+    wf, ws, wv, small, normed, values, hid, slope, prob, joined, lf = attend_call(pa, pt, pf)
+    result, gmid, gmix, half, gg2 = ffn_call(lf, joined, tokens[0], small, grad_out[0])
+    out_f, out_a, out_s, gtok = back_call(
+        wf, ws, wv, normed, values, hid, slope, prob, gmix, gg2, half, tokens[0], gmid, small
+    )
     low = out_a[:, :, 24:].astype(f32)
     to_all = lambda v: v.transpose((1, 0) + tuple(range(2, v.ndim))).reshape((heads_all,) + v.shape[2:])
     gb1 = to_all(low[:, :, :, 704])

time: 420 us -> 365 us (0.87)
  Pallas kernels: 391 us -> 341 us
    pallas_call x5 -> x1, Pallas kernels: 323 us -> 144 us  [back_call(): pl.pallas_call(back_kernel, grid=(heads, GROUP), out_shape=(shape_of((row...]
    pallas_call x1, Pallas kernels: 36.6 us -> 152 us  [attend_call(): pl.pallas_call(attend_kernel, grid=(heads, GROUP), out_shape=(shape_of((h...]
    pallas_call x1, Pallas kernels: 31.5 us -> 44.2 us  [ffn_call(): pl.pallas_call(ffn_kernel, out_shape=(shape_of((slots, width), f32), shap...]
where the time goes in v3:
time: 365 us; the launch traced here: 364 us
  Pallas kernels  341 us (93%)
  local copies, waits for them, and re-layouts  19.4 us (5%)
    pallas_call x1, Pallas kernels, attend_call(): pl.pallas_call(attend_kernel, grid=(heads, GROUP), out_shape=(shape_of((h...  152 us
    pallas_call x1, Pallas kernels, back_call(): pl.pallas_call(back_kernel, grid=(heads, GROUP), out_shape=(shape_of((row...  144 us
    pallas_call x1, Pallas kernels, ffn_call(): pl.pallas_call(ffn_kernel, out_shape=(shape_of((slots, width), f32), shap...  44.2 us

profile of v3, /device:TPU:0, one launch (start us, length us, event | category | flops | bytes accessed | tf_op | source)
XLA Modules:
  0.0 364.4 jit_solution(5234566337162783253)
XLA Ops:
  0.6 0.0 copy-start.4
  0.7 0.0 copy-start
  0.7 0.0 copy-start.6
  1.4 0.7 pad_maximum_fusion.1
  2.1 0.7 reshape.63
  2.8 0.1 copy.45
  2.9 0.7 reshape.64
  3.7 0.1 copy.44
  3.8 0.9 reshape.62
  4.7 0.1 concatenate.15
  4.8 0.8 slice_dynamic-update-slice_fusion.3
  5.6 0.8 slice_dynamic-update-slice_fusion.2
  6.4 0.8 slice_dynamic-update-slice_fusion.1
  7.2 0.8 slice_dynamic-update-slice_fusion
  7.9 0.8 constant_dynamic-update-slice_fusion.2
  8.7 0.9 constant_dynamic-update-slice_fusion.pf
  9.6 0.0 copy-done
  9.6 0.0 copy-start.5
  9.7 1.0 pad_maximum_fusion.pt
  10.6 0.0 copy-done.4
  10.6 0.0 copy-done.6
  10.6 1.0 fusion.4.pa
  11.6 0.0 copy-done.5
  11.6 152.1 %shard_map.220 = (bf16[3,768,768]{2,1,0:T(8,128)(2,1)}, bf16[3,768,512]{2,1,0:T(8,128)(2,1)}, bf16[768,256]{1,0:T(8,128)(2,1)}, f32[8,768]{1,0:T(8,128)}, bf16[4...) custom-call(bf16[4,3,48,768]{3,2,1,0:T(8,128)(2,1)} %fusion.4.pa, ...), custom_call_target="tpu_custom_call" | custom-call | tf_op jit(solution)/shard_map/pallas_call | solution.py:424
  163.7 44.2 %shard_map.221 = (f32[512,768]{1,0:T(8,128)}, f32[512,768]{1,0:T(8,128)}, bf16[4,512,256]{2,1,0:T(8,128)(2,1)}, bf16[2,2,4,224,768]{4,3,2,1,0:T(8,128)(2,1)}, f32[8,768]{1,0:T(8,128)}) custom-call(bf16[2,2,2,4,224,768]{5,4,3,2,1,0:T(8,128)(2,1)} %get-tuple-element.32.lf, bf16[4,512,256]{2,1,0:T(8,128)(2,1)} %get-tuple-element.33.joined, ...), custom_call_target="tpu_custom_call" | custom-call | tf_op jit(solution)/shard_map/pallas_call | solution.py:597
  207.9 144.3 %shard_map.222 = (f32[224,768]{1,0:T(8,128)}, bf16[3,4,48,768]{3,2,1,0:T(8,128)(2,1)}, f32[8,256]{1,0:T(8,128)}, f32[512,768]{1,0:T(8,128)}) custom-call(bf16[3,768,768]{2,1,0:T(8,128)(2,1)} %get-tuple-element.36.wf, bf16[3,768,512]{2,1,0:T(8,128)(2,1)} %get-tuple-element.37.ws, bf16[768,256]{1,0:T(8,128)(2,1)} %get-tuple-element.38.wv, ...), custom_call_target="tpu_custom_call" | custom-call | tf_op jit(solution)/shard_map/pallas_call | solution.py:867
  352.2 0.0 copy-start.3
  352.3 1.3 slice.59
  353.6 1.5 slice.60
  355.1 1.8 fusion.5
  356.9 0.7 copy.51
  357.6 0.0 copy-done.3
  357.7 0.2 convert_bitcast_fusion
  357.8 1.0 copy.47
  358.8 0.0 copy-start.1
  358.8 0.2 slice_reduce_fusion
  359.0 0.6 reshape.68
  359.6 0.1 slice_reduce_fusion.1
  359.7 0.7 slice_reduce_fusion.2
  360.4 0.1 slice_bitcast_fusion
  360.5 0.9 copy.49
  361.3 0.0 copy-start.2
  361.4 0.7 reshape.65
  362.1 0.0 copy-done.1
  362.1 1.1 copy.63
  363.3 0.0 copy-done.2
  363.3 1.1 copy.64
  (10 shorter events, 0.1 us)
Async XLA Ops:
  0.6 10.0 %copy-start.4 = (bf16[12,24,768]{2,1,0:T(8,128)(2,1)S(1)}, bf16[12,24,768]{2,1,0:T(8,128)(2,1)}, u32[]{:S(2)}) copy-start(bf16[12,24,768]{2,1,0:T(8,128)(2,1)} %param.17) | copy-start | bytes 1327108
  0.7 9.0 %copy-start = (bf16[1,512,768]{2,1,0:T(8,128)(2,1)S(1)}, bf16[1,512,768]{2,1,0:T(8,128)(2,1)}, u32[]{:S(2)}) copy-start(bf16[1,512,768]{2,1,0:T(8,128)(2,1)} %param.13) | copy-start | bytes 2359300
  0.7 10.0 %copy-start.6 = (bf16[12,24,512]{2,1,0:T(8,128)(2,1)S(1)}, bf16[12,24,512]{2,1,0:T(8,128)(2,1)}, u32[]{:S(2)}) copy-start(bf16[12,24,512]{2,1,0:T(8,128)(2,1)} %param.19) | copy-start | bytes 884740
  9.6 2.0 copy-start.5
  352.2 5.4 %copy-start.3 = (bf16[3,4,48,768]{3,2,1,0:T(8,128)(2,1)S(1)}, bf16[3,4,48,768]{3,2,1,0:T(8,128)(2,1)}, u32[]{:S(2)}) copy-start(bf16[3,4,48,768]{3,2,1,0:T(8,128)(2,1)} %get-tuple-element.49) | copy-start | bytes 2654212
  358.8 3.3 copy-start.1
  361.3 1.9 copy-start.2

commit v4 on v3

--- a/solution.py
+++ b/solution.py
@@ -208,6 +208,101 @@
     return [(z + k) % 4 for k in (1, 2, 3)]
 
 
+def line_place():
+    z = lax.axis_index("narrow")
+    side = z // 2
+    end, inner = 3 * side, 1 + side
+    return end, inner, 2 - side, 3 - 3 * side, end + inner - z, z == inner
+
+
+class Spread:
+    def __init__(self, slabs, send, recv):
+        t, c, z = place()
+        end, inner, other, far, near, is_inner = line_place()
+        self.is_inner = is_inner
+        move = lambda o, k, to: remote(slabs(o), slabs(o), send.at[k], recv.at[o], (t, c, to))
+        self.own = lambda: [move(z, 0, other), move(z, 1, near)]
+        self.on = lambda: [move(other, 2, end), move(far, 3, end)]
+        self.near = lambda: move(near, 0, near)
+
+    def begin(self):
+        start(self.own())
+
+    def forward(self):
+        @pl.when(self.is_inner)
+        def _():
+            for copy in self.on():
+                copy.wait_recv()
+            start(self.on())
+
+    def finish(self):
+        self.near().wait_recv()
+
+        @pl.when(jnp.logical_not(self.is_inner))
+        def _():
+            for copy in self.on():
+                copy.wait_recv()
+
+        for copy in self.own():
+            copy.wait_send()
+
+        @pl.when(self.is_inner)
+        def _():
+            for copy in self.on():
+                copy.wait_send()
+
+
+class Gather:
+    def __init__(self, slabs, land, add, send, recv):
+        t, c, z = place()
+        end, inner, other, far, near, is_inner = line_place()
+        self.is_inner, self.add, self.z = is_inner, add, z
+        self.other, self.far = other, far
+        move = lambda o, slot, k, to: remote(slabs(o), land(slot), send.at[k], recv.at[slot], (t, c, to))
+        self.out = lambda: [move(far, 2, 0, inner), move(other, 1, 1, inner), move(inner, 0, 2, inner)]
+        self.back = lambda: [move(end, 0, 2, end)]
+        self.on_far = lambda: [move(far, 1, 0, far)]
+        self.on_other = lambda: [move(other, 3, 1, other)]
+        self.got = lambda slot: move(z, slot, 0, near).wait_recv()
+
+    def begin(self):
+        @pl.when(self.is_inner)
+        def _():
+            start(self.back())
+
+        @pl.when(jnp.logical_not(self.is_inner))
+        def _():
+            start(self.out())
+
+    def forward(self):
+        @pl.when(self.is_inner)
+        def _():
+            self.got(2)
+            self.add(self.far, 2)
+            start(self.on_far())
+            self.got(1)
+            self.add(self.other, 1)
+            start(self.on_other())
+
+    def finish(self):
+        self.got(0)
+        self.add(self.z, 0)
+
+        @pl.when(self.is_inner)
+        def _():
+            self.got(3)
+            self.add(self.z, 3)
+            for copy in self.back() + self.on_far() + self.on_other():
+                copy.wait_send()
+
+        @pl.when(jnp.logical_not(self.is_inner))
+        def _():
+            self.got(1)
+            self.add(self.z, 1)
+            for copy in self.out():
+                copy.wait_send()
+
+
 def greet(devices):
     barrier = pltpu.get_barrier_semaphore()
     for device in devices:
@@ -258,7 +353,7 @@
 
 def attend_kernel(
     pa, pt, pf, wf, ws, wv, small, normed, values, hid, slope, prob, joined, lf,
-    la, lt, nrm, val, cols, b2, join, own, s1, r1, s2, r2, s3, r3, st, rt, sf, rf, sj, rj,
+    la, lt, nrm, val, cols, b2, join, own, s1, r1, s2, r2, s3, r3, st, rt, s1f, r1f, sf, rf, sj, rj,
 ):
     h, r = pl.program_id(0), pl.program_id(1)
     width = wf.shape[-1]
@@ -271,20 +366,18 @@
     a1 = lambda i: [
         remote(pa.at[p, i], la.at[i, c, z, t], s1.at[i, k], r1.at[i, k], (p, c, z)) for k, p in enumerate(tps)
     ]
-    a2 = lambda i: [
-        remote(la.at[i, c, z], la.at[i, c, z], s2.at[i, k], r2.at[i, k], (t, c, p)) for k, p in enumerate(zs)
-    ]
+    a2 = lambda i: Spread(lambda o: la.at[i, c, o], s2.at[i], r2.at[i])
     a3 = lambda i: [remote(la.at[i, c], la.at[i, c], s3.at[i], r3.at[i], sibling)]
     mine = lambda i: [local(pa.at[t, i], la.at[i, c, z, t], own.at[i])]
     mine_t = lambda: [local(pt, lt.at[3], own.at[heads])]
     mine_f = lambda: [local(pf, lf.at[c, slow, fast, z], own.at[heads + 1])]
     mine_j = lambda: [local(join.at[3], joined.at[t], own.at[heads + 2])]
     toks = lambda: [remote(pt, lt.at[k], st.at[k], rt.at[k], (p, c, z)) for k, p in enumerate(tps)]
-    f1 = lambda: [remote(pf, lf.at[c, slow, fast, z], sf.at[k], rf.at[k], (t, c, p)) for k, p in enumerate(zs)]
-    f2 = lambda: [remote(lf.at[c, slow, fast], lf.at[c, slow, fast], sf.at[3], rf.at[3], fast_dev)]
-    f3 = lambda: [remote(lf.at[c, slow], lf.at[c, slow], sf.at[4], rf.at[4], slow_dev)]
-    f4 = lambda: [remote(lf.at[c, slow], lf.at[c, slow], sf.at[5], rf.at[5], sibling)]
-    f5 = lambda: [remote(lf.at[c, 1 - slow], lf.at[c, 1 - slow], sf.at[6], rf.at[6], sibling)]
+    f1 = lambda: Spread(lambda o: lf.at[c, slow, fast, o], s1f, r1f)
+    f2 = lambda: [remote(lf.at[c, slow, fast], lf.at[c, slow, fast], sf.at[0], rf.at[0], fast_dev)]
+    f3 = lambda: [remote(lf.at[c, slow], lf.at[c, slow], sf.at[1], rf.at[1], slow_dev)]
+    f4 = lambda: [remote(lf.at[c, slow], lf.at[c, slow], sf.at[2], rf.at[2], sibling)]
+    f5 = lambda: [remote(lf.at[c, 1 - slow], lf.at[c, 1 - slow], sf.at[3], rf.at[3], sibling)]
     out_j = lambda k: [remote(join.at[k], joined.at[t], sj.at[k], rj.at[k], (tps[k], c, z))]
 
     def at_step(i, j):
@@ -293,25 +386,32 @@
     @at_step(0, 0)
     def _():
         greet([(p, c, z) for p in tps] + [(t, c, p) for p in zs] + [sibling])
+        start(mine_f())
         for i in range(heads):
             start(mine(i) + a1(i))
-        start(mine_f() + f1() + mine_t() + toks())
+        start(mine_t())
+        wait(mine_f())
+        f1().begin()
+        start(toks())
         for i in range(heads):
             wait(mine(i) + a1(i))
-            start(a2(i))
-        wait(a2(0))
+        a2(0).begin()
+        f1().forward()
+        a2(1).begin()
+        f1().finish()
+        start(f2())
+        a2(0).forward()
+        a2(0).finish()
         start(a3(0))
+        a2(1).forward()
+        a2(2).begin()
         wait(mine_t() + toks() + a3(0))
 
-    @at_step(0, 1)
-    def _():
-        wait(mine_f() + f1())
-        start(f2())
-
     @at_step(1, 0)
     def _():
-        wait(a2(1))
+        a2(1).finish()
         start(a3(1))
+        a2(2).forward()
         wait(a3(1))
 
     @at_step(1, 1)
@@ -321,7 +421,7 @@
 
     @at_step(2, 0)
     def _():
-        wait(a2(2))
+        a2(2).finish()
         start(a3(2))
         wait(a3(2))
 
@@ -462,14 +562,16 @@
             DMA((heads + 3,)),
             DMA((heads, 3)),
             DMA((heads, 3)),
-            DMA((heads, 3)),
-            DMA((heads, 3)),
+            DMA((heads, 4)),
+            DMA((heads, 4)),
             DMA((heads,)),
             DMA((heads,)),
             DMA((3,)),
             DMA((3,)),
-            DMA((7,)),
-            DMA((7,)),
+            DMA((4,)),
+            DMA((4,)),
+            DMA((4,)),
+            DMA((4,)),
             DMA((3,)),
             DMA((3,)),
         ],
@@ -628,7 +730,7 @@
 def back_kernel(
     wf, ws, wv, normed, values, hid, slope, prob, gmix, gg2, half, tokens, gmid, small, out_f, out_a, out_s, gtok,
     awf, aws, ab1, ab2, gn, gv, awv, ag1, ga, gs, gnb, nb, fs, fb2, fb3, fb4, cb1, cb2, sb1, sb2,
-    own, s1, r1, s2, r2, s3, r3, sn, rn, sf, rf, sv, rv,
+    own, s1, r1, s2, r2, s3, r3, sn, rn, sf, rf, s4, r4, sv, rv,
 ):
     h, r = pl.program_id(0), pl.program_id(1)
     width = wf.shape[-1]
@@ -639,9 +741,20 @@
     slow, fast, slow_dev, fast_dev = square()
 
     a1 = lambda i: [remote(ga.at[i, 1 - c], cb1.at[i], s1.at[i], r1.at[i], sibling)]
-    a2 = lambda i: [
-        remote(ga.at[i, c, p], cb2.at[i, k], s2.at[i, k], r2.at[i, k], (t, c, p)) for k, p in enumerate(zs)
-    ]
+    def add_heads(i):
+        def add(o, slot):
+            def one(j, carry):
+                ga[i, c, o, j] = (ga[i, c, o, j].astype(f32) + cb2[i, slot, j].astype(f32)).astype(bf16)
+                return carry
+
+            lax.fori_loop(0, GROUP, one, 0)
+
+        return add
+
+    def add_f(o, slot):
+        fs[fast, o] = (fs[fast, o].astype(f32) + fb4[slot].astype(f32)).astype(bf16)
+
+    a2 = lambda i: Gather(lambda o: ga.at[i, c, o], lambda k: cb2.at[i, k], add_heads(i), s2.at[i], r2.at[i])
     a3 = lambda i: [
         remote(ga.at[i, c, z, p], out_a.at[i, t], s3.at[i, k], r3.at[i, k], (p, c, z)) for k, p in enumerate(tps)
     ]
@@ -651,9 +764,7 @@
     v2 = lambda: [remote(gs.at[c, p], sb2.at[k], sv.at[1 + k], rv.at[1 + k], (t, c, p)) for k, p in enumerate(zs)]
     f2 = lambda: [remote(half.at[1 - slow], fb2, sf.at[0], rf.at[0], slow_dev)]
     f3 = lambda: [remote(fs.at[1 - fast], fb3, sf.at[1], rf.at[1], fast_dev)]
-    f4 = lambda: [
-        remote(fs.at[fast, p], fb4.at[k], sf.at[2 + k], rf.at[2 + k], (t, c, p)) for k, p in enumerate(zs)
-    ]
+    f4 = lambda: Gather(lambda o: fs.at[fast, o], lambda k: fb4.at[k], add_f, s4, r4)
     out_n = lambda k: [remote(gnb.at[k], nb.at[k], sn.at[k], rn.at[k], (tps[k], c, z))]
 
     def at_step(i, j):
@@ -668,19 +779,10 @@
             return carry
 
         lax.fori_loop(0, 4, line, 0)
-        start(a2(i))
+        a2(i).begin()
 
     def deal(i):
-        wait(a2(i))
-
-        def fold(j, carry):
-            total = ga[i, c, z, j].astype(f32)
-            for k in range(3):
-                total = total + cb2[i, k, j].astype(f32)
-            ga[i, c, z, j] = total.astype(bf16)
-            return carry
-
-        lax.fori_loop(0, GROUP, fold, 0)
+        a2(i).finish()
         start(mine(i) + a3(i))
 
     def add_slabs(total, more):
@@ -706,15 +808,27 @@
         start(f3())
         add_slabs(fast, fb2.at[fast])
 
+    @at_step(1, 2)
+    def _():
+        a2(0).forward()
+
     @at_step(2, 0)
     def _():
         meet(1)
+
+    @at_step(2, 1)
+    def _():
+        deal(0)
+
+    @at_step(2, 2)
+    def _():
+        a2(1).forward()
 
     @at_step(2, 3)
     def _():
         wait(f3())
         add_slabs(fast, fb3)
-        start(f4())
+        f4().begin()
 
     @pl.when(r == 0)
     def _():
@@ -828,9 +942,10 @@
         wait(v1())
         gs[c] += sb1[...]
         start(v2())
-        deal(0)
+        f4().forward()
         for k in range(3):
             wait(out_n(k))
+        a2(2).forward()
 
         def ln_back(i, carry):
             at = pl.ds(pl.multiple_of(i * 128, 128), 128)
@@ -845,11 +960,8 @@
 
         lax.fori_loop(0, 4, ln_back, 0)
         deal(1)
-        wait(f4())
-        total = fs[fast, z].astype(f32)
-        for k in range(3):
-            total = total + fb4[k].astype(f32)
-        out_f[...] = total
+        f4().finish()
+        out_f[...] = fs[fast, z].astype(f32)
         wait(v2())
         out_s[...] = gs[c, z] + sb2[0] + sb2[1] + sb2[2]
         deal(2)
@@ -906,22 +1018,24 @@
             pltpu.VMEM((2, 4, rows, width), bf16),
             pltpu.VMEM((2, 4, rows, width), bf16),
             pltpu.VMEM((4, rows, width), bf16),
-            pltpu.VMEM((3, rows, width), bf16),
+            pltpu.VMEM((4, rows, width), bf16),
             pltpu.VMEM((heads, 4, GROUP, 48, width), bf16),
-            pltpu.VMEM((heads, 3, GROUP, 48, width), bf16),
+            pltpu.VMEM((heads, 4, GROUP, 48, width), bf16),
             pltpu.VMEM((4, 8, 256), f32),
             pltpu.VMEM((3, 8, 256), f32),
             DMA((heads + 1,)),
             DMA((heads,)),
             DMA((heads,)),
             DMA((heads, 3)),
-            DMA((heads, 3)),
+            DMA((heads, 4)),
             DMA((heads, 3)),
             DMA((heads, 3)),
             DMA((3,)),
             DMA((3,)),
-            DMA((5,)),
-            DMA((5,)),
+            DMA((2,)),
+            DMA((2,)),
+            DMA((3,)),
+            DMA((4,)),
             DMA((4,)),
             DMA((4,)),
         ],

time: 365 us -> 323 us (0.88)
  Pallas kernels: 341 us -> 299 us
    pallas_call x1, Pallas kernels: 144 us -> 116 us  [back_call(): pl.pallas_call(back_kernel, grid=(heads, GROUP), out_shape=(shape_of((row...]
    pallas_call x1, Pallas kernels: 152 us -> 139 us  [attend_call(): pl.pallas_call(attend_kernel, grid=(heads, GROUP), out_shape=(shape_of((h...]
where the time goes in v4:
time: 323 us
  Pallas kernels  299 us (93%)
  local copies, waits for them, and re-layouts  19.4 us (6%)
    pallas_call x1, Pallas kernels, attend_call(): pl.pallas_call(attend_kernel, grid=(heads, GROUP), out_shape=(shape_of((h...  139 us
    pallas_call x1, Pallas kernels, back_call(): pl.pallas_call(back_kernel, grid=(heads, GROUP), out_shape=(shape_of((row...  116 us
    pallas_call x1, Pallas kernels, ffn_call(): pl.pallas_call(ffn_kernel, out_shape=(shape_of((slots, width), f32), shap...  44.2 us

profile of v4, /device:TPU:0, one launch (start us, length us, event | category | flops | bytes accessed | tf_op | source)
XLA Modules:
  0.0 322.7 jit_solution(8891911446085381326)
XLA Ops:
  0.6 0.0 copy-start.4
  0.7 0.0 copy-start
  0.7 0.0 copy-start.6
  1.4 0.7 pad_maximum_fusion.1
  2.1 0.7 reshape.63
  2.8 0.1 copy.45
  2.9 0.7 reshape.64
  3.7 0.1 copy.44
  3.8 0.9 reshape.62
  4.7 0.1 concatenate.15
  4.8 0.8 slice_dynamic-update-slice_fusion.3
  5.6 0.8 slice_dynamic-update-slice_fusion.2
  6.4 0.8 slice_dynamic-update-slice_fusion.1
  7.2 0.8 slice_dynamic-update-slice_fusion
  7.9 0.8 constant_dynamic-update-slice_fusion.2
  8.7 0.9 constant_dynamic-update-slice_fusion.pf
  9.6 0.0 copy-done
  9.6 0.0 copy-start.5
  9.7 1.0 pad_maximum_fusion.pt
  10.6 0.0 copy-done.4
  10.6 0.0 copy-done.6
  10.6 1.0 fusion.4.pa
  11.6 0.0 copy-done.5
  11.6 138.9 %shard_map.220 = (bf16[3,768,768]{2,1,0:T(8,128)(2,1)}, bf16[3,768,512]{2,1,0:T(8,128)(2,1)}, bf16[768,256]{1,0:T(8,128)(2,1)}, f32[8,768]{1,0:T(8,128)}, bf16[4...) custom-call(bf16[4,3,48,768]{3,2,1,0:T(8,128)(2,1)} %fusion.4.pa, ...), custom_call_target="tpu_custom_call" | custom-call | tf_op jit(solution)/shard_map/pallas_call | solution.py:524
  150.5 44.2 %shard_map.221 = (f32[512,768]{1,0:T(8,128)}, f32[512,768]{1,0:T(8,128)}, bf16[4,512,256]{2,1,0:T(8,128)(2,1)}, bf16[2,2,4,224,768]{4,3,2,1,0:T(8,128)(2,1)}, f32[8,768]{1,0:T(8,128)}) custom-call(bf16[2,2,2,4,224,768]{5,4,3,2,1,0:T(8,128)(2,1)} %get-tuple-element.32.lf, bf16[4,512,256]{2,1,0:T(8,128)(2,1)} %get-tuple-element.33.joined, ...), custom_call_target="tpu_custom_call" | custom-call | tf_op jit(solution)/shard_map/pallas_call | solution.py:699
  194.8 115.8 %shard_map.222 = (f32[224,768]{1,0:T(8,128)}, bf16[3,4,48,768]{3,2,1,0:T(8,128)(2,1)}, f32[8,256]{1,0:T(8,128)}, f32[512,768]{1,0:T(8,128)}) custom-call(bf16[3,768,768]{2,1,0:T(8,128)(2,1)} %get-tuple-element.36.wf, bf16[3,768,512]{2,1,0:T(8,128)(2,1)} %get-tuple-element.37.ws, bf16[768,256]{1,0:T(8,128)(2,1)} %get-tuple-element.38.wv, ...), custom_call_target="tpu_custom_call" | custom-call | tf_op jit(solution)/shard_map/pallas_call | solution.py:979
  310.5 0.0 copy-start.3
  310.6 1.3 slice.59
  311.9 1.5 slice.60
  313.4 1.8 fusion.5
  315.2 0.7 copy.51
  316.0 0.0 copy-done.3
  316.0 0.2 convert_bitcast_fusion
  316.1 1.0 copy.47
  317.1 0.0 copy-start.1
  317.1 0.2 slice_reduce_fusion
  317.3 0.6 reshape.68
  317.9 0.1 slice_reduce_fusion.1
  318.0 0.7 slice_reduce_fusion.2
  318.7 0.1 slice_bitcast_fusion
  318.8 0.9 copy.49
  319.6 0.0 copy-start.2
  319.7 0.7 reshape.65
  320.4 0.0 copy-done.1
  320.4 1.1 copy.63
  321.6 0.0 copy-done.2
  321.6 1.1 copy.64
  (10 shorter events, 0.1 us)
Async XLA Ops:
  0.6 10.0 %copy-start.4 = (bf16[12,24,768]{2,1,0:T(8,128)(2,1)S(1)}, bf16[12,24,768]{2,1,0:T(8,128)(2,1)}, u32[]{:S(2)}) copy-start(bf16[12,24,768]{2,1,0:T(8,128)(2,1)} %param.17) | copy-start | bytes 1327108
  0.7 9.0 %copy-start = (bf16[1,512,768]{2,1,0:T(8,128)(2,1)S(1)}, bf16[1,512,768]{2,1,0:T(8,128)(2,1)}, u32[]{:S(2)}) copy-start(bf16[1,512,768]{2,1,0:T(8,128)(2,1)} %param.13) | copy-start | bytes 2359300
  0.7 10.0 %copy-start.6 = (bf16[12,24,512]{2,1,0:T(8,128)(2,1)S(1)}, bf16[12,24,512]{2,1,0:T(8,128)(2,1)}, u32[]{:S(2)}) copy-start(bf16[12,24,512]{2,1,0:T(8,128)(2,1)} %param.19) | copy-start | bytes 884740
  9.6 2.0 copy-start.5
  310.5 5.4 %copy-start.3 = (bf16[3,4,48,768]{3,2,1,0:T(8,128)(2,1)S(1)}, bf16[3,4,48,768]{3,2,1,0:T(8,128)(2,1)}, u32[]{:S(2)}) copy-start(bf16[3,4,48,768]{3,2,1,0:T(8,128)(2,1)} %get-tuple-element.49) | copy-start | bytes 2654212
  317.1 3.3 %copy-start.1 = (f32[512,768]{1,0:T(8,128)S(1)}, f32[512,768]{1,0:T(8,128)}, u32[]{:S(2)}) copy-start(f32[512,768]{1,0:T(8,128)} %get-tuple-element.35) | copy-start | bytes 4718596
  319.6 1.9 copy-start.2

commit v5 on v4

--- a/solution.py
+++ b/solution.py
@@ -216,12 +216,14 @@
 
 
 class Spread:
-    def __init__(self, slabs, send, recv):
+    def __init__(self, slabs, send, recv, source=None):
         t, c, z = place()
         end, inner, other, far, near, is_inner = line_place()
         self.is_inner = is_inner
         move = lambda o, k, to: remote(slabs(o), slabs(o), send.at[k], recv.at[o], (t, c, to))
-        self.own = lambda: [move(z, 0, other), move(z, 1, near)]
+        source = slabs(z) if source is None else source
+        give = lambda k, to: remote(source, slabs(z), send.at[k], recv.at[z], (t, c, to))
+        self.own = lambda: [give(0, other), give(1, near)]
         self.on = lambda: [move(other, 2, end), move(far, 3, end)]
         self.near = lambda: move(near, 0, near)
 
@@ -307,7 +309,10 @@
     barrier = pltpu.get_barrier_semaphore()
     for device in devices:
         pl.semaphore_signal(barrier, inc=1, device_id=device, device_id_type=MESH)
-    pl.semaphore_wait(barrier, len(devices))
+
+
+def met(count):
+    pl.semaphore_wait(pltpu.get_barrier_semaphore(), count)
 
 
 def remote(src, dst, send, recv, device):
@@ -351,29 +356,38 @@
     return shifted * scale, scale
 
 
+ROWS = ((0, 144), (144, 272), (272, 384))
+
+
+def part(i):
+    return slice(*ROWS[i])
+
+
 def attend_kernel(
-    pa, pt, pf, wf, ws, wv, small, normed, values, hid, slope, prob, joined, lf,
-    la, lt, nrm, val, cols, b2, join, own, s1, r1, s2, r2, s3, r3, st, rt, s1f, r1f, sf, rf, sj, rj,
+    tokens, extra, w_first, w_second, w_out, w_up, w_down,
+    wf, ws, wv, small, normed, values, hid, slope, prob, joined, lf,
+    pa, pf, la, lt, nrm, val, cols, b2, masks, join, own, s1, r1, s2, r2, s3, r3, st, rt, s1f, r1f, sf, rf, sj, rj,
 ):
     h, r = pl.program_id(0), pl.program_id(1)
     width = wf.shape[-1]
-    heads = la.shape[0]
+    heads = w_first.shape[0] // GROUP
     t, c, z = place()
     sibling = (t, 1 - c, z)
     tps, zs = group_peers(), line_peers()
     slow, fast, slow_dev, fast_dev = square()
 
     a1 = lambda i: [
-        remote(pa.at[p, i], la.at[i, c, z, t], s1.at[i, k], r1.at[i, k], (p, c, z)) for k, p in enumerate(tps)
+        remote(pa.at[p, part(i)], la.at[c, z, t, part(i)], s1.at[i, k], r1.at[i, k], (p, c, z))
+        for k, p in enumerate(tps)
     ]
-    a2 = lambda i: Spread(lambda o: la.at[i, c, o], s2.at[i], r2.at[i])
-    a3 = lambda i: [remote(la.at[i, c], la.at[i, c], s3.at[i], r3.at[i], sibling)]
-    mine = lambda i: [local(pa.at[t, i], la.at[i, c, z, t], own.at[i])]
-    mine_t = lambda: [local(pt, lt.at[3], own.at[heads])]
+    a2 = lambda i: Spread(lambda o: la.at[c, o, :, part(i)], s2.at[i], r2.at[i])
+    a3 = lambda i: [remote(la.at[c, :, :, part(i)], la.at[c, :, :, part(i)], s3.at[i], r3.at[i], sibling)]
+    mine = lambda i: [local(pa.at[t, part(i)], la.at[c, z, t, part(i)], own.at[i])]
+    mine_t = lambda: [local(tokens.at[0], lt.at[3], own.at[heads])]
     mine_f = lambda: [local(pf, lf.at[c, slow, fast, z], own.at[heads + 1])]
     mine_j = lambda: [local(join.at[3], joined.at[t], own.at[heads + 2])]
-    toks = lambda: [remote(pt, lt.at[k], st.at[k], rt.at[k], (p, c, z)) for k, p in enumerate(tps)]
-    f1 = lambda: Spread(lambda o: lf.at[c, slow, fast, o], s1f, r1f)
+    toks = lambda: [remote(tokens.at[0], lt.at[k], st.at[k], rt.at[k], (p, c, z)) for k, p in enumerate(tps)]
+    f1 = lambda: Spread(lambda o: lf.at[c, slow, fast, o], s1f, r1f, pf)
     f2 = lambda: [remote(lf.at[c, slow, fast], lf.at[c, slow, fast], sf.at[0], rf.at[0], fast_dev)]
     f3 = lambda: [remote(lf.at[c, slow], lf.at[c, slow], sf.at[1], rf.at[1], slow_dev)]
     f4 = lambda: [remote(lf.at[c, slow], lf.at[c, slow], sf.at[2], rf.at[2], sibling)]
@@ -386,38 +400,49 @@
     @at_step(0, 0)
     def _():
         greet([(p, c, z) for p in tps] + [(t, c, p) for p in zs] + [sibling])
-        start(mine_f())
+        blocks = lambda v: [v[:, k : k + 256] for k in range(0, v.shape[1], 256)]
+        ups = [w_up[:, k : k + width].astype(f32) for k in range(0, w_up.shape[1], width)]
+        pf[0:96] = jnp.concatenate(ups, 0).astype(bf16)
+        pf[96:128] = jnp.concatenate([w_out[...].astype(f32), jnp.zeros((8, width), f32)], 0).astype(bf16)
+        pf[128:224] = w_down[...]
+        for p in range(GROUP):
+            stack = [extra[p].astype(f32)]
+            for i in range(heads):
+                stack += blocks(w_first[heads * p + i].astype(f32)) + blocks(w_second[heads * p + i].astype(f32))
+            pa[p] = jnp.concatenate(stack, 0).astype(bf16)
+        met(7)
+        f1().begin()
         for i in range(heads):
             start(mine(i) + a1(i))
-        start(mine_t())
-        wait(mine_f())
-        f1().begin()
+        start(mine_f() + mine_t())
+        wait(mine(0) + a1(0))
+        a2(0).begin()
+        wait(mine(1) + a1(1))
+        wait(mine(2) + a1(2))
         start(toks())
-        for i in range(heads):
-            wait(mine(i) + a1(i))
-        a2(0).begin()
         f1().forward()
         a2(1).begin()
+        a2(0).forward()
         f1().finish()
+        wait(mine_f())
         start(f2())
-        a2(0).forward()
+        a2(2).begin()
         a2(0).finish()
         start(a3(0))
         a2(1).forward()
-        a2(2).begin()
         wait(mine_t() + toks() + a3(0))
+
+    @at_step(0, 2)
+    def _():
+        a2(2).forward()
 
     @at_step(1, 0)
     def _():
         a2(1).finish()
         start(a3(1))
-        a2(2).forward()
-        wait(a3(1))
-
-    @at_step(1, 1)
-    def _():
         wait(f2())
         start(f3() + f4())
+        wait(a3(1))
 
     @at_step(2, 0)
     def _():
@@ -425,48 +450,61 @@
         start(a3(2))
         wait(a3(2))
 
-    @pl.when(r == 0)
-    def _():
-        def unpack(i, carry):
+    def unpack(i):
+        def one(tt, carry):
             for cc in range(2):
                 for zz in range(0, 4, 2):
-                    tops, lows = [], []
-                    for k in range(2):
-                        tops.append(la[h, cc, zz + k, i, 0:32, :].astype(f32)[0:24])
-                        lows.append(la[h, cc, zz + k, i, 16:48, :].astype(f32)[8:32])
-                    top, low = jnp.concatenate(tops, 0), jnp.concatenate(lows, 0)
-                    at = pl.ds(pl.multiple_of((i * 8 + cc * 4 + zz) * 24, 48), 48)
-                    wf[0, at, :] = top.astype(bf16)
-                    ws[0, at, :] = low[:, :512].astype(bf16)
-
-                    @pl.when(h == 0)
-                    def _():
-                        last = low[:, 640:768]
-                        cols[at, :] = last
-                        lane = lax.broadcasted_iota(jnp.int32, last.shape, 1)
-                        wv[at, 0:128] = low[:, 512:640].astype(bf16)
-                        wv[at, 128:256] = jnp.where(lane < 64, last, 0.0).astype(bf16)
+                    at = pl.ds(pl.multiple_of((tt * 8 + cc * 4 + zz) * 24, 48), 48)
+
+                    def block(first):
+                        low = first // 16 * 16
+                        both = [la[cc, zz + k, tt, low : low + 32].astype(f32)[first - low :][:24] for k in range(2)]
+                        return jnp.concatenate(both, 0)
+
+                    base = 24 + 120 * i
+                    for j in range(3):
+                        wf[0, at, 256 * j : 256 * j + 256] = block(base + 24 * j).astype(bf16)
+                    for j in range(2):
+                        ws[0, at, 256 * j : 256 * j + 256] = block(base + 72 + 24 * j).astype(bf16)
+                    if i == 0:
+                        both = block(0)
+                        cols[at, :] = both[:, 128:256]
+                        lane = lax.broadcasted_iota(jnp.int32, both.shape, 1)
+                        wv[at, :] = jnp.where(lane < 192, both, 0.0).astype(bf16)
 
             return carry
 
-        lax.fori_loop(0, GROUP, unpack, 0)
-
-        @pl.when(h == 0)
+        lax.fori_loop(0, GROUP, one, 0)
+
+    for i in range(heads):
+
+        @at_step(i, 0)
         def _():
-            small[...] = cols[...].T[64:72]
-            mine_rows = cols[pl.ds(pl.multiple_of(t * 192, 192), 192), :].astype(bf16)
-            lane = lax.broadcasted_iota(jnp.int32, (128, 512), 0)
-            spot = lax.broadcasted_iota(jnp.int32, (128, 512), 1)
-            spread = dot_nn(mine_rows, jnp.where(lane - 69 == spot % 8, 1.0, 0.0).astype(bf16))
-            row = lax.broadcasted_iota(jnp.int32, (64, 512), 0)
-            spot = lax.broadcasted_iota(jnp.int32, (64, 512), 1)
-            for i in range(heads):
-                picked = jnp.where(row == spot // 8, spread[64 * i : 64 * i + 64], 0.0)
-                b2[i] = jnp.broadcast_to(jnp.sum(picked, axis=0, keepdims=True), (8, 512))
+            unpack(i)
+
+    @at_step(0, 0)
+    def _():
+        small[...] = cols[...].T[64:72]
+        mine_rows = cols[pl.ds(pl.multiple_of(t * 192, 192), 192), :].astype(bf16)
+        lane = lax.broadcasted_iota(jnp.int32, (128, 512), 0)
+        spot = lax.broadcasted_iota(jnp.int32, (128, 512), 1)
+        spread = dot_nn(mine_rows, jnp.where(lane - 69 == spot % 8, 1.0, 0.0).astype(bf16))
+        row = lax.broadcasted_iota(jnp.int32, (64, 512), 0)
+        spot = lax.broadcasted_iota(jnp.int32, (64, 512), 1)
+        for i in range(heads):
+            picked = jnp.where(row == spot // 8, spread[64 * i : 64 * i + 64], 0.0)
+            b2[i] = jnp.broadcast_to(jnp.sum(picked, axis=0, keepdims=True), (8, 512))
+        for k, p in enumerate(tps + [t]):
+            line = cols[pl.ds(pl.multiple_of((p * 8 + c * 4 + z) * 24, 8), 8), :]
+            lane = lax.broadcasted_iota(jnp.int32, line.shape, 1)
+            digits = jnp.where(lane == 77, 16.0 * line, jnp.where(lane == 78, line, 0.0))
+            length = jnp.sum(digits, axis=1, keepdims=True)
+            spot = lax.broadcasted_iota(jnp.int32, (8, 512), 1).astype(f32)
+            masks[k] = jnp.where(spot < length, 0.0, -1e30)
 
     @pl.when(h == 0)
     def _():
-        unit, _ = centre_rows(lt[r, 0:512, :].astype(f32))
+        unit, _ = centre_rows(lt[r].astype(f32))
         out = (unit * small[3:4]).astype(bf16)
         nrm[r] = out
         normed[0] = out
@@ -474,10 +512,9 @@
         val[r] = v
         values[0] = v
 
-    mask = lt[r, 512:528, 0:512].astype(f32)[0:1]
     row = lax.broadcasted_iota(jnp.int32, (8, width), 0)
     b1 = jnp.sum(jnp.where(row == h, small[...], 0.0), axis=0, keepdims=True)
-    shift = b2[h, 0:1] + mask
+    shift = b2[h, 0:1] + masks[r, 0:1]
     tile = pl.ds(pl.multiple_of((h // 2) * 128, 128), 128)
     step = 256
     for m in range(0, 512, step):
@@ -502,7 +539,7 @@
         def _():
             start(out_j(k))
 
-    @at_step(2, 2)
+    @at_step(2, 1)
     def _():
         wait(f3())
         start(f5())
@@ -515,12 +552,13 @@
         wait(mine_j() + f4() + f5())
 
 
-def attend_call(pa, pt, pf):
-    heads, width = pa.shape[1], pa.shape[-1]
-    slots = 512
+def attend_call(tokens, extra, w_first, w_second, w_out, w_up, w_down):
+    _, slots, width = tokens.shape
+    heads = w_first.shape[0] // GROUP
     by_row = lambda h, r: (jnp.where(h == 0, r, GROUP - 1), 0, 0)
     by_head = lambda h, r: (h, 0, 0)
     both = lambda h, r: (h, r, 0, 0)
+    rows_f = 2 * w_down.shape[0] + 32
     return pl.pallas_call(
         attend_kernel,
         grid=(heads, GROUP),
@@ -535,9 +573,9 @@
             shape_of((heads, GROUP, slots, width), bf16),
             shape_of((heads, GROUP, slots, slots), bf16),
             shape_of((GROUP, slots, 256), bf16),
-            shape_of((2, 2, 2, 4) + pf.shape, bf16),
+            shape_of((2, 2, 2, 4, rows_f, width), bf16),
         ),
-        in_specs=[ANY] * 3,
+        in_specs=[ANY] + [FULL] * 6,
         out_specs=(
             pl.BlockSpec((1, width, width), by_head),
             pl.BlockSpec((1, width, slots), by_head),
@@ -552,12 +590,15 @@
             ANY,
         ),
         scratch_shapes=[
-            pltpu.VMEM((heads, 2, 4, GROUP) + pa.shape[2:], bf16),
-            pltpu.VMEM((GROUP,) + pt.shape, bf16),
+            pltpu.VMEM((GROUP, 384, 256), bf16),
+            pltpu.VMEM((rows_f, width), bf16),
+            pltpu.VMEM((2, 4, GROUP, 384, 256), bf16),
+            pltpu.VMEM((GROUP, slots, width), bf16),
             pltpu.VMEM((GROUP, slots, width), bf16),
             pltpu.VMEM((GROUP, slots, 256), bf16),
             pltpu.VMEM((width, 128), f32),
             pltpu.VMEM((heads, 8, slots), f32),
+            pltpu.VMEM((GROUP, 8, slots), f32),
             pltpu.VMEM((GROUP, slots, 256), bf16),
             DMA((heads + 3,)),
             DMA((heads, 3)),
@@ -576,7 +617,7 @@
             DMA((3,)),
         ],
         compiler_params=pltpu.CompilerParams(collective_id=1, has_side_effects=True, vmem_limit_bytes=VMEM_LIMIT),
-    )(pa, pt, pf)
+    )(tokens, extra, w_first, w_second, w_out, w_up, w_down)
 
 
 def slab(t, c, z):
@@ -585,8 +626,8 @@
 
 
 def ffn_kernel(
-    lf, joined, tokens, small, gout, result, gmid, gmix, half, gg2,
-    gf, gj, more, wu, wo, n2, acc, gn2, gwu, own, sg, rg, sx, rx,
+    lf_far, joined, tokens, small, gout, result, gmid, gmix, half, gg2,
+    lf, loads, middles, gf, gj, more, wu, wo, n2, acc, gn2, gwu, own, sg, rg, sx, rx,
 ):
     width = tokens.shape[-1]
     me, core, z_me = place()
@@ -600,20 +641,27 @@
     ]
     out_g = lambda k: [remote(gj.at[tps[k]], gmix.at[k], sg.at[k], rg.at[k], (tps[k], core, z_me))]
     greet([(p, core, z_me) for p in tps] + [sibling])
+    load = lambda k: local(lf_far.at[:, :, :, :, parts[k], :], lf.at[:, :, :, :, parts[k], :], loads.at[k])
+    for k in (2, 0, 1):
+        load(k).start()
+    load(2).wait()
     wo[...] = jnp.zeros_like(wo)
     for t in range(GROUP):
         for c in range(2):
             for z in range(0, 4, 2):
-                pair = [lf[slab(t, c, z + k)][96:128].astype(f32)[0:24] for k in range(2)]
+                pair = [lf[slab(t, c, z + k) + (slice(96, 128),)].astype(f32)[0:24] for k in range(2)]
                 wo[t, (c * 4 + z) * 24 : (c * 4 + z) * 24 + 48, :] = jnp.concatenate(pair, 0).astype(bf16)
     middle = tokens[...].astype(f32)
     for t in range(GROUP):
         middle = middle + dot_nn(joined[t], wo[t])
     acc[...] = middle
+    middles[...] = middle
     g2 = small[4:5]
     unit, _ = centre_rows(middle)
     n2[...] = (unit * g2).astype(bf16)
     gn2[...] = jnp.zeros_like(gn2)
+    load(0).wait()
+    load(1).wait()
 
     def block(p, carry):
         rows = pl.ds(pl.multiple_of(p * 48, 16), 48)
@@ -649,12 +697,10 @@
         return carry
 
     lax.fori_loop(0, 2, block, 0)
+    met(4)
     start(cross(0) + cross(1))
     result[...] = acc[...]
-    middle = tokens[...].astype(f32)
-    for t in range(GROUP):
-        middle = middle + dot_nn(joined[t], wo[t])
-    unit, scale = centre_rows(middle)
+    unit, scale = centre_rows(middles[...])
     gn = gn2[...]
     gg2[...] = jnp.sum((gn * unit).reshape(-1, 8, width), axis=0)
     gu = gn * g2
@@ -705,9 +751,12 @@
             shape_of(lf.shape[1:], bf16),
             shape_of((8, width), f32),
         ),
-        in_specs=[FULL] * 5,
+        in_specs=[ANY] + [FULL] * 4,
         out_specs=(FULL, FULL, ANY, FULL, FULL),
         scratch_shapes=[
+            pltpu.VMEM(lf.shape, bf16),
+            DMA((3,)),
+            pltpu.VMEM((slots, width), f32),
             pltpu.VMEM(lf.shape, bf16),
             pltpu.VMEM(joined.shape, bf16),
             pltpu.VMEM(lf.shape[1:], bf16),
@@ -729,22 +778,24 @@
 
 def back_kernel(
     wf, ws, wv, normed, values, hid, slope, prob, gmix, gg2, half, tokens, gmid, small, out_f, out_a, out_s, gtok,
-    awf, aws, ab1, ab2, gn, gv, awv, ag1, ga, gs, gnb, nb, fs, fb2, fb3, fb4, cb1, cb2, sb1, sb2,
+    awf, aws, ab1, ab2, gn, gv, awv, ag1, stash, ga, gs, gnb, nb, fs, fb2, fb3, fb4, cb1, cb2, sb1, sb2,
     own, s1, r1, s2, r2, s3, r3, sn, rn, sf, rf, s4, r4, sv, rv,
 ):
-    h, r = pl.program_id(0), pl.program_id(1)
+    step, r = pl.program_id(0), pl.program_id(1)
     width = wf.shape[-1]
-    heads = ga.shape[0]
+    heads = ab1.shape[0]
+    h = heads - 1 - step
     t, c, z = place()
     sibling = (t, 1 - c, z)
     tps, zs = group_peers(), line_peers()
     slow, fast, slow_dev, fast_dev = square()
 
-    a1 = lambda i: [remote(ga.at[i, 1 - c], cb1.at[i], s1.at[i], r1.at[i], sibling)]
+    a1 = lambda i: [remote(ga.at[1 - c, :, :, part(i)], cb1.at[:, :, part(i)], s1.at[i], r1.at[i], sibling)]
     def add_heads(i):
         def add(o, slot):
             def one(j, carry):
-                ga[i, c, o, j] = (ga[i, c, o, j].astype(f32) + cb2[i, slot, j].astype(f32)).astype(bf16)
+                here = ga[c, o, j, part(i)].astype(f32) + cb2[slot, j, part(i)].astype(f32)
+                ga[c, o, j, part(i)] = here.astype(bf16)
                 return carry
 
             lax.fori_loop(0, GROUP, one, 0)
@@ -754,11 +805,14 @@
     def add_f(o, slot):
         fs[fast, o] = (fs[fast, o].astype(f32) + fb4[slot].astype(f32)).astype(bf16)
 
-    a2 = lambda i: Gather(lambda o: ga.at[i, c, o], lambda k: cb2.at[i, k], add_heads(i), s2.at[i], r2.at[i])
+    a2 = lambda i: Gather(
+        lambda o: ga.at[c, o, :, part(i)], lambda k: cb2.at[k, :, part(i)], add_heads(i), s2.at[i], r2.at[i]
+    )
     a3 = lambda i: [
-        remote(ga.at[i, c, z, p], out_a.at[i, t], s3.at[i, k], r3.at[i, k], (p, c, z)) for k, p in enumerate(tps)
+        remote(ga.at[c, z, p, part(i)], out_a.at[t, part(i)], s3.at[i, k], r3.at[i, k], (p, c, z))
+        for k, p in enumerate(tps)
     ]
-    mine = lambda i: [local(ga.at[i, c, z, t], out_a.at[i, t], own.at[i])]
+    mine = lambda i: [local(ga.at[c, z, t, part(i)], out_a.at[t, part(i)], own.at[i])]
     mine_f = lambda: [local(half.at[slow], fs, own.at[heads])]
     v1 = lambda: [remote(gs.at[1 - c], sb1, sv.at[0], rv.at[0], sibling)]
     v2 = lambda: [remote(gs.at[c, p], sb2.at[k], sv.at[1 + k], rv.at[1 + k], (t, c, p)) for k, p in enumerate(zs)]
@@ -768,14 +822,15 @@
     out_n = lambda k: [remote(gnb.at[k], nb.at[k], sn.at[k], rn.at[k], (tps[k], c, z))]
 
     def at_step(i, j):
-        return pl.when((h == i) & (r == j))
+        return pl.when((step == i) & (r == j))
 
     def meet(i):
         wait(a1(i))
 
         def line(k, carry):
             for j in range(GROUP):
-                ga[i, c, k, j] = (ga[i, c, k, j].astype(f32) + cb1[i, k, j].astype(f32)).astype(bf16)
+                here = ga[c, k, j, part(i)].astype(f32) + cb1[k, j, part(i)].astype(f32)
+                ga[c, k, j, part(i)] = here.astype(bf16)
             return carry
 
         lax.fori_loop(0, 4, line, 0)
@@ -795,11 +850,16 @@
     @at_step(0, 0)
     def _():
         greet([(p, c, z) for p in tps] + [(t, c, p) for p in zs] + [sibling])
+        met(7)
         start(f2() + mine_f())
 
     @at_step(1, 0)
     def _():
-        meet(0)
+        meet(2)
+
+    @at_step(1, 2)
+    def _():
+        a2(2).forward()
 
     @at_step(1, 3)
     def _():
@@ -808,17 +868,13 @@
         start(f3())
         add_slabs(fast, fb2.at[fast])
 
-    @at_step(1, 2)
-    def _():
-        a2(0).forward()
-
     @at_step(2, 0)
     def _():
         meet(1)
 
     @at_step(2, 1)
     def _():
-        deal(0)
+        deal(2)
 
     @at_step(2, 2)
     def _():
@@ -834,7 +890,7 @@
     def _():
         awf[...] = jnp.zeros_like(awf)
         aws[...] = jnp.zeros_like(aws)
-        ab1[...] = jnp.zeros_like(ab1)
+        ab1[h] = jnp.zeros(ab1.shape[1:], f32)
         ab2[h] = jnp.zeros(ab2.shape[1:], f32)
 
     tile = pl.ds(pl.multiple_of((h // 2) * 128, 128), 128)
@@ -847,32 +903,32 @@
     ab2[h] += jnp.sum(gl.astype(f32).reshape(-1, 8, 512), axis=0)
     gvh = dot_tn(p, gm)
 
-    @pl.when(h != 1)
+    @pl.when(h != 0)
     def _():
         gv[r, :, tile] = gvh
 
-    @pl.when(h == 1)
+    @pl.when(h == 0)
     def _():
         gv[r, :, tile] += gvh
 
     aws[...] += dot_tn(hid[0, 0], gl)
     gb = (dot_nt(gl, ws[0]) * slope[0, 0].astype(f32)).astype(bf16)
-    ab1[...] += jnp.sum(gb.astype(f32).reshape(-1, 8, width), axis=0)
+    ab1[h] += jnp.sum(gb.astype(f32).reshape(-1, 8, width), axis=0)
     awf[...] += dot_tn(normed[0], gb)
-    part = dot_nt(gb, wf[0])
-
-    @pl.when(h == 0)
-    def _():
-        gn[r] = part
-
-    @pl.when(h == 1)
-    def _():
-        gn[r] += part
-
-    @pl.when(h == 2)
+    more_gn = dot_nt(gb, wf[0])
+
+    @pl.when(step == 0)
+    def _():
+        gn[r] = more_gn
+
+    @pl.when(step == 1)
+    def _():
+        gn[r] += more_gn
+
+    @pl.when(step == 2)
     def _():
         gvb = gv[r].astype(bf16)
-        total = gn[r] + part + dot_nt(gvb, wv[...])
+        total = gn[r] + more_gn + dot_nt(gvb, wv[...])
         gn[r] = total
         both = (total * normed[0].astype(f32)).reshape(-1, 8, width)
         ag1[...] = jnp.where(r == 0, 0.0, ag1[...]) + jnp.sum(both, axis=0)
@@ -893,41 +949,46 @@
                 gnb[k] = total.astype(bf16)
                 start(out_n(k))
 
-    @pl.when(r == GROUP - 1)
-    def _():
-        last = h == 2
-        row = lax.broadcasted_iota(jnp.int32, (128, width), 0)
-        stack = jnp.where(row == 64, jnp.sum(ab1[...], axis=0, keepdims=True), 0.0)
-        gains = jnp.sum(ag1[...], axis=0, keepdims=True) / small[3:4]
-        stack = jnp.where(last & (row == 65), gains, stack)
-        stack = jnp.where(last & (row == 66), jnp.sum(gg2[...], axis=0, keepdims=True), stack)
-        cols = stack.T
-        lane = lax.broadcasted_iota(jnp.int32, (width, 128), 1)
-
-        @pl.when(jnp.logical_not(last))
-        def _():
-            awv[:, 0:128] = jnp.zeros((width, 128), f32)
-            awv[:, 128:256] = cols
-
-        @pl.when(last)
-        def _():
-            awv[:, 128:256] = jnp.where(lane < 64, awv[:, 128:256], cols)
-
-        def pack(i, carry):
+    def pack(i):
+        def one(tt, carry):
             for cc in range(2):
                 for zz in range(4):
-                    at = pl.ds(pl.multiple_of((i * 8 + cc * 4 + zz) * 24, 8), 24)
-                    low = jnp.concatenate([aws[at, :], awv[at, :]], 1)
-                    ga[h, cc, zz, i] = jnp.concatenate([awf[at, :], low], 0).astype(bf16)
+                    at = pl.ds(pl.multiple_of((tt * 8 + cc * 4 + zz) * 24, 8), 24)
+                    stack = [awf[at, 256 * j : 256 * j + 256] for j in range(3)]
+                    stack += [aws[at, 256 * j : 256 * j + 256] for j in range(2)]
+                    if i == 0:
+                        stack = [awv[at, :]] + stack
+                    if i == 1:
+                        stack = stack + [stash[cc, zz, tt]]
+                    whole = jnp.concatenate(stack, 0)
+                    if i == 2:
+                        stash[cc, zz, tt] = whole[0:8]
+                        whole = whole[8:]
+                    ga[cc, zz, tt, part(i)] = whole.astype(bf16)
             return carry
 
-        lax.fori_loop(0, GROUP, pack, 0)
-
-    for i in range(heads):
-
-        @at_step(i, 3)
-        def _():
-            start(a1(i))
+        lax.fori_loop(0, GROUP, one, 0)
+        start(a1(i))
+
+    @at_step(0, 3)
+    def _():
+        pack(2)
+
+    @at_step(1, 3)
+    def _():
+        pack(1)
+
+    @at_step(2, 3)
+    def _():
+        row = lax.broadcasted_iota(jnp.int32, (128, width), 0)
+        stack = jnp.zeros((128, width), f32)
+        gains = jnp.sum(ag1[...], axis=0, keepdims=True) / small[3:4]
+        lines = [jnp.sum(ab1[i], axis=0, keepdims=True) for i in range(heads)]
+        for k, line in enumerate(lines + [gains, jnp.sum(gg2[...], axis=0, keepdims=True)]):
+            stack = jnp.where(row == 64 + k, line, stack)
+        lane = lax.broadcasted_iota(jnp.int32, (width, 128), 1)
+        awv[:, 128:256] = jnp.where(lane < 64, awv[:, 128:256], stack.T)
+        pack(0)
 
     @at_step(2, 3)
     def _():
@@ -938,14 +999,14 @@
                 s = (cc * 4 + zz) * 192
                 gs[cc, zz] = (pltpu.roll(flat, 1536 - s, 1) if s else flat)[:, 0:256]
         start(v1())
-        meet(2)
+        meet(0)
         wait(v1())
         gs[c] += sb1[...]
         start(v2())
         f4().forward()
         for k in range(3):
             wait(out_n(k))
-        a2(2).forward()
+        a2(0).forward()
 
         def ln_back(i, carry):
             at = pl.ds(pl.multiple_of(i * 128, 128), 128)
@@ -964,7 +1025,7 @@
         out_f[...] = fs[fast, z].astype(f32)
         wait(v2())
         out_s[...] = gs[c, z] + sb2[0] + sb2[1] + sb2[2]
-        deal(2)
+        deal(0)
         for i in range(heads):
             wait(mine(i) + a3(i))
 
@@ -972,16 +1033,16 @@
 def back_call(wf, ws, wv, normed, values, hid, slope, prob, gmix, gg2, half, tokens, gmid, small):
     heads, width, slots = ws.shape
     rows = half.shape[-2]
-    by_head = lambda h, r: (h, 0, 0)
+    by_head = lambda h, r: (heads - 1 - h, 0, 0)
     row = lambda h, r: (r, 0, 0)
-    both = lambda h, r: (h, r, 0, 0)
+    both = lambda h, r: (heads - 1 - h, r, 0, 0)
     flat = lambda h, r: (0, 0)
     return pl.pallas_call(
         back_kernel,
         grid=(heads, GROUP),
         out_shape=(
             shape_of((rows, width), f32),
-            shape_of((heads, GROUP, 48, width), bf16),
+            shape_of((GROUP, 384, 256), bf16),
             shape_of((8, 256), f32),
             shape_of(tokens.shape, f32),
         ),
@@ -1005,13 +1066,14 @@
         scratch_shapes=[
             pltpu.VMEM((width, width), f32),
             pltpu.VMEM((width, slots), f32),
-            pltpu.VMEM((8, width), f32),
+            pltpu.VMEM((heads, 8, width), f32),
             pltpu.VMEM((heads, 8, slots), f32),
             pltpu.VMEM((GROUP, slots, width), f32),
             pltpu.VMEM((GROUP, slots, 256), f32),
             pltpu.VMEM((width, 256), f32),
             pltpu.VMEM((8, width), f32),
-            pltpu.VMEM((heads, 2, 4, GROUP, 48, width), bf16),
+            pltpu.VMEM((2, 4, GROUP, 8, 256), f32),
+            pltpu.VMEM((2, 4, GROUP, 384, 256), bf16),
             pltpu.VMEM((2, 4, 8, 256), f32),
             pltpu.VMEM((3, slots, width), bf16),
             pltpu.VMEM((3, slots, width), bf16),
@@ -1019,8 +1081,8 @@
             pltpu.VMEM((2, 4, rows, width), bf16),
             pltpu.VMEM((4, rows, width), bf16),
             pltpu.VMEM((4, rows, width), bf16),
-            pltpu.VMEM((heads, 4, GROUP, 48, width), bf16),
-            pltpu.VMEM((heads, 4, GROUP, 48, width), bf16),
+            pltpu.VMEM((4, GROUP, 384, 256), bf16),
+            pltpu.VMEM((4, GROUP, 384, 256), bf16),
             pltpu.VMEM((4, 8, 256), f32),
             pltpu.VMEM((3, 8, 256), f32),
             DMA((heads + 1,)),
@@ -1043,56 +1105,41 @@
     )(wf, ws, wv, normed, values, hid, slope, prob, gmix, gg2, half, tokens, gmid, small)
 
 
-def pack_inputs(tokens, lengths, gain_one, w_value, w_first, b_first, w_second, b_second, w_out, gain_two, w_up, w_down):
-    _, slots, width = tokens.shape
-    heads_all, depth, _ = w_first.shape
-    heads = heads_all // GROUP
-    split = lambda v: v.reshape((GROUP, heads) + v.shape[1:])
-    cols = jnp.concatenate(
-        [
-            b_first.reshape(GROUP, heads, depth).transpose(0, 2, 1),
-            jnp.broadcast_to(jnp.stack([gain_one, gain_two], 1), (GROUP, depth, 2)),
-            jnp.broadcast_to(b_second.reshape(depth, 8), (GROUP, depth, 8)),
-            jnp.zeros((GROUP, depth, 51), bf16),
-        ],
-        2,
-    )
-    head_zero = jnp.concatenate([w_value.reshape(depth, GROUP, -1).transpose(1, 0, 2), cols], 2)
-    extra = jnp.pad(head_zero[:, None], ((0, 0), (0, heads - 1), (0, 0), (0, 0)))
-    low = jnp.concatenate([split(w_second), extra], 3)
-    pa = jnp.concatenate([split(w_first), low], 2)
-    spot = lax.broadcasted_iota(jnp.int32, (16, width), 1)
-    mask = jnp.where(spot < lengths[0], 0.0, -1e30).astype(bf16)
-    pt = jnp.concatenate([tokens[0], mask], 0)
-    ups = [w_up[:, k * width : (k + 1) * width] for k in range(w_up.shape[1] // width)]
-    pf = jnp.concatenate(ups + [w_out, jnp.zeros((8, width), bf16), w_down], 0)
-    return pa, pt, pf
-
-
 def on_device_fast(tokens, lengths, gain_one, w_value, w_first, b_first, w_second, b_second, w_out, gain_two, w_up, w_down, grad_out):
     _, slots, width = tokens.shape
     heads_all, depth, _ = w_first.shape
     heads = heads_all // GROUP
-    pa, pt, pf = pack_inputs(
-        tokens, lengths, gain_one, w_value, w_first, b_first, w_second, b_second, w_out, gain_two, w_up, w_down
+    digits = jnp.stack([lengths[0] // 16, lengths[0] % 16]).astype(bf16)
+    extra = jnp.concatenate(
+        [
+            w_value.reshape(depth, GROUP, -1).transpose(1, 0, 2),
+            b_first.reshape(GROUP, heads, depth).transpose(0, 2, 1),
+            jnp.broadcast_to(jnp.stack([gain_one, gain_two], 1), (GROUP, depth, 2)),
+            jnp.broadcast_to(b_second.reshape(depth, 8), (GROUP, depth, 8)),
+            jnp.broadcast_to(digits, (GROUP, depth, 2)),
+            jnp.zeros((GROUP, depth, 49), bf16),
+        ],
+        2,
     )
-    wf, ws, wv, small, normed, values, hid, slope, prob, joined, lf = attend_call(pa, pt, pf)
+    wf, ws, wv, small, normed, values, hid, slope, prob, joined, lf = attend_call(
+        tokens, extra, w_first, w_second, w_out, w_up, w_down
+    )
     result, gmid, gmix, half, gg2 = ffn_call(lf, joined, tokens[0], small, grad_out[0])
     out_f, out_a, out_s, gtok = back_call(
         wf, ws, wv, normed, values, hid, slope, prob, gmix, gg2, half, tokens[0], gmid, small
     )
-    low = out_a[:, :, 24:].astype(f32)
-    to_all = lambda v: v.transpose((1, 0) + tuple(range(2, v.ndim))).reshape((heads_all,) + v.shape[2:])
-    gb1 = to_all(low[:, :, :, 704])
-    gains = jnp.sum(low[2, :, :, 705:707], axis=0)
+    side = out_a[:, :depth].astype(f32)
+    blocks = out_a[:, depth:].reshape(GROUP, heads, 5, depth, 256)
+    widen = lambda v: v.transpose(0, 1, 3, 2, 4).reshape(heads_all, depth, -1).astype(f32)
+    gains = jnp.sum(side[:, :, 195:197], axis=0)
     return (
         result[None],
         gtok[None],
         gains[:, 0],
-        low[2, :, :, 512:704].transpose(1, 0, 2).reshape(depth, width),
-        to_all(out_a[:, :, :24].astype(f32)),
-        gb1,
-        to_all(low[:, :, :, :512]),
+        side[:, :, :192].transpose(1, 0, 2).reshape(depth, width),
+        widen(blocks[:, :, :3]),
+        side[:, :, 192:195].transpose(0, 2, 1).reshape(heads_all, depth),
+        widen(blocks[:, :, 3:]),
         out_s[0, : b_second.shape[0]],
         out_f[4 * depth : 5 * depth],
         gains[:, 1],

time: 323 us -> 301 us (0.932)
  Pallas kernels: 299 us -> 280 us
    pallas_call x1, Pallas kernels: 139 us -> 125 us  [attend_call(): pl.pallas_call(attend_kernel, grid=(heads, GROUP), out_shape=(shape_of((h...]
where the time goes in v5:
time: 301 us
  Pallas kernels  280 us (93%)
  local copies, waits for them, and re-layouts  17.7 us (6%)
    pallas_call x1, Pallas kernels, attend_call(): pl.pallas_call(attend_kernel, grid=(heads, GROUP), out_shape=(shape_of((h...  125 us
    pallas_call x1, Pallas kernels, back_call(): pl.pallas_call(back_kernel, grid=(heads, GROUP), out_shape=(shape_of((row...  114 us
    pallas_call x1, Pallas kernels, ffn_call(): pl.pallas_call(ffn_kernel, out_shape=(shape_of((slots, width), f32), shap...  41.2 us

profile of v5, /device:TPU:0, one launch (start us, length us, event | category | flops | bytes accessed | tf_op | source)
XLA Modules:
  0.0 300.8 jit_solution(15649313320074316258)
XLA Ops:
  1.3 0.1 pad_maximum_fusion.1
  1.4 0.7 pad_maximum_fusion
  2.1 0.7 reshape.55
  2.8 0.1 copy.47
  2.9 0.7 reshape.56
  3.7 0.1 copy.46
  3.8 0.9 reshape.54
  4.7 0.7 concatenate.3.extra
  5.4 124.7 %shard_map.220 = (bf16[3,768,768]{2,1,0:T(8,128)(2,1)}, bf16[3,768,512]{2,1,0:T(8,128)(2,1)}, bf16[768,256]{1,0:T(8,128)(2,1)}, f32[8,768]{1,0:T(8,128)}, bf16[4...) custom-call(bf16[1,512,768]{2,1,0:T(8,128)(2,1)} %tokens.1, ...), custom_call_target="tpu_custom_call" | custom-call | tf_op jit(solution)/shard_map/pallas_call | solution.py:562
  130.2 41.2 %shard_map.221 = (f32[512,768]{1,0:T(8,128)}, f32[512,768]{1,0:T(8,128)}, bf16[4,512,256]{2,1,0:T(8,128)(2,1)}, bf16[2,2,4,224,768]{4,3,2,1,0:T(8,128)(2,1)}, f32[8,768]{1,0:T(8,128)}) custom-call(bf16[2,2,2,4,224,768]{5,4,3,2,1,0:T(8,128)(2,1)} %get-tuple-element.32.lf_far, bf16[4,512,256]{2,1,0:T(8,128)(2,1)} %get-tuple-element.33.joined, ...), custom_call_target="tpu_custom_call" | custom-call | tf_op jit(solution)/shard_map/pallas_call | solution.py:745
  171.4 113.9 %shard_map.222 = (f32[224,768]{1,0:T(8,128)}, bf16[4,384,256]{2,1,0:T(8,128)(2,1)}, f32[8,256]{1,0:T(8,128)}, f32[512,768]{1,0:T(8,128)}) custom-call(bf16[3,768,768]{2,1,0:T(8,128)(2,1)} %get-tuple-element.36.wf, bf16[3,768,512]{2,1,0:T(8,128)(2,1)} %get-tuple-element.37.ws, bf16[768,256]{1,0:T(8,128)(2,1)} %get-tuple-element.38.wv, ...), custom_call_target="tpu_custom_call" | custom-call | tf_op jit(solution)/shard_map/pallas_call | solution.py:1040
  285.4 0.0 copy-start.2
  285.4 1.3 slice.47
  286.7 1.5 slice.48
  288.2 1.8 fusion
  290.0 0.7 copy.54
  290.8 0.8 slice_convert_fusion.1
  291.6 0.0 copy-done.2
  291.6 0.1 slice.43
  291.6 0.1 slice_reduce_fusion
  291.7 0.7 slice_reduce_fusion.1
  292.4 0.1 slice_bitcast_fusion.1
  292.5 0.1 copy.50
  292.6 0.6 reshape.59
  293.3 0.7 reshape.57
  294.0 0.3 copy.51
  294.4 1.3 reshape.63
  295.6 0.1 slice_convert_fusion
  295.7 0.0 copy-start
  295.7 0.5 copy.58
  296.2 1.5 reshape.62
  297.7 0.0 copy-done
  297.7 0.0 copy-start.1
  297.7 1.1 copy.63
  298.9 0.8 copy-done.1
  299.7 1.1 copy.64
  (8 shorter events, 0.1 us)
Async XLA Ops:
  285.4 6.2 %copy-start.2 = (bf16[4,384,256]{2,1,0:T(8,128)(2,1)S(1)}, bf16[4,384,256]{2,1,0:T(8,128)(2,1)}, u32[]{:S(2)}) copy-start(bf16[4,384,256]{2,1,0:T(8,128)(2,1)} %get-tuple-element.49) | copy-start | bytes 2359300
  295.7 2.0 copy-start
  297.7 2.0 copy-start.1

commit v6 on v5

--- a/solution.py
+++ b/solution.py
@@ -386,12 +386,20 @@
     mine_t = lambda: [local(tokens.at[0], lt.at[3], own.at[heads])]
     mine_f = lambda: [local(pf, lf.at[c, slow, fast, z], own.at[heads + 1])]
     mine_j = lambda: [local(join.at[3], joined.at[t], own.at[heads + 2])]
-    toks = lambda: [remote(tokens.at[0], lt.at[k], st.at[k], rt.at[k], (p, c, z)) for k, p in enumerate(tps)]
-    f1 = lambda: Spread(lambda o: lf.at[c, slow, fast, o], s1f, r1f, pf)
-    f2 = lambda: [remote(lf.at[c, slow, fast], lf.at[c, slow, fast], sf.at[0], rf.at[0], fast_dev)]
-    f3 = lambda: [remote(lf.at[c, slow], lf.at[c, slow], sf.at[1], rf.at[1], slow_dev)]
-    f4 = lambda: [remote(lf.at[c, slow], lf.at[c, slow], sf.at[2], rf.at[2], sibling)]
-    f5 = lambda: [remote(lf.at[c, 1 - slow], lf.at[c, 1 - slow], sf.at[3], rf.at[3], sibling)]
+    tok_fast = lambda: remote(tokens.at[0], lt.at[c], st.at[0], rt.at[0], fast_dev)
+    tok_slow = lambda: remote(tokens.at[0], lt.at[1 - c], st.at[1], rt.at[1], slow_dev)
+    tok_on = lambda: remote(lt.at[c], lt.at[2], st.at[2], rt.at[2], slow_dev)
+    cut = lambda k: slice(*((0, 128), (128, 224))[k])
+    f1 = lambda k: Spread(lambda o: lf.at[c, slow, fast, o, cut(k)], s1f.at[k], r1f.at[k], pf.at[cut(k)])
+
+    def whole(k, spot, n, device):
+        piece = lf.at[spot + (slice(None),) * (4 - len(spot)) + (cut(k),)]
+        return [remote(piece, piece, sf.at[k, n], rf.at[k, n], device)]
+
+    f2 = lambda k: whole(k, (c, slow, fast), 0, fast_dev)
+    f3 = lambda k: whole(k, (c, slow), 1, slow_dev)
+    f4 = lambda k: whole(k, (c, slow), 2, sibling)
+    f5 = lambda k: whole(k, (c, 1 - slow), 3, sibling)
     out_j = lambda k: [remote(join.at[k], joined.at[t], sj.at[k], rj.at[k], (tps[k], c, z))]
 
     def at_step(i, j):
@@ -411,7 +419,7 @@
                 stack += blocks(w_first[heads * p + i].astype(f32)) + blocks(w_second[heads * p + i].astype(f32))
             pa[p] = jnp.concatenate(stack, 0).astype(bf16)
         met(7)
-        f1().begin()
+        f1(0).begin()
         for i in range(heads):
             start(mine(i) + a1(i))
         start(mine_f() + mine_t())
@@ -419,20 +427,34 @@
         a2(0).begin()
         wait(mine(1) + a1(1))
         wait(mine(2) + a1(2))
-        start(toks())
-        f1().forward()
+        start([tok_fast(), tok_slow()])
+        f1(0).forward()
+        f1(1).begin()
+        a2(0).forward()
         a2(1).begin()
-        a2(0).forward()
-        f1().finish()
+        tok_fast().wait_recv()
+        tok_on().start()
+        f1(0).finish()
         wait(mine_f())
-        start(f2())
-        a2(2).begin()
+        start(f2(0))
         a2(0).finish()
         start(a3(0))
+        f1(1).forward()
         a2(1).forward()
-        wait(mine_t() + toks() + a3(0))
-
-    @at_step(0, 2)
+        a2(2).begin()
+        wait(mine_t() + a3(0))
+        tok_fast().wait_send()
+        tok_slow().wait()
+        tok_on().wait()
+
+    @at_step(0, 1)
+    def _():
+        wait(f2(0))
+        start(f3(0) + f4(0))
+        f1(1).finish()
+        start(f2(1))
+
+    @at_step(0, 3)
     def _():
         a2(2).forward()
 
@@ -440,14 +462,19 @@
     def _():
         a2(1).finish()
         start(a3(1))
-        wait(f2())
-        start(f3() + f4())
         wait(a3(1))
+
+    @at_step(1, 1)
+    def _():
+        wait(f2(1))
+        start(f3(1) + f4(1))
 
     @at_step(2, 0)
     def _():
         a2(2).finish()
         start(a3(2))
+        wait(f3(0))
+        start(f5(0))
         wait(a3(2))
 
     def unpack(i):
@@ -526,7 +553,7 @@
         slope[0, 0, at, :] = grad.astype(bf16)
         logits = dot_nn(hidden, ws[0]) + shift
         e = jnp.exp(logits - jnp.max(logits, axis=-1, keepdims=True))
-        p = (e / jnp.sum(e, axis=-1, keepdims=True)).astype(bf16)
+        p = (e * (1.0 / jnp.sum(e, axis=-1, keepdims=True))).astype(bf16)
         prob[0, 0, at, :] = p
         mix = dot_nn(p, val[r, :, tile])
         lane = lax.broadcasted_iota(jnp.int32, mix.shape, 1)
@@ -539,17 +566,19 @@
         def _():
             start(out_j(k))
 
-    @at_step(2, 1)
-    def _():
-        wait(f3())
-        start(f5())
+    @at_step(2, 2)
+    def _():
+        wait(f3(1))
+        start(f5(1))
 
     @at_step(2, 3)
     def _():
         start(mine_j())
+        for k in range(2):
+            wait(f4(k) + f5(k))
         for k in range(3):
             wait(out_j(k))
-        wait(mine_j() + f4() + f5())
+        wait(mine_j())
 
 
 def attend_call(tokens, extra, w_first, w_second, w_out, w_up, w_down):
@@ -609,10 +638,10 @@
             DMA((heads,)),
             DMA((3,)),
             DMA((3,)),
-            DMA((4,)),
-            DMA((4,)),
-            DMA((4,)),
-            DMA((4,)),
+            DMA((2, 4)),
+            DMA((2, 4)),
+            DMA((2, 4)),
+            DMA((2, 4)),
             DMA((3,)),
             DMA((3,)),
         ],

time: 301 us -> 283 us (0.940)
  Pallas kernels: 280 us -> 262 us
    pallas_call x1, Pallas kernels: 125 us -> 107 us  [attend_call(): pl.pallas_call(attend_kernel, grid=(heads, GROUP), out_shape=(shape_of((h...]
where the time goes in v6:
time: 283 us
  Pallas kernels  262 us (93%)
  local copies, waits for them, and re-layouts  17.7 us (6%)
    pallas_call x1, Pallas kernels, back_call(): pl.pallas_call(back_kernel, grid=(heads, GROUP), out_shape=(shape_of((row...  114 us
    pallas_call x1, Pallas kernels, attend_call(): pl.pallas_call(attend_kernel, grid=(heads, GROUP), out_shape=(shape_of((h...  107 us
    pallas_call x1, Pallas kernels, ffn_call(): pl.pallas_call(ffn_kernel, out_shape=(shape_of((slots, width), f32), shap...  40.8 us

profile of v6, /device:TPU:0, one launch (start us, length us, event | category | flops | bytes accessed | tf_op | source)
XLA Modules:
  0.0 283.0 jit_solution(17735878224244917216)
XLA Ops:
  1.3 0.1 pad_maximum_fusion.1
  1.4 0.7 pad_maximum_fusion
  2.1 0.7 reshape.55
  2.8 0.1 copy.47
  2.9 0.7 reshape.56
  3.7 0.1 copy.46
  3.8 0.9 reshape.54
  4.7 0.7 concatenate.3.extra
  5.4 107.3 %shard_map.220 = (bf16[3,768,768]{2,1,0:T(8,128)(2,1)}, bf16[3,768,512]{2,1,0:T(8,128)(2,1)}, bf16[768,256]{1,0:T(8,128)(2,1)}, f32[8,768]{1,0:T(8,128)}, bf16[4...) custom-call(bf16[1,512,768]{2,1,0:T(8,128)(2,1)} %tokens.1, ...), custom_call_target="tpu_custom_call" | custom-call | tf_op jit(solution)/shard_map/pallas_call | solution.py:591
  112.8 40.8 %shard_map.221 = (f32[512,768]{1,0:T(8,128)}, f32[512,768]{1,0:T(8,128)}, bf16[4,512,256]{2,1,0:T(8,128)(2,1)}, bf16[2,2,4,224,768]{4,3,2,1,0:T(8,128)(2,1)}, f32[8,768]{1,0:T(8,128)}) custom-call(bf16[2,2,2,4,224,768]{5,4,3,2,1,0:T(8,128)(2,1)} %get-tuple-element.32.lf_far, bf16[4,512,256]{2,1,0:T(8,128)(2,1)} %get-tuple-element.33.joined, ...), custom_call_target="tpu_custom_call" | custom-call | tf_op jit(solution)/shard_map/pallas_call | solution.py:774
  153.5 113.9 %shard_map.222 = (f32[224,768]{1,0:T(8,128)}, bf16[4,384,256]{2,1,0:T(8,128)(2,1)}, f32[8,256]{1,0:T(8,128)}, f32[512,768]{1,0:T(8,128)}) custom-call(bf16[3,768,768]{2,1,0:T(8,128)(2,1)} %get-tuple-element.36.wf, bf16[3,768,512]{2,1,0:T(8,128)(2,1)} %get-tuple-element.37.ws, bf16[768,256]{1,0:T(8,128)(2,1)} %get-tuple-element.38.wv, ...), custom_call_target="tpu_custom_call" | custom-call | tf_op jit(solution)/shard_map/pallas_call | solution.py:1069
  267.5 0.0 copy-start.2
  267.5 1.3 slice.47
  268.8 1.5 slice.48
  270.4 1.8 fusion
  272.2 0.7 copy.54
  272.9 0.8 slice_convert_fusion.1
  273.7 0.0 copy-done.2
  273.7 0.1 slice.43
  273.8 0.1 slice_reduce_fusion
  273.8 0.7 slice_reduce_fusion.1
  274.5 0.1 slice_bitcast_fusion.1
  274.6 0.1 copy.50
  274.7 0.6 reshape.59
  275.4 0.7 reshape.57
  276.2 0.3 copy.51
  276.5 1.3 reshape.63
  277.8 0.1 slice_convert_fusion
  277.9 0.0 copy-start
  277.9 0.5 copy.58
  278.3 1.5 reshape.62
  279.8 0.0 copy-done
  279.9 0.0 copy-start.1
  279.9 1.1 copy.63
  281.0 0.8 copy-done.1
  281.8 1.1 copy.64
  (8 shorter events, 0.1 us)
Async XLA Ops:
  267.5 6.2 %copy-start.2 = (bf16[4,384,256]{2,1,0:T(8,128)(2,1)S(1)}, bf16[4,384,256]{2,1,0:T(8,128)(2,1)}, u32[]{:S(2)}) copy-start(bf16[4,384,256]{2,1,0:T(8,128)(2,1)} %get-tuple-element.49) | copy-start | bytes 2359300
  277.9 2.0 copy-start
  279.9 2.0 copy-start.1

commit v7 on v6

--- a/solution.py
+++ b/solution.py
@@ -200,7 +200,7 @@
     t, c, z = place()
     along_x = t + 1 - 2 * (t % 2)
     along_y = (t + 2) % GROUP
-    return [along_x, along_y, GROUP - 1 - t]
+    return [GROUP - 1 - t, (1 - c) * along_x + c * along_y, (1 - c) * along_y + c * along_x]
 
 
 def line_peers():
@@ -340,9 +340,7 @@
     y, x = t // 2, t % 2
     tps = group_peers()
     slow, fast = (1 - c) * y + c * x, (1 - c) * x + c * y
-    fast_peer = (1 - c) * tps[0] + c * tps[1]
-    slow_peer = (1 - c) * tps[1] + c * tps[0]
-    return slow, fast, (slow_peer, c, z), (fast_peer, c, z)
+    return slow, fast, (tps[2], c, z), (tps[1], c, z)
 
 
 def gelu_pair(v):
@@ -386,10 +384,9 @@
     mine_t = lambda: [local(tokens.at[0], lt.at[3], own.at[heads])]
     mine_f = lambda: [local(pf, lf.at[c, slow, fast, z], own.at[heads + 1])]
     mine_j = lambda: [local(join.at[3], joined.at[t], own.at[heads + 2])]
-    tok_fast = lambda: remote(tokens.at[0], lt.at[c], st.at[0], rt.at[0], fast_dev)
-    tok_slow = lambda: remote(tokens.at[0], lt.at[1 - c], st.at[1], rt.at[1], slow_dev)
-    tok_on = lambda: remote(lt.at[c], lt.at[2], st.at[2], rt.at[2], slow_dev)
-    cut = lambda k: slice(*((0, 128), (128, 224))[k])
+    tok_fast = lambda: remote(tokens.at[0], lt.at[1], st.at[0], rt.at[0], fast_dev)
+    tok_slow = lambda: remote(tokens.at[0], lt.at[2], st.at[1], rt.at[1], slow_dev)
+    tok_on = lambda: remote(lt.at[1], lt.at[0], st.at[2], rt.at[2], slow_dev)
     f1 = lambda k: Spread(lambda o: lf.at[c, slow, fast, o, cut(k)], s1f.at[k], r1f.at[k], pf.at[cut(k)])
 
     def whole(k, spot, n, device):
@@ -654,13 +651,21 @@
     return (0, y, x, z) if c == 0 else (1, x, y, z)
 
 
+CUTS = ((0, 128), (128, 224))
+
+
+def cut(k):
+    return slice(*CUTS[k])
+
+
 def ffn_kernel(
     lf_far, joined, tokens, small, gout, result, gmid, gmix, half, gg2,
-    lf, loads, middles, gf, gj, more, wu, wo, n2, acc, gn2, gwu, own, sg, rg, sx, rx,
+    lf, gf, gj, more, meet_b, acts, slopes, wu, wo, n2, gn2, gwu, loads, own, sg, rg, sx, rx, sb, rb,
 ):
     width = tokens.shape[-1]
     me, core, z_me = place()
     tps = group_peers()
+    slow, fast, slow_dev, fast_dev = square()
     sibling = (me, 1 - core, z_me)
     parts = (slice(0, 96), slice(128, 224), slice(96, 128))
     cross = lambda k: [
@@ -668,6 +673,7 @@
             gf.at[1 - core, :, :, :, parts[k], :], more.at[:, :, :, parts[k], :], sx.at[k], rx.at[k], sibling
         )
     ]
+    over = lambda: remote(gf.at[core, 1 - slow, :, :, cut(1), :], meet_b, sb, rb, slow_dev)
     out_g = lambda k: [remote(gj.at[tps[k]], gmix.at[k], sg.at[k], rg.at[k], (tps[k], core, z_me))]
     greet([(p, core, z_me) for p in tps] + [sibling])
     load = lambda k: local(lf_far.at[:, :, :, :, parts[k], :], lf.at[:, :, :, :, parts[k], :], loads.at[k])
@@ -683,16 +689,25 @@
     middle = tokens[...].astype(f32)
     for t in range(GROUP):
         middle = middle + dot_nn(joined[t], wo[t])
-    acc[...] = middle
-    middles[...] = middle
+    result[...] = middle
+    gmid[...] = middle
     g2 = small[4:5]
     unit, _ = centre_rows(middle)
     n2[...] = (unit * g2).astype(bf16)
     gn2[...] = jnp.zeros_like(gn2)
     load(0).wait()
-    load(1).wait()
-
-    def block(p, carry):
+
+    def fold(k):
+        def one(i, carry):
+            for j in range(2):
+                for z in range(4):
+                    spot = (i, j, z, parts[k])
+                    gf[(core,) + spot] = (gf[(core,) + spot].astype(f32) + more[spot].astype(f32)).astype(bf16)
+            return carry
+
+        lax.fori_loop(0, 2, one, 0)
+
+    def ahead(p, carry):
         rows = pl.ds(pl.multiple_of(p * 48, 16), 48)
         for t in range(GROUP):
             for c in range(2):
@@ -701,22 +716,29 @@
                     at = (t * 8 + c * 4 + z) * 24
                     for k in range(2):
                         both = jnp.concatenate([e[24 * k : 24 * k + 24] for e in ends], 0)
-                        wu[k, at : at + 48, :] = both.astype(bf16)
+                        wu[2 * p + k, at : at + 48, :] = both.astype(bf16)
+        branch = gout[...].astype(bf16)
+        for k in range(2):
+            act, slope = gelu_pair(dot_nn(n2[...], wu[2 * p + k]))
+            act = act.astype(bf16)
+            acts[2 * p + k] = act
+            slopes[2 * p + k] = slope.astype(bf16)
+            gwd = dot_tn(act, branch).astype(bf16)
+            gf[0, p, k, :, 128:224, :] = gwd[:384].reshape(4, 96, width)
+            gf[1, k, p, :, 128:224, :] = gwd[384:].reshape(4, 96, width)
+        return carry
+
+    def behind(p, carry):
+        rows = pl.ds(pl.multiple_of(p * 48, 16), 48)
         branch = gout[...].astype(bf16)
         for k in range(2):
             wd = jnp.concatenate(
                 [lf[0, p, k, :, 128:224, :].reshape(384, width), lf[1, k, p, :, 128:224, :].reshape(384, width)], 0
             )
-            up = dot_nn(n2[...], wu[k])
-            act, slope = gelu_pair(up)
-            act = act.astype(bf16)
-            acc[...] += dot_nn(act, wd)
-            gup = (dot_nt(branch, wd) * slope).astype(bf16)
-            gwd = dot_tn(act, branch).astype(bf16)
-            gf[0, p, k, :, 128:224, :] = gwd[:384].reshape(4, 96, width)
-            gf[1, k, p, :, 128:224, :] = gwd[384:].reshape(4, 96, width)
+            gup = (dot_nt(branch, wd) * slopes[2 * p + k].astype(f32)).astype(bf16)
             gwu[k] = dot_tn(n2[...], gup)
-            gn2[...] += dot_nt(gup, wu[k])
+            gn2[...] += dot_nt(gup, wu[2 * p + k])
+            result[...] += dot_nn(acts[2 * p + k], wd)
         for t in range(GROUP):
             for c in range(2):
                 for z in range(4):
@@ -725,11 +747,23 @@
                     gf[slab(t, c, z) + (rows,)] = both.astype(bf16)
         return carry
 
-    lax.fori_loop(0, 2, block, 0)
+    lax.fori_loop(0, 2, ahead, 0)
     met(4)
-    start(cross(0) + cross(1))
-    result[...] = acc[...]
-    unit, scale = centre_rows(middles[...])
+    start(cross(1))
+    load(1).wait()
+
+    def turn(p, carry):
+        @pl.when(p == 1)
+        def _():
+            wait(cross(1))
+            fold(1)
+            over().start()
+
+        return behind(p, carry)
+
+    lax.fori_loop(0, 2, turn, 0)
+    start(cross(0))
+    unit, scale = centre_rows(gmid[...])
     gn = gn2[...]
     gg2[...] = jnp.sum((gn * unit).reshape(-1, 8, width), axis=0)
     gu = gn * g2
@@ -743,7 +777,7 @@
         gj[t] = dot_nt(ga, wo[t]).astype(bf16)
     for k in range(3):
         start(out_g(k))
-    mine = local(gj.at[me], gmix.at[3], own)
+    mine = local(gj.at[me], gmix.at[3], own.at[0])
     mine.start()
     for t in range(GROUP):
         gwo = dot_tn(joined[t], ga)
@@ -753,20 +787,24 @@
                 padded = jnp.concatenate([gwo[at : at + 24, :], jnp.zeros((8, width), f32)], 0)
                 gf[slab(t, c, z) + (slice(96, 128),)] = padded.astype(bf16)
     start(cross(2))
-    for k in range(3):
+    for k in (0, 2):
         wait(cross(k))
-
-        def fold(i, carry):
-            for j in range(2):
-                for z in range(4):
-                    spot = (i, j, z, parts[k])
-                    half[spot] = (gf[(core,) + spot].astype(f32) + more[spot].astype(f32)).astype(bf16)
-            return carry
-
-        lax.fori_loop(0, 2, fold, 0)
+        fold(k)
+    over().wait()
+
+    def arrived(j, carry):
+        for z in range(4):
+            spot = (core, slow, j, z, cut(1))
+            gf[spot] = (gf[spot].astype(f32) + meet_b[j, z].astype(f32)).astype(bf16)
+        return carry
+
+    lax.fori_loop(0, 2, arrived, 0)
+    leave = local(gf.at[core], half, own.at[1])
+    leave.start()
     for k in range(3):
         wait(out_g(k))
     mine.wait()
+    leave.wait()
 
 
 def ffn_call(lf, joined, tokens, small, gout):
@@ -781,25 +819,28 @@
             shape_of((8, width), f32),
         ),
         in_specs=[ANY] + [FULL] * 4,
-        out_specs=(FULL, FULL, ANY, FULL, FULL),
+        out_specs=(FULL, FULL, ANY, ANY, FULL),
         scratch_shapes=[
             pltpu.VMEM(lf.shape, bf16),
-            DMA((3,)),
-            pltpu.VMEM((slots, width), f32),
             pltpu.VMEM(lf.shape, bf16),
             pltpu.VMEM(joined.shape, bf16),
             pltpu.VMEM(lf.shape[1:], bf16),
-            pltpu.VMEM((2, width, width), bf16),
+            pltpu.VMEM((2, 4, 96, width), bf16),
+            pltpu.VMEM((4, slots, width), bf16),
+            pltpu.VMEM((4, slots, width), bf16),
+            pltpu.VMEM((4, width, width), bf16),
             pltpu.VMEM((GROUP, 256, width), bf16),
             pltpu.VMEM((slots, width), bf16),
             pltpu.VMEM((slots, width), f32),
-            pltpu.VMEM((slots, width), f32),
             pltpu.VMEM((2, width, width), f32),
-            DMA,
+            DMA((3,)),
+            DMA((2,)),
             DMA((3,)),
             DMA((3,)),
             DMA((3,)),
             DMA((3,)),
+            DMA,
+            DMA,
         ],
         compiler_params=pltpu.CompilerParams(collective_id=2, has_side_effects=True, vmem_limit_bytes=VMEM_LIMIT),
     )(lf, joined, tokens, small, gout)
@@ -807,19 +848,20 @@
 
 def back_kernel(
     wf, ws, wv, normed, values, hid, slope, prob, gmix, gg2, half, tokens, gmid, small, out_f, out_a, out_s, gtok,
-    awf, aws, ab1, ab2, gn, gv, awv, ag1, stash, ga, gs, gnb, nb, fs, fb2, fb3, fb4, cb1, cb2, sb1, sb2,
+    wcat, gb_all, awf, aws, ab1, ab2, gn, gv, awv, stash, ga, gs, nb, tok, fs, fb2, fb3, fb4, cb1, cb2, sb1, sb2,
     own, s1, r1, s2, r2, s3, r3, sn, rn, sf, rf, s4, r4, sv, rv,
 ):
     step, r = pl.program_id(0), pl.program_id(1)
-    width = wf.shape[-1]
+    width = ws.shape[1]
     heads = ab1.shape[0]
-    h = heads - 1 - step
+    h = jnp.maximum(heads - 1 - step, 0)
     t, c, z = place()
     sibling = (t, 1 - c, z)
     tps, zs = group_peers(), line_peers()
     slow, fast, slow_dev, fast_dev = square()
 
     a1 = lambda i: [remote(ga.at[1 - c, :, :, part(i)], cb1.at[:, :, part(i)], s1.at[i], r1.at[i], sibling)]
+
     def add_heads(i):
         def add(o, slot):
             def one(j, carry):
@@ -831,8 +873,11 @@
 
         return add
 
-    def add_f(o, slot):
-        fs[fast, o] = (fs[fast, o].astype(f32) + fb4[slot].astype(f32)).astype(bf16)
+    def add_f(k):
+        def add(o, slot):
+            fs[fast, o, cut(k)] = (fs[fast, o, cut(k)].astype(f32) + fb4[slot, cut(k)].astype(f32)).astype(bf16)
+
+        return add
 
     a2 = lambda i: Gather(
         lambda o: ga.at[c, o, :, part(i)], lambda k: cb2.at[k, :, part(i)], add_heads(i), s2.at[i], r2.at[i]
@@ -843,12 +888,19 @@
     ]
     mine = lambda i: [local(ga.at[c, z, t, part(i)], out_a.at[t, part(i)], own.at[i])]
     mine_f = lambda: [local(half.at[slow], fs, own.at[heads])]
+    mine_t = lambda: [local(tokens, tok, own.at[heads + 1]), local(gmid, gtok, own.at[heads + 2])]
+    mine_w = lambda: [
+        local(wf.at[i], wcat.at[:, i * width : (i + 1) * width], own.at[heads + 3 + i]) for i in range(heads)
+    ]
     v1 = lambda: [remote(gs.at[1 - c], sb1, sv.at[0], rv.at[0], sibling)]
     v2 = lambda: [remote(gs.at[c, p], sb2.at[k], sv.at[1 + k], rv.at[1 + k], (t, c, p)) for k, p in enumerate(zs)]
-    f2 = lambda: [remote(half.at[1 - slow], fb2, sf.at[0], rf.at[0], slow_dev)]
-    f3 = lambda: [remote(fs.at[1 - fast], fb3, sf.at[1], rf.at[1], fast_dev)]
-    f4 = lambda: Gather(lambda o: fs.at[fast, o], lambda k: fb4.at[k], add_f, s4, r4)
-    out_n = lambda k: [remote(gnb.at[k], nb.at[k], sn.at[k], rn.at[k], (tps[k], c, z))]
+    f2 = lambda: [remote(half.at[1 - slow, :, :, cut(0), :], fb2, sf.at[0], rf.at[0], slow_dev)]
+    f3 = lambda k: [remote(fs.at[1 - fast, :, cut(k)], fb3.at[:, cut(k)], sf.at[1 + k], rf.at[1 + k], fast_dev)]
+    f4 = lambda k: Gather(
+        lambda o: fs.at[fast, o, cut(k)], lambda n: fb4.at[n, cut(k)], add_f(k), s4.at[k], r4.at[k]
+    )
+    line_n = lambda k: gb_all.at[k, :, 0:width]
+    out_n = lambda k: remote(line_n(k), nb.at[k], sn.at[k], rn.at[k], (fast_dev, fast_dev, slow_dev)[k])
 
     def at_step(i, j):
         return pl.when((step == i) & (r == j))
@@ -869,9 +921,10 @@
         a2(i).finish()
         start(mine(i) + a3(i))
 
-    def add_slabs(total, more):
-        def one(k, carry):
-            fs[total, k] = (fs[total, k].astype(f32) + more[k].astype(f32)).astype(bf16)
+    def add_slabs(total, more, k):
+        def one(i, carry):
+            here = fs[total, i, cut(k)].astype(f32) + more(i).astype(f32)
+            fs[total, i, cut(k)] = here.astype(bf16)
             return carry
 
         lax.fori_loop(0, 4, one, 0)
@@ -879,8 +932,17 @@
     @at_step(0, 0)
     def _():
         greet([(p, c, z) for p in tps] + [(t, c, p) for p in zs] + [sibling])
+        start(mine_f() + mine_w() + mine_t())
         met(7)
-        start(f2() + mine_f())
+        start(f2())
+        wait(mine_f())
+        start(f3(1))
+
+    @at_step(0, 3)
+    def _():
+        wait(f3(1))
+        add_slabs(fast, lambda i: fb3[i, cut(1)], 1)
+        f4(1).begin()
 
     @at_step(1, 0)
     def _():
@@ -888,80 +950,70 @@
 
     @at_step(1, 2)
     def _():
+        f4(1).forward()
+
+    @at_step(1, 3)
+    def _():
+        wait(f2())
+        add_slabs(1 - fast, lambda i: fb2[1 - fast, i], 0)
+        start(f3(0))
+        add_slabs(fast, lambda i: fb2[fast, i], 0)
+
+    @at_step(2, 0)
+    def _():
         a2(2).forward()
-
-    @at_step(1, 3)
-    def _():
-        wait(f2() + mine_f())
-        add_slabs(1 - fast, fb2.at[1 - fast])
-        start(f3())
-        add_slabs(fast, fb2.at[fast])
-
-    @at_step(2, 0)
-    def _():
         meet(1)
 
-    @at_step(2, 1)
+    @at_step(2, 2)
+    def _():
+        wait(f3(0))
+        add_slabs(fast, lambda i: fb3[i, cut(0)], 0)
+        f4(0).begin()
+
+    @at_step(2, 3)
     def _():
         deal(2)
 
-    @at_step(2, 2)
-    def _():
-        a2(1).forward()
-
-    @at_step(2, 3)
-    def _():
-        wait(f3())
-        add_slabs(fast, fb3)
-        f4().begin()
-
-    @pl.when(r == 0)
+    @at_step(3, 0)
+    def _():
+        wait(mine_w())
+
+    @pl.when((r == 0) & (step < heads))
     def _():
         awf[...] = jnp.zeros_like(awf)
         aws[...] = jnp.zeros_like(aws)
         ab1[h] = jnp.zeros(ab1.shape[1:], f32)
         ab2[h] = jnp.zeros(ab2.shape[1:], f32)
 
-    tile = pl.ds(pl.multiple_of((h // 2) * 128, 128), 128)
-    lane = lax.broadcasted_iota(jnp.int32, (512, 128), 1)
-    gm = jnp.where(lane // 64 == h % 2, gmix[0, :, tile].astype(f32), 0.0).astype(bf16)
-    gw = dot_nt(gm, values[0, :, tile])
-    p = prob[0, 0]
-    p32 = p.astype(f32)
-    gl = (p32 * (gw - jnp.sum(p32 * gw, axis=-1, keepdims=True))).astype(bf16)
-    ab2[h] += jnp.sum(gl.astype(f32).reshape(-1, 8, 512), axis=0)
-    gvh = dot_tn(p, gm)
-
-    @pl.when(h != 0)
-    def _():
-        gv[r, :, tile] = gvh
-
-    @pl.when(h == 0)
-    def _():
-        gv[r, :, tile] += gvh
-
-    aws[...] += dot_tn(hid[0, 0], gl)
-    gb = (dot_nt(gl, ws[0]) * slope[0, 0].astype(f32)).astype(bf16)
-    ab1[h] += jnp.sum(gb.astype(f32).reshape(-1, 8, width), axis=0)
-    awf[...] += dot_tn(normed[0], gb)
-    more_gn = dot_nt(gb, wf[0])
-
-    @pl.when(step == 0)
-    def _():
-        gn[r] = more_gn
-
-    @pl.when(step == 1)
-    def _():
-        gn[r] += more_gn
-
-    @pl.when(step == 2)
-    def _():
-        gvb = gv[r].astype(bf16)
-        total = gn[r] + more_gn + dot_nt(gvb, wv[...])
-        gn[r] = total
-        both = (total * normed[0].astype(f32)).reshape(-1, 8, width)
-        ag1[...] = jnp.where(r == 0, 0.0, ag1[...]) + jnp.sum(both, axis=0)
-        more = dot_tn(normed[0], gvb)
+    @pl.when(step < heads)
+    def _():
+        tile = pl.ds(pl.multiple_of((h // 2) * 128, 128), 128)
+        lane = lax.broadcasted_iota(jnp.int32, (512, 128), 1)
+        gm = jnp.where(lane // 64 == h % 2, gmix[0, :, tile].astype(f32), 0.0).astype(bf16)
+        gw = dot_nt(gm, values[0, :, tile])
+        p = prob[0, 0]
+        p32 = p.astype(f32)
+        gl = (p32 * (gw - jnp.sum(p32 * gw, axis=-1, keepdims=True))).astype(bf16)
+        ab2[h] += jnp.sum(gl.astype(f32).reshape(-1, 8, 512), axis=0)
+        gvh = dot_tn(p, gm)
+
+        @pl.when(h != 0)
+        def _():
+            gv[r, :, tile] = gvh.astype(bf16)
+
+        @pl.when(h == 0)
+        def _():
+            gv[r, :, tile] = (gv[r, :, tile].astype(f32) + gvh).astype(bf16)
+
+        aws[...] += dot_tn(hid[0, 0], gl)
+        gb = (dot_nt(gl, ws[0]) * slope[0, 0].astype(f32)).astype(bf16)
+        gb_all[r, :, pl.ds(pl.multiple_of(h * width, 128), width)] = gb
+        ab1[h] += jnp.sum(gb.astype(f32).reshape(-1, 8, width), axis=0)
+        awf[...] += dot_tn(normed[0], gb)
+
+    @pl.when(step == heads - 1)
+    def _():
+        more = dot_tn(normed[0], gv[r])
 
         @pl.when(r == 0)
         def _():
@@ -970,13 +1022,6 @@
         @pl.when(r != 0)
         def _():
             awv[...] += more
-
-        for k in range(3):
-
-            @pl.when(r == k)
-            def _():
-                gnb[k] = total.astype(bf16)
-                start(out_n(k))
 
     def pack(i):
         def one(tt, carry):
@@ -1011,13 +1056,34 @@
     def _():
         row = lax.broadcasted_iota(jnp.int32, (128, width), 0)
         stack = jnp.zeros((128, width), f32)
-        gains = jnp.sum(ag1[...], axis=0, keepdims=True) / small[3:4]
         lines = [jnp.sum(ab1[i], axis=0, keepdims=True) for i in range(heads)]
-        for k, line in enumerate(lines + [gains, jnp.sum(gg2[...], axis=0, keepdims=True)]):
+        for k, line in enumerate(lines + [jnp.sum(gg2[...], axis=0, keepdims=True)]):
             stack = jnp.where(row == 64 + k, line, stack)
         lane = lax.broadcasted_iota(jnp.int32, (width, 128), 1)
         awv[:, 128:256] = jnp.where(lane < 64, awv[:, 128:256], stack.T)
         pack(0)
+
+    @pl.when(step == heads)
+    def _():
+        total = dot_nt(gb_all[r], wcat[...]) + dot_nt(gv[r], wv[...])
+
+        @pl.when(r < 3)
+        def _():
+            gb_all[r, :, 0:width] = total.astype(bf16)
+
+        @pl.when(r == 3)
+        def _():
+            gn[...] = total
+
+    @at_step(3, 0)
+    def _():
+        out_n(0).start()
+        meet(0)
+
+    @at_step(3, 1)
+    def _():
+        out_n(1).start()
+        a2(1).forward()
 
     @at_step(2, 3)
     def _():
@@ -1028,30 +1094,47 @@
                 s = (cc * 4 + zz) * 192
                 gs[cc, zz] = (pltpu.roll(flat, 1536 - s, 1) if s else flat)[:, 0:256]
         start(v1())
-        meet(0)
+
+    @at_step(3, 2)
+    def _():
+        f4(0).forward()
         wait(v1())
         gs[c] += sb1[...]
         start(v2())
-        f4().forward()
-        for k in range(3):
-            wait(out_n(k))
+
+    @at_step(3, 3)
+    def _():
+        out_n(0).wait()
+
+        def join(i, carry):
+            at = pl.ds(pl.multiple_of(i * 128, 128), 128)
+            here = gb_all[2, at, 0:width].astype(f32) + nb[0, at, :].astype(f32)
+            gb_all[2, at, 0:width] = here.astype(bf16)
+            return carry
+
+        lax.fori_loop(0, 4, join, 0)
+        out_n(2).start()
+        deal(1)
         a2(0).forward()
+        f4(1).finish()
+        f4(0).finish()
+        out_f[...] = fs[fast, z].astype(f32)
+        out_n(1).wait()
+        out_n(2).wait()
+        wait(mine_t())
 
         def ln_back(i, carry):
             at = pl.ds(pl.multiple_of(i * 128, 128), 128)
-            g = gn[3, at, :] + nb[0, at, :].astype(f32) + nb[1, at, :].astype(f32) + nb[2, at, :].astype(f32)
-            unit, scale = centre_rows(tokens[at, :].astype(f32))
+            g = gn[at, :] + nb[1, at, :].astype(f32) + nb[2, at, :].astype(f32)
+            unit, scale = centre_rows(tok[at, :].astype(f32))
             gu = g * small[3:4]
             back = scale * (
                 gu - jnp.mean(gu, axis=-1, keepdims=True) - unit * jnp.mean(gu * unit, axis=-1, keepdims=True)
             )
-            gtok[at, :] = gmid[at, :] + back
+            gtok[at, :] += back
             return carry
 
         lax.fori_loop(0, 4, ln_back, 0)
-        deal(1)
-        f4().finish()
-        out_f[...] = fs[fast, z].astype(f32)
         wait(v2())
         out_s[...] = gs[c, z] + sb2[0] + sb2[1] + sb2[2]
         deal(0)
@@ -1062,13 +1145,16 @@
 def back_call(wf, ws, wv, normed, values, hid, slope, prob, gmix, gg2, half, tokens, gmid, small):
     heads, width, slots = ws.shape
     rows = half.shape[-2]
-    by_head = lambda h, r: (heads - 1 - h, 0, 0)
+    head = lambda h: jnp.maximum(heads - 1 - h, 0)
+    held = lambda h, r: jnp.where(h < heads, r, GROUP - 1)
+    by_head = lambda h, r: (head(h), 0, 0)
     row = lambda h, r: (r, 0, 0)
-    both = lambda h, r: (heads - 1 - h, r, 0, 0)
+    early = lambda h, r: (held(h, r), 0, 0)
+    both = lambda h, r: (head(h), held(h, r), 0, 0)
     flat = lambda h, r: (0, 0)
     return pl.pallas_call(
         back_kernel,
-        grid=(heads, GROUP),
+        grid=(heads + 1, GROUP),
         out_shape=(
             shape_of((rows, width), f32),
             shape_of((GROUP, 384, 256), bf16),
@@ -1076,45 +1162,46 @@
             shape_of(tokens.shape, f32),
         ),
         in_specs=[
-            pl.BlockSpec((1, width, width), by_head),
+            ANY,
             pl.BlockSpec((1, width, slots), by_head),
             pl.BlockSpec((width, 256), flat),
             pl.BlockSpec((1, slots, width), row),
-            pl.BlockSpec((1, slots, 256), row),
+            pl.BlockSpec((1, slots, 256), early),
             pl.BlockSpec((1, 1, slots, width), both),
             pl.BlockSpec((1, 1, slots, width), both),
             pl.BlockSpec((1, 1, slots, slots), both),
-            pl.BlockSpec((1, slots, 256), row),
+            pl.BlockSpec((1, slots, 256), early),
             pl.BlockSpec((8, width), flat),
             ANY,
-            FULL,
-            FULL,
+            ANY,
+            ANY,
             pl.BlockSpec((8, width), flat),
         ],
         out_specs=(FULL, ANY, FULL, FULL),
         scratch_shapes=[
+            pltpu.VMEM((width, heads * width), bf16),
+            pltpu.VMEM((GROUP, slots, heads * width), bf16),
             pltpu.VMEM((width, width), f32),
             pltpu.VMEM((width, slots), f32),
             pltpu.VMEM((heads, 8, width), f32),
             pltpu.VMEM((heads, 8, slots), f32),
-            pltpu.VMEM((GROUP, slots, width), f32),
-            pltpu.VMEM((GROUP, slots, 256), f32),
+            pltpu.VMEM((slots, width), f32),
+            pltpu.VMEM((GROUP, slots, 256), bf16),
             pltpu.VMEM((width, 256), f32),
-            pltpu.VMEM((8, width), f32),
             pltpu.VMEM((2, 4, GROUP, 8, 256), f32),
             pltpu.VMEM((2, 4, GROUP, 384, 256), bf16),
             pltpu.VMEM((2, 4, 8, 256), f32),
             pltpu.VMEM((3, slots, width), bf16),
-            pltpu.VMEM((3, slots, width), bf16),
+            pltpu.VMEM((slots, width), bf16),
             pltpu.VMEM((2, 4, rows, width), bf16),
-            pltpu.VMEM((2, 4, rows, width), bf16),
+            pltpu.VMEM((2, 4, 128, width), bf16),
             pltpu.VMEM((4, rows, width), bf16),
             pltpu.VMEM((4, rows, width), bf16),
             pltpu.VMEM((4, GROUP, 384, 256), bf16),
             pltpu.VMEM((4, GROUP, 384, 256), bf16),
             pltpu.VMEM((4, 8, 256), f32),
             pltpu.VMEM((3, 8, 256), f32),
-            DMA((heads + 1,)),
+            DMA((2 * heads + 3,)),
             DMA((heads,)),
             DMA((heads,)),
             DMA((heads, 3)),
@@ -1123,15 +1210,60 @@
             DMA((heads, 3)),
             DMA((3,)),
             DMA((3,)),
-            DMA((2,)),
-            DMA((2,)),
             DMA((3,)),
-            DMA((4,)),
+            DMA((3,)),
+            DMA((2, 3)),
+            DMA((2, 4)),
             DMA((4,)),
             DMA((4,)),
         ],
         compiler_params=pltpu.CompilerParams(collective_id=3, has_side_effects=True, vmem_limit_bytes=VMEM_LIMIT),
     )(wf, ws, wv, normed, values, hid, slope, prob, gmix, gg2, half, tokens, gmid, small)
+
+
+def finish_kernel(sums_a, sums_f, w_first, w_value, out_first, out_second, out_value, out_up, out_out, out_down, dots):
+    heads_all, depth, width = w_first.shape
+    heads = heads_all // GROUP
+    total = jnp.zeros((depth, 256), f32)
+    for t in range(GROUP):
+        whole = sums_a[t].astype(f32)
+        out_value[t] = whole[0:depth]
+        total += jnp.where(
+            lax.broadcasted_iota(jnp.int32, (depth, 256), 1) < 192, whole[0:depth] * w_value[t].astype(f32), 0.0
+        )
+        for i in range(heads):
+            block = lambda j: whole[depth * (1 + 5 * i + j) : depth * (2 + 5 * i + j)]
+            weight = w_first[heads * t + i].astype(f32)
+            for j in range(3):
+                at = slice(256 * j, 256 * j + 256)
+                out_first[heads * t + i, :, at] = block(j)
+                total += block(j) * weight[:, at]
+            for j in range(2):
+                out_second[heads * t + i, :, 256 * j : 256 * j + 256] = block(3 + j)
+    dots[...] = jnp.broadcast_to(jnp.sum(total, axis=1, keepdims=True), dots.shape)
+    for k in range(4):
+        out_up[:, width * k : width * k + width] = sums_f[depth * k : depth * k + depth]
+    out_out[...] = sums_f[4 * depth : 5 * depth]
+    out_down[...] = sums_f[128:224]
+
+
+def finish_call(sums_a, sums_f, w_first, w_value, slots):
+    heads_all, depth, width = w_first.shape
+    return pl.pallas_call(
+        finish_kernel,
+        out_shape=(
+            shape_of((heads_all, depth, width), f32),
+            shape_of((heads_all, depth, slots), f32),
+            shape_of((GROUP, depth, 256), f32),
+            shape_of((depth, 4 * width), f32),
+            shape_of((depth, width), f32),
+            shape_of((4 * depth, width), f32),
+            shape_of((depth, 128), f32),
+        ),
+        in_specs=[FULL] * 4,
+        out_specs=(FULL,) * 7,
+        compiler_params=pltpu.CompilerParams(vmem_limit_bytes=VMEM_LIMIT),
+    )(sums_a, sums_f, w_first, w_value)
 
 
 def on_device_fast(tokens, lengths, gain_one, w_value, w_first, b_first, w_second, b_second, w_out, gain_two, w_up, w_down, grad_out):
@@ -1157,23 +1289,22 @@
     out_f, out_a, out_s, gtok = back_call(
         wf, ws, wv, normed, values, hid, slope, prob, gmix, gg2, half, tokens[0], gmid, small
     )
-    side = out_a[:, :depth].astype(f32)
-    blocks = out_a[:, depth:].reshape(GROUP, heads, 5, depth, 256)
-    widen = lambda v: v.transpose(0, 1, 3, 2, 4).reshape(heads_all, depth, -1).astype(f32)
-    gains = jnp.sum(side[:, :, 195:197], axis=0)
+    grad_first, grad_second, side, grad_up, grad_out_w, grad_down, dots = finish_call(
+        out_a, out_f, w_first, extra, slots
+    )
     return (
         result[None],
         gtok[None],
-        gains[:, 0],
+        dots[:, 0] / gain_one.astype(f32),
         side[:, :, :192].transpose(1, 0, 2).reshape(depth, width),
-        widen(blocks[:, :, :3]),
+        grad_first,
         side[:, :, 192:195].transpose(0, 2, 1).reshape(heads_all, depth),
-        widen(blocks[:, :, 3:]),
+        grad_second,
         out_s[0, : b_second.shape[0]],
-        out_f[4 * depth : 5 * depth],
-        gains[:, 1],
-        out_f[: 4 * depth].reshape(4, depth, width).transpose(1, 0, 2).reshape(depth, 4 * width),
-        out_f[128:],
+        grad_out_w,
+        jnp.sum(side[:, :, 195], axis=0),
+        grad_up,
+        grad_down,
     )
 
 

time: 283 us -> 274 us (0.968)
  local copies, waits for them, and re-layouts: 17.7 us -> 11.1 us
  Pallas kernels: 262 us -> 258 us
    pallas_call x1 -> x2, Pallas kernels: 114 us -> 104 us  [the longest x1 101 us: back_call(): pl.pallas_call(back_kernel, grid=(heads + 1, GROUP), out_shape=(shape_of(...]
    pallas_call x1, Pallas kernels: 40.8 us -> 46.3 us  [ffn_call(): pl.pallas_call(ffn_kernel, out_shape=(shape_of((slots, width), f32), shap...]
    slice x4 -> x1, local copies, waits for them, and re-layouts: 4.08 us -> 0.82 us  [on_device_fast(): dots[:, 0] / gain_one.astype(f32)]
    convert_element_type x3 -> x0, local copies, waits for them, and re-layouts: 3.11 us -> none  [on_device_fast(): v.transpose(0, 1, 3, 2, 4).reshape(heads_all, depth, -1).astype(f32)]
where the time goes in v7:
time: 274 us; the launch traced here: 273 us
  Pallas kernels  258 us (94%)
  local copies, waits for them, and re-layouts  11.1 us (4%)
  other arithmetic  2.78 us (1%)
    pallas_call x1, Pallas kernels, attend_call(): pl.pallas_call(attend_kernel, grid=(heads, GROUP), out_shape=(shape_of((h...  108 us
    pallas_call x1, Pallas kernels, back_call(): pl.pallas_call(back_kernel, grid=(heads + 1, GROUP), out_shape=(shape_of(...  101 us
    pallas_call x1, Pallas kernels, ffn_call(): pl.pallas_call(ffn_kernel, out_shape=(shape_of((slots, width), f32), shap...  46.3 us

profile of v7, /device:TPU:0, one launch (start us, length us, event | category | flops | bytes accessed | tf_op | source)
XLA Modules:
  0.0 273.3 jit_solution(12098023312177638484)
XLA Ops:
  1.3 0.1 pad_maximum_fusion.1
  1.4 0.7 pad_maximum_fusion
  2.1 0.7 reshape.40
  2.8 0.1 copy.28
  2.9 0.7 reshape.41
  3.7 0.1 copy.27
  3.8 0.9 reshape.39
  4.7 0.7 concatenate.3.extra.w_value
  5.4 108.2 %shard_map.220 = (bf16[3,768,768]{2,1,0:T(8,128)(2,1)}, bf16[3,768,512]{2,1,0:T(8,128)(2,1)}, bf16[768,256]{1,0:T(8,128)(2,1)}, f32[8,768]{1,0:T(8,128)}, bf16[4...) custom-call(bf16[1,512,768]{2,1,0:T(8,128)(2,1)} %tokens.1, ...), custom_call_target="tpu_custom_call" | custom-call | tf_op jit(solution)/shard_map/pallas_call | solution.py:588
  113.6 46.3 %shard_map.221 = (f32[512,768]{1,0:T(8,128)}, f32[512,768]{1,0:T(8,128)}, bf16[4,512,256]{2,1,0:T(8,128)(2,1)}, bf16[2,2,4,224,768]{4,3,2,1,0:T(8,128)(2,1)}, f32[8,768]{1,0:T(8,128)}) custom-call(bf16[2,2,2,4,224,768]{5,4,3,2,1,0:T(8,128)(2,1)} %get-tuple-element.39.lf_far, bf16[4,512,256]{2,1,0:T(8,128)(2,1)} %get-tuple-element.40.joined, ...), custom_call_target="tpu_custom_call" | custom-call | tf_op jit(solution)/shard_map/pallas_call | solution.py:812
  159.9 0.0 copy-start.2
  159.9 100.6 %shard_map.222 = (f32[224,768]{1,0:T(8,128)}, bf16[4,384,256]{2,1,0:T(8,128)(2,1)}, f32[8,256]{1,0:T(8,128)}, f32[512,768]{1,0:T(8,128)}) custom-call(bf16[3,768,768]{2,1,0:T(8,128)(2,1)} %get-tuple-element.43.wf, bf16[3,768,512]{2,1,0:T(8,128)(2,1)} %get-tuple-element.44.ws, bf16[768,256]{1,0:T(8,128)(2,1)} %get-tuple-element.45.wv, ...), custom_call_target="tpu_custom_call" | custom-call | tf_op jit(solution)/shard_map/pallas_call | solution.py:1155
  260.5 0.0 copy-start
  260.6 0.0 copy-start.1
  260.6 1.4 slice.18
  262.0 2.9 %shard_map.223 = (f32[12,24,768]{2,1,0:T(8,128)}, f32[12,24,512]{2,1,0:T(8,128)}, f32[4,24,256]{2,1,0:T(8,128)}, f32[24,3072]{1,0:T(8,128)}, f32[24,768]{1,0:T(8...) custom-call(bf16[4,384,256]{2,1,0:T(8,128)(2,1)} %get-tuple-element.56.sums_a, f32[224,768]{1,0:T(8,128)} %get-tuple-element.57.sums_f, ...), custom_call_target="tpu_custom_call" | custom-call | tf_op jit(solution)/shard_map/pallas_call | solution.py:1252
  264.9 0.8 slice_reduce_fusion.1
  265.7 0.0 copy-done.2
  265.7 0.5 convert_divide_fusion
  266.3 1.5 slice_reduce_fusion
  267.8 0.9 slice_bitcast_fusion.1
  268.6 0.1 copy.30
  268.7 0.6 reshape.43
  269.3 0.9 slice_bitcast_fusion
  270.3 0.7 reshape.42
  271.0 0.0 copy-done
  271.0 1.1 copy.36
  272.2 0.0 copy-done.1
  272.2 1.1 copy.37
  (6 shorter events, 0.1 us)
Async XLA Ops:
  159.9 105.8 %copy-start.2 = (bf16[24]{0:T(256)(128)(2,1)S(1)}, bf16[24]{0:T(256)(128)(2,1)}, u32[]{:S(2)}) copy-start(bf16[24]{0:T(256)(128)(2,1)} %param.15) | copy-start | bytes 148
  260.5 10.5 %copy-start = (f32[512,768]{1,0:T(8,128)S(1)}, f32[512,768]{1,0:T(8,128)}, u32[]{:S(2)}) copy-start(f32[512,768]{1,0:T(8,128)} %get-tuple-element.42) | copy-start | bytes 4718596
  260.6 11.6 %copy-start.1 = (f32[512,768]{1,0:T(8,128)S(1)}, f32[512,768]{1,0:T(8,128)}, u32[]{:S(2)}) copy-start(f32[512,768]{1,0:T(8,128)} %get-tuple-element.55) | copy-start | bytes 4718596

commit v8 on v7

--- a/solution.py
+++ b/solution.py
@@ -667,7 +667,8 @@
     tps = group_peers()
     slow, fast, slow_dev, fast_dev = square()
     sibling = (me, 1 - core, z_me)
-    parts = (slice(0, 96), slice(128, 224), slice(96, 128))
+    parts = (slice(0, 48), slice(128, 224), slice(96, 128), slice(48, 96))
+    wanted = (slice(0, 96), slice(128, 224), slice(96, 128))
     cross = lambda k: [
         remote(
             gf.at[1 - core, :, :, :, parts[k], :], more.at[:, :, :, parts[k], :], sx.at[k], rx.at[k], sibling
@@ -676,7 +677,7 @@
     over = lambda: remote(gf.at[core, 1 - slow, :, :, cut(1), :], meet_b, sb, rb, slow_dev)
     out_g = lambda k: [remote(gj.at[tps[k]], gmix.at[k], sg.at[k], rg.at[k], (tps[k], core, z_me))]
     greet([(p, core, z_me) for p in tps] + [sibling])
-    load = lambda k: local(lf_far.at[:, :, :, :, parts[k], :], lf.at[:, :, :, :, parts[k], :], loads.at[k])
+    load = lambda k: local(lf_far.at[:, :, :, :, wanted[k], :], lf.at[:, :, :, :, wanted[k], :], loads.at[k])
     for k in (2, 0, 1):
         load(k).start()
     load(2).wait()
@@ -728,23 +729,42 @@
             gf[1, k, p, :, 128:224, :] = gwd[384:].reshape(4, 96, width)
         return carry
 
+    def down_block(p, k):
+        return jnp.concatenate(
+            [lf[0, p, k, :, 128:224, :].reshape(384, width), lf[1, k, p, :, 128:224, :].reshape(384, width)], 0
+        )
+
     def behind(p, carry):
-        rows = pl.ds(pl.multiple_of(p * 48, 16), 48)
+        @pl.when(p == 1)
+        def _():
+            wait(cross(1))
+            fold(1)
+            over().start()
+
         branch = gout[...].astype(bf16)
         for k in range(2):
-            wd = jnp.concatenate(
-                [lf[0, p, k, :, 128:224, :].reshape(384, width), lf[1, k, p, :, 128:224, :].reshape(384, width)], 0
-            )
-            gup = (dot_nt(branch, wd) * slopes[2 * p + k].astype(f32)).astype(bf16)
-            gwu[k] = dot_tn(n2[...], gup)
+            gup = (dot_nt(branch, down_block(p, k)) * slopes[2 * p + k].astype(f32)).astype(bf16)
+            slopes[2 * p + k] = gup
             gn2[...] += dot_nt(gup, wu[2 * p + k])
-            result[...] += dot_nn(acts[2 * p + k], wd)
+        return carry
+
+    def weights(p, carry):
+        rows = pl.ds(pl.multiple_of(p * 48, 16), 48)
+        for k in range(2):
+            gwu[k] = dot_tn(n2[...], slopes[2 * p + k])
+            result[...] += dot_nn(acts[2 * p + k], down_block(p, k))
         for t in range(GROUP):
             for c in range(2):
                 for z in range(4):
                     at = (t * 8 + c * 4 + z) * 24
                     both = jnp.concatenate([gwu[0, at : at + 24, :], gwu[1, at : at + 24, :]], 0)
                     gf[slab(t, c, z) + (rows,)] = both.astype(bf16)
+        for k, n in ((0, 0), (1, 3)):
+
+            @pl.when(p == k)
+            def _():
+                start(cross(n))
+
         return carry
 
     lax.fori_loop(0, 2, ahead, 0)
@@ -752,17 +772,7 @@
     start(cross(1))
     load(1).wait()
 
-    def turn(p, carry):
-        @pl.when(p == 1)
-        def _():
-            wait(cross(1))
-            fold(1)
-            over().start()
-
-        return behind(p, carry)
-
-    lax.fori_loop(0, 2, turn, 0)
-    start(cross(0))
+    lax.fori_loop(0, 2, behind, 0)
     unit, scale = centre_rows(gmid[...])
     gn = gn2[...]
     gg2[...] = jnp.sum((gn * unit).reshape(-1, 8, width), axis=0)
@@ -787,9 +797,7 @@
                 padded = jnp.concatenate([gwo[at : at + 24, :], jnp.zeros((8, width), f32)], 0)
                 gf[slab(t, c, z) + (slice(96, 128),)] = padded.astype(bf16)
     start(cross(2))
-    for k in (0, 2):
-        wait(cross(k))
-        fold(k)
+    lax.fori_loop(0, 2, weights, 0)
     over().wait()
 
     def arrived(j, carry):
@@ -799,12 +807,16 @@
         return carry
 
     lax.fori_loop(0, 2, arrived, 0)
-    leave = local(gf.at[core], half, own.at[1])
-    leave.start()
+    leave = [local(gf.at[core, :, :, :, cut(k), :], half.at[:, :, :, cut(k), :], own.at[1 + k]) for k in range(2)]
+    leave[1].start()
+    for k in (2, 0, 3):
+        wait(cross(k))
+        fold(k)
+    leave[0].start()
     for k in range(3):
         wait(out_g(k))
     mine.wait()
-    leave.wait()
+    wait(leave)
 
 
 def ffn_call(lf, joined, tokens, small, gout):
@@ -834,11 +846,11 @@
             pltpu.VMEM((slots, width), f32),
             pltpu.VMEM((2, width, width), f32),
             DMA((3,)),
-            DMA((2,)),
             DMA((3,)),
             DMA((3,)),
             DMA((3,)),
-            DMA((3,)),
+            DMA((4,)),
+            DMA((4,)),
             DMA,
             DMA,
         ],
@@ -1079,11 +1091,11 @@
     def _():
         out_n(0).start()
         meet(0)
+        a2(1).forward()
 
     @at_step(3, 1)
     def _():
         out_n(1).start()
-        a2(1).forward()
 
     @at_step(2, 3)
     def _():
@@ -1221,16 +1233,20 @@
     )(wf, ws, wv, normed, values, hid, slope, prob, gmix, gg2, half, tokens, gmid, small)
 
 
-def finish_kernel(sums_a, sums_f, w_first, w_value, out_first, out_second, out_value, out_up, out_out, out_down, dots):
+def finish_kernel(
+    sums_a, sums_f, sums_b, w_first, extra,
+    out_one, out_value, out_first, out_b1, out_second, out_b2, out_out, out_two, out_up, out_down,
+):
     heads_all, depth, width = w_first.shape
     heads = heads_all // GROUP
     total = jnp.zeros((depth, 256), f32)
+    lane = lax.broadcasted_iota(jnp.int32, (depth, 256), 1)
+    sides = []
     for t in range(GROUP):
         whole = sums_a[t].astype(f32)
-        out_value[t] = whole[0:depth]
-        total += jnp.where(
-            lax.broadcasted_iota(jnp.int32, (depth, 256), 1) < 192, whole[0:depth] * w_value[t].astype(f32), 0.0
-        )
+        out_value[:, 192 * t : 192 * t + 192] = whole[0:depth, 0:192]
+        sides.append(whole[0:depth, 128:256])
+        total += jnp.where(lane < 192, whole[0:depth] * extra[t].astype(f32), 0.0)
         for i in range(heads):
             block = lambda j: whole[depth * (1 + 5 * i + j) : depth * (2 + 5 * i + j)]
             weight = w_first[heads * t + i].astype(f32)
@@ -1240,30 +1256,45 @@
                 total += block(j) * weight[:, at]
             for j in range(2):
                 out_second[heads * t + i, :, 256 * j : 256 * j + 256] = block(3 + j)
-    dots[...] = jnp.broadcast_to(jnp.sum(total, axis=1, keepdims=True), dots.shape)
+    gain = jnp.sum(jnp.where(lane == 195, extra[0].astype(f32), 0.0), axis=1, keepdims=True)
+    gain_grad = jnp.sum(total, axis=1, keepdims=True) / gain
+    low = lax.broadcasted_iota(jnp.int32, (depth, 128), 1)
+    sides[0] = jnp.where(low == 68, gain_grad, sides[0])
+    turned = jnp.concatenate(sides + [jnp.zeros((128 - GROUP * depth, 128), f32)], 0).T
+    two = jnp.zeros((1, 128), f32)
+    for t in range(GROUP):
+        mine = pltpu.roll(turned, 128 - depth * t, 1) if t else turned
+        out_b1[heads * t : heads * t + heads, :] = mine[64 : 64 + heads, 0:depth]
+        two += mine[67:68]
+    out_two[...] = two[:, 0:depth]
+    out_one[...] = turned[68:69, 0:depth]
+    out_b2[...] = sums_b[0:1, 0 : out_b2.shape[1]]
     for k in range(4):
         out_up[:, width * k : width * k + width] = sums_f[depth * k : depth * k + depth]
     out_out[...] = sums_f[4 * depth : 5 * depth]
     out_down[...] = sums_f[128:224]
 
 
-def finish_call(sums_a, sums_f, w_first, w_value, slots):
+def finish_call(sums_a, sums_f, sums_b, w_first, extra, slots, shard):
     heads_all, depth, width = w_first.shape
     return pl.pallas_call(
         finish_kernel,
         out_shape=(
+            shape_of((1, depth), f32),
+            shape_of((depth, width), f32),
             shape_of((heads_all, depth, width), f32),
+            shape_of((heads_all, depth), f32),
             shape_of((heads_all, depth, slots), f32),
-            shape_of((GROUP, depth, 256), f32),
+            shape_of((1, shard), f32),
+            shape_of((depth, width), f32),
+            shape_of((1, depth), f32),
             shape_of((depth, 4 * width), f32),
-            shape_of((depth, width), f32),
             shape_of((4 * depth, width), f32),
-            shape_of((depth, 128), f32),
         ),
-        in_specs=[FULL] * 4,
-        out_specs=(FULL,) * 7,
+        in_specs=[FULL] * 5,
+        out_specs=(FULL,) * 10,
         compiler_params=pltpu.CompilerParams(vmem_limit_bytes=VMEM_LIMIT),
-    )(sums_a, sums_f, w_first, w_value)
+    )(sums_a, sums_f, sums_b, w_first, extra)
 
 
 def on_device_fast(tokens, lengths, gain_one, w_value, w_first, b_first, w_second, b_second, w_out, gain_two, w_up, w_down, grad_out):
@@ -1289,23 +1320,8 @@
     out_f, out_a, out_s, gtok = back_call(
         wf, ws, wv, normed, values, hid, slope, prob, gmix, gg2, half, tokens[0], gmid, small
     )
-    grad_first, grad_second, side, grad_up, grad_out_w, grad_down, dots = finish_call(
-        out_a, out_f, w_first, extra, slots
-    )
-    return (
-        result[None],
-        gtok[None],
-        dots[:, 0] / gain_one.astype(f32),
-        side[:, :, :192].transpose(1, 0, 2).reshape(depth, width),
-        grad_first,
-        side[:, :, 192:195].transpose(0, 2, 1).reshape(heads_all, depth),
-        grad_second,
-        out_s[0, : b_second.shape[0]],
-        grad_out_w,
-        jnp.sum(side[:, :, 195], axis=0),
-        grad_up,
-        grad_down,
-    )
+    outs = finish_call(out_a, out_f, out_s, w_first, extra, slots, b_second.shape[0])
+    return (result[None], gtok[None]) + tuple(v[0] if k in (0, 5, 7) else v for k, v in enumerate(outs))
 
 
 def solution(mesh):

time: 274 us -> 265 us (0.967)
  local copies, waits for them, and re-layouts: 11.1 us -> 5.6 us
where the time goes in v8:
time: 265 us
  Pallas kernels  257 us (97%)
  local copies, waits for them, and re-layouts  5.6 us (2%)
    pallas_call x1, Pallas kernels, attend_call(): pl.pallas_call(attend_kernel, grid=(heads, GROUP), out_shape=(shape_of((h...  108 us
    pallas_call x1, Pallas kernels, back_call(): pl.pallas_call(back_kernel, grid=(heads + 1, GROUP), out_shape=(shape_of(...  101 us
    pallas_call x1, Pallas kernels, ffn_call(): pl.pallas_call(ffn_kernel, out_shape=(shape_of((slots, width), f32), shap...  45.1 us

profile of v8, /device:TPU:0, one launch (start us, length us, event | category | flops | bytes accessed | tf_op | source)
XLA Modules:
  0.0 265.1 jit_solution(11146884921683990145)
XLA Ops:
  1.3 0.1 pad_maximum_fusion.1
  1.4 0.7 pad_maximum_fusion
  2.1 0.7 reshape.34
  2.8 0.1 copy.28
  2.9 0.7 reshape.35
  3.7 0.1 copy.27
  3.8 0.9 reshape.33
  4.7 0.7 concatenate.3.extra
  5.4 108.2 %shard_map.220 = (bf16[3,768,768]{2,1,0:T(8,128)(2,1)}, bf16[3,768,512]{2,1,0:T(8,128)(2,1)}, bf16[768,256]{1,0:T(8,128)(2,1)}, f32[8,768]{1,0:T(8,128)}, bf16[4...) custom-call(bf16[1,512,768]{2,1,0:T(8,128)(2,1)} %tokens.1, ...), custom_call_target="tpu_custom_call" | custom-call | tf_op jit(solution)/shard_map/pallas_call | solution.py:588
  113.6 45.1 %shard_map.221 = (f32[512,768]{1,0:T(8,128)}, f32[512,768]{1,0:T(8,128)}, bf16[4,512,256]{2,1,0:T(8,128)(2,1)}, bf16[2,2,4,224,768]{4,3,2,1,0:T(8,128)(2,1)}, f32[8,768]{1,0:T(8,128)}) custom-call(bf16[2,2,2,4,224,768]{5,4,3,2,1,0:T(8,128)(2,1)} %get-tuple-element.42.lf_far, bf16[4,512,256]{2,1,0:T(8,128)(2,1)} %get-tuple-element.43.joined, ...), custom_call_target="tpu_custom_call" | custom-call | tf_op jit(solution)/shard_map/pallas_call | solution.py:824
  158.7 0.0 copy-start
  158.8 100.7 %shard_map.222 = (f32[224,768]{1,0:T(8,128)}, bf16[4,384,256]{2,1,0:T(8,128)(2,1)}, f32[8,256]{1,0:T(8,128)}, f32[512,768]{1,0:T(8,128)}) custom-call(bf16[3,768,768]{2,1,0:T(8,128)(2,1)} %get-tuple-element.46.wf, bf16[3,768,512]{2,1,0:T(8,128)(2,1)} %get-tuple-element.47.ws, bf16[768,256]{1,0:T(8,128)(2,1)} %get-tuple-element.48.wv, ...), custom_call_target="tpu_custom_call" | custom-call | tf_op jit(solution)/shard_map/pallas_call | solution.py:1167
  259.5 0.0 copy-start.1
  259.5 3.3 %shard_map.223 = (f32[1,24]{1,0:T(1,128)}, f32[24,768]{1,0:T(8,128)}, f32[12,24,768]{2,1,0:T(8,128)}, f32[12,24]{1,0:T(8,128)}, f32[12,24,512]{2,1,0:T(8,128)}, ...) custom-call(bf16[4,384,256]{2,1,0:T(8,128)(2,1)} %get-tuple-element.59.su, ...), custom_call_target="tpu_custom_call" | custom-call | tf_op jit(solution)/shard_map/pallas_call | solution.py:1280
  262.8 0.0 copy-done
  262.8 1.1 copy.34
  263.9 0.0 copy-done.1
  264.0 1.1 copy.35
  (5 shorter events, 0.0 us)
Async XLA Ops:
  158.7 104.1 %copy-start = (f32[512,768]{1,0:T(8,128)S(1)}, f32[512,768]{1,0:T(8,128)}, u32[]{:S(2)}) copy-start(f32[512,768]{1,0:T(8,128)} %get-tuple-element.45) | copy-start | bytes 4718596
  259.5 4.5 %copy-start.1 = (f32[512,768]{1,0:T(8,128)S(1)}, f32[512,768]{1,0:T(8,128)}, u32[]{:S(2)}) copy-start(f32[512,768]{1,0:T(8,128)} %get-tuple-element.58) | copy-start | bytes 4718596

commit v9 on v8

--- a/solution.py
+++ b/solution.py
@@ -409,16 +409,16 @@
         ups = [w_up[:, k : k + width].astype(f32) for k in range(0, w_up.shape[1], width)]
         pf[0:96] = jnp.concatenate(ups, 0).astype(bf16)
         pf[96:128] = jnp.concatenate([w_out[...].astype(f32), jnp.zeros((8, width), f32)], 0).astype(bf16)
-        pf[128:224] = w_down[...]
+        met(7)
+        f1(0).begin()
         for p in range(GROUP):
             stack = [extra[p].astype(f32)]
             for i in range(heads):
                 stack += blocks(w_first[heads * p + i].astype(f32)) + blocks(w_second[heads * p + i].astype(f32))
             pa[p] = jnp.concatenate(stack, 0).astype(bf16)
-        met(7)
-        f1(0).begin()
         for i in range(heads):
             start(mine(i) + a1(i))
+        pf[128:224] = w_down[...]
         start(mine_f() + mine_t())
         wait(mine(0) + a1(0))
         a2(0).begin()
@@ -540,7 +540,7 @@
     b1 = jnp.sum(jnp.where(row == h, small[...], 0.0), axis=0, keepdims=True)
     shift = b2[h, 0:1] + masks[r, 0:1]
     tile = pl.ds(pl.multiple_of((h // 2) * 128, 128), 128)
-    step = 256
+    step = 512
     for m in range(0, 512, step):
         at = slice(m, m + step)
         before = dot_nn(nrm[r, at, :], wf[0]) + b1

time: 265 us -> 265 us (level)
  no operation moved by 1% of the time
where the time goes in v9:
time: 265 us
  Pallas kernels  257 us (97%)
  local copies, waits for them, and re-layouts  5.6 us (2%)
    pallas_call x1, Pallas kernels, attend_call(): pl.pallas_call(attend_kernel, grid=(heads, GROUP), out_shape=(shape_of((h...  108 us
    pallas_call x1, Pallas kernels, back_call(): pl.pallas_call(back_kernel, grid=(heads + 1, GROUP), out_shape=(shape_of(...  101 us
    pallas_call x1, Pallas kernels, ffn_call(): pl.pallas_call(ffn_kernel, out_shape=(shape_of((slots, width), f32), shap...  45.1 us

profile of v9, /device:TPU:0, one launch (start us, length us, event | category | flops | bytes accessed | tf_op | source)
XLA Modules:
  0.0 264.9 jit_solution(14133992929648944349)
XLA Ops:
  1.3 0.1 pad_maximum_fusion.1
  1.4 0.7 pad_maximum_fusion
  2.1 0.7 reshape.34
  2.8 0.1 copy.28
  2.9 0.7 reshape.35
  3.7 0.1 copy.27
  3.8 0.9 reshape.33
  4.7 0.7 concatenate.3.extra
  5.4 107.9 %shard_map.220 = (bf16[3,768,768]{2,1,0:T(8,128)(2,1)}, bf16[3,768,512]{2,1,0:T(8,128)(2,1)}, bf16[768,256]{1,0:T(8,128)(2,1)}, f32[8,768]{1,0:T(8,128)}, bf16[4...) custom-call(bf16[1,512,768]{2,1,0:T(8,128)(2,1)} %tokens.1, ...), custom_call_target="tpu_custom_call" | custom-call | tf_op jit(solution)/shard_map/pallas_call | solution.py:588
  113.4 45.1 %shard_map.221 = (f32[512,768]{1,0:T(8,128)}, f32[512,768]{1,0:T(8,128)}, bf16[4,512,256]{2,1,0:T(8,128)(2,1)}, bf16[2,2,4,224,768]{4,3,2,1,0:T(8,128)(2,1)}, f32[8,768]{1,0:T(8,128)}) custom-call(bf16[2,2,2,4,224,768]{5,4,3,2,1,0:T(8,128)(2,1)} %get-tuple-element.42.lf_far, bf16[4,512,256]{2,1,0:T(8,128)(2,1)} %get-tuple-element.43.joined, ...), custom_call_target="tpu_custom_call" | custom-call | tf_op jit(solution)/shard_map/pallas_call | solution.py:824
  158.5 0.0 copy-start
  158.5 100.8 %shard_map.222 = (f32[224,768]{1,0:T(8,128)}, bf16[4,384,256]{2,1,0:T(8,128)(2,1)}, f32[8,256]{1,0:T(8,128)}, f32[512,768]{1,0:T(8,128)}) custom-call(bf16[3,768,768]{2,1,0:T(8,128)(2,1)} %get-tuple-element.46.wf, bf16[3,768,512]{2,1,0:T(8,128)(2,1)} %get-tuple-element.47.ws, bf16[768,256]{1,0:T(8,128)(2,1)} %get-tuple-element.48.wv, ...), custom_call_target="tpu_custom_call" | custom-call | tf_op jit(solution)/shard_map/pallas_call | solution.py:1167
  259.3 0.0 copy-start.1
  259.3 3.3 %shard_map.223 = (f32[1,24]{1,0:T(1,128)}, f32[24,768]{1,0:T(8,128)}, f32[12,24,768]{2,1,0:T(8,128)}, f32[12,24]{1,0:T(8,128)}, f32[12,24,512]{2,1,0:T(8,128)}, ...) custom-call(bf16[4,384,256]{2,1,0:T(8,128)(2,1)} %get-tuple-element.59.su, ...), custom_call_target="tpu_custom_call" | custom-call | tf_op jit(solution)/shard_map/pallas_call | solution.py:1280
  262.6 0.0 copy-done
  262.6 1.1 copy.34
  263.8 0.0 copy-done.1
  263.8 1.1 copy.35
  (5 shorter events, 0.0 us)
Async XLA Ops:
  158.5 104.1 %copy-start = (f32[512,768]{1,0:T(8,128)S(1)}, f32[512,768]{1,0:T(8,128)}, u32[]{:S(2)}) copy-start(f32[512,768]{1,0:T(8,128)} %get-tuple-element.45) | copy-start | bytes 4718596
  259.3 4.5 %copy-start.1 = (f32[512,768]{1,0:T(8,128)S(1)}, f32[512,768]{1,0:T(8,128)}, u32[]{:S(2)}) copy-start(f32[512,768]{1,0:T(8,128)} %get-tuple-element.58) | copy-start | bytes 4718596
